TPU v7x, 32 devices: a whole 2x2x4 slice. The times are simulated.
32 devices in a mesh: groups: 2 (over x), sector: 8 (over z, y), mpo: 2 (over core).
Axes of the slice: x: 2, y: 2, z: 4, core: 2. Of those that a mesh axis runs over, the one named last changes fastest.
Arguments:
- psi: bfloat16 [128, 256, 256], P(('groups', 'sector')), parts along dimension 0, may hold values from -4 to 4
- left_env: bfloat16 [52, 64, 256, 256], P(('groups', 'mpo'), 'sector'), parts along dimension 0, may hold values from -0.375 to 0.375
- right_env: bfloat16 [52, 64, 256, 256], P(('groups', 'mpo'), 'sector'), parts along dimension 0, may hold values from -0.375 to 0.375
- term_class: int32 [52], P(('groups', 'mpo')), parts along dimension 0, may hold values from 0 to 4
- active: int32 [52, 64], P(('groups', 'mpo'), 'sector'), parts along dimension 0, may hold values 0 or 1
- dest: int32 [10, 64], P('groups', 'sector'), parts along dimension 0, may hold values from 0 to 63, as said below
- sector_rows: int32 [128], P(('groups', 'sector')), parts along dimension 0, may hold values from 64 to 256
Outputs:
- h_psi: bfloat16 [128, 256, 256], P(('groups', 'sector'), 'mpo'), parts along dimension 0
There are 2 independent parts, one for each index of `groups`. A program takes and returns all parts, laid end to end along the dimension named above; each array names one. Nothing has to cross between parts.
Inputs may be any that keep to these rules, and one draw needn't show every extreme that they name: For each shift c, dest[c] is a permutation of the 64 sectors. Sector s = d * 8 + i goes to sector ((d + k) mod 8) * 8 + p, where k and p depend on c and i only; over all c and i, no value of k occurs more than 6 times, and some value occurs exactly 6 times.
All inputs are finite; a program needn't handle non-finite values. No bound on the sum of `active` on one device may be relied on, other than what follows from the above.
Results may differ from a plain program's by a relative error of at most 0.01.
Values may be sent and summed in bfloat16 or wider, within the bound.
No kernel may reach another device: no remote copies, remote signals or barrier semaphores. Data moves between devices by JAX's collectives and lax.ppermute only.
A program may use at most 192 MiB of HBM per device.

v0:
```python
import jax
import jax.numpy as jnp
from jax import lax
from jax.sharding import PartitionSpec as P


def body(psi, left_env, right_env, term_class, active, dest, sector_rows):
    sec_dev = psi.shape[0]
    blk = psi.shape[1]
    classes = dest.shape[0]
    sec_count = lax.axis_size("sector")
    mpo_count = lax.axis_size("mpo")
    half = blk // mpo_count
    line = jnp.arange(blk, dtype=jnp.int32)
    keep = line[None, :, None] < sector_rows[:, None, None]
    masked = jnp.where(keep, psi, jnp.zeros_like(psi))
    inner = jnp.einsum(
        "wsij,sjk->wsik", left_env, masked, preferred_element_type=jnp.float32
    ).astype(jnp.bfloat16)
    terms = jnp.einsum("wsij,wsjk->wsik", inner, right_env, preferred_element_type=jnp.float32)
    picks = (term_class[None, :] == jnp.arange(classes, dtype=jnp.int32)[:, None]).astype(
        jnp.float32
    )
    weights = picks[:, :, None] * active[None, :, :].astype(jnp.float32)
    partial_sum = jnp.einsum("cws,wsik->csik", weights, terms, precision=lax.Precision.HIGHEST)
    summed_all = lax.psum(partial_sum.astype(jnp.bfloat16), "mpo").astype(jnp.float32)
    mine = lax.dynamic_slice_in_dim(summed_all, lax.axis_index("mpo") * half, half, 2)
    blocks = mine.astype(jnp.bfloat16).reshape(classes * sec_dev, half * blk)
    target = dest.reshape(classes * sec_dev)
    peer = target // sec_dev
    local_idx = target % sec_dev
    cap = (classes * sec_dev + sec_count - 1) // sec_count + 1
    count = classes * sec_dev
    order_ids = jnp.arange(count, dtype=jnp.int32)
    earlier = (peer[:, None] == peer[None, :]) & (order_ids[None, :] < order_ids[:, None])
    rank = jnp.sum(earlier.astype(jnp.int32), axis=1)
    position = peer * cap + rank
    slots = jnp.arange(sec_count * cap, dtype=jnp.int32)
    chosen = position[None, :] == slots[:, None]
    packed = jnp.dot(chosen.astype(jnp.bfloat16), blocks, preferred_element_type=jnp.float32)
    packed = packed.astype(jnp.bfloat16).reshape(sec_count * cap, half, blk)
    slot_target = jnp.max(jnp.where(chosen, local_idx[None, :], -1), axis=1)
    arrived, arrived_idx = (
        lax.all_to_all(packed, "sector", split_axis=0, concat_axis=0, tiled=True),
        lax.all_to_all(slot_target, "sector", split_axis=0, concat_axis=0, tiled=True),
    )
    select = (arrived_idx[None, :] == jnp.arange(sec_dev, dtype=jnp.int32)[:, None]).astype(
        jnp.bfloat16
    )
    total = jnp.dot(
        select, arrived.reshape(sec_count * cap, half * blk), preferred_element_type=jnp.float32
    ).reshape(sec_dev, half, blk)
    row_ids = lax.axis_index("mpo") * half + jnp.arange(half, dtype=jnp.int32)
    live = row_ids[None, :, None] < sector_rows[:, None, None]
    return jnp.where(live, total, jnp.float32(0.0)).astype(jnp.bfloat16)


def solution(mesh):
    placed = (
        P(("groups", "sector"), None, None),
        P(("groups", "mpo"), "sector", None, None),
        P(("groups", "mpo"), "sector", None, None),
        P(("groups", "mpo")),
        P(("groups", "mpo"), "sector"),
        P("groups", "sector"),
        P(("groups", "sector")),
    )
    return jax.shard_map(
        body,
        mesh=mesh,
        in_specs=placed,
        out_specs=P(("groups", "sector"), "mpo", None),
        check_vma=False,
    )
```

profile of v0, /device:TPU:0, one launch (start us, length us, event | category | flops | bytes accessed | tf_op | source)
XLA Modules:
  0.0 222.3 jit_solution(12186085789367129755)
XLA Ops:
  6.5 0.0 all-reduce.2.cloned.1.call-start
  6.5 0.7 iota_compare_fusion.3
  7.3 0.7 convert_element_type.44
  8.0 0.7 fusion.31
  8.6 10.2 %convert_bitcast_fusion = bf16[13,8,256,256]{2,3,0,1:T(8,128)(2,1)} fusion(bf16[13,8,256,256]{3,2,1,0:T(8,128)(2,1)} %param.8, bf16[8,256,256]{2,1,0:T(8,128)(2,1)} %param.7, pred[8,256]{1,0:T(8,128)(4,1)S(1)} %iota_compare_fusion.3), kind=kOutput, calls=%fused_computation.7 | convolution fusion | flops 3497000960 | bytes 28313600 | tf_op jit(solution)/shard_map/wsij,sjk->wsik/dot_general | solution.py:17
  18.9 20.0 %fusion.2 = f32[13,8,256,256]{3,2,1,0:T(8,128)} fusion(bf16[13,8,256,256]{3,2,1,0:T(8,128)(2,1)} %param.9, bf16[13,8,256,256]{2,3,0,1:T(8,128)(2,1)} %convert_bitcast_fusion), kind=kOutput, calls=%fused_computation.3 | convolution fusion | flops 3489660928 | bytes 54525952 | tf_op jit(solution)/shard_map/wsij,wsjk->wsik/dot_general | solution.py:20
  38.9 53.0 %fusion = bf16[8,256,256,5]{2,3,1,0:T(8,128)(2,1)S(1)} fusion(f32[13,8,256,256]{3,2,1,0:T(8,128)} %fusion.2, f32[13,8]{0,1:T(8,128)S(1)} %convert_element_type.44, f32[5,13]{1,0:T(8,128)S(1)} %fusion.31), kind=kOutput, calls=%fused_computation.1 | convolution fusion | flops 408945152 | bytes 32506532 | tf_op jit(solution)/shard_map/cws,wsik->csik/dot_general | solution.py:25
  91.9 0.0 copy-start
  92.0 3.7 %copy.68 = bf16[8,256,256,5]{2,1,0,3:T(8,128)(2,1)} copy(bf16[8,256,256,5]{2,3,1,0:T(8,128)(2,1)S(1)} %fusion) | data formatting | bytes 10485760 | tf_op jit(solution)/shard_map/cws,wsik->csik/dot_general | solution.py:25
  95.7 0.0 all-reduce.2.cloned.1.call-update
  95.7 0.0 copy-done
  95.7 0.1 reshape.190
  95.8 0.2 convert_reduce_fusion
  96.0 0.1 select_reduce_fusion
  96.1 0.7 all_to_all.9
  96.8 7.3 %all-to-all-start = ((s32[8,6,1]{1,2,0:T(1,128)}), s32[8,6,1]{1,2,0:T(1,128)S(1)}, u32[]{:S(2)}, u32[]{:S(2)}) async-start(s32[8,6,1]{1,2,0:T(1,128)} %bitcast), calls=%async_computation | async-start | bytes 8192 | tf_op jit(solution)/shard_map/all_to_all | solution.py:45
  104.0 24.6 %all-reduce.2.cloned.1.call-done = bf16[5,8,256,256]{3,2,1,0:T(8,128)(2,1)} async-done(((bf16[5,8,256,256]{3,2,1,0:T(8,128)(2,1)}), bf16[5,8,256,256]{3,2,1,0:T(8,128)(2,1)}) %all-reduce.2.cloned.1.call-update) | async-done | bytes 5242896 | tf_op jit(solution)/shard_map/psum | solution.py:26
  128.7 2.0 fusion.12
  130.7 1.6 copy.43
  132.3 0.0 copy-start.1
  132.3 1.1 convolution_convert_fusion
  133.4 2.4 %copy.44 = bf16[6,8,128,256]{3,2,1,0:T(8,128)(2,1)} copy(bf16[6,8,128,256]{3,1,2,0:T(8,128)(2,1)S(1)} %bitcast.44) | data formatting | bytes 6291456
  135.8 0.0 all-to-all-done
  135.8 5.8 %all-to-all-start.1 = ((bf16[48,128,256]{2,1,0:T(8,128)(2,1)}), bf16[48,128,256]{2,1,0:T(8,128)(2,1)S(1)}, u32[]{:S(2)}, u32[]{:S(2)}) async-start(bf16[48,128,256]{2,1,0:T(8,128)(2,1)} %bitcast.17), calls=%async_computation.1 | async-start | bytes 6291456 | tf_op jit(solution)/shard_map/all_to_all | solution.py:44
  141.6 0.0 copy-done.1
  141.6 0.1 broadcast_compare_fusion
  141.7 0.5 broadcast.175
  142.2 0.7 reduce.3
  142.9 0.1 eq.66
  142.9 69.8 %all-to-all-done.1 = bf16[48,128,256]{2,1,0:T(8,128)(2,1)S(1)} async-done(((bf16[48,128,256]{2,1,0:T(8,128)(2,1)}), bf16[48,128,256]{2,1,0:T(8,128)(2,1)S(1)}, u32[]{:S(2)}, u32[]{:S(2)}) %all-to-all-start.1) | async-done | bytes 3145760 | tf_op jit(solution)/shard_map/all_to_all | solution.py:44
  212.7 1.8 fusion.16
  214.6 0.9 copy.35
  (3 shorter events, 0.0 us)
Async XLA Ops:
  6.5 122.1 %all-reduce.2.cloned.1.call-start = ((), (), s32[]{:S(2)}) async-start(), calls=%async_computation.2 | async-start | bytes 10485760 | tf_op jit(solution)/shard_map/psum | solution.py:26
  91.9 3.7 %copy-start = (s32[5,8]{1,0:T(8,128)S(1)}, s32[5,8]{1,0:T(8,128)}, u32[]{:S(2)}) copy-start(s32[5,8]{1,0:T(8,128)} %param.12) | copy-start | bytes 484
  96.8 39.0 %all-to-all-start = ((s32[8,6,1]{1,2,0:T(1,128)}), s32[8,6,1]{1,2,0:T(1,128)S(1)}, u32[]{:S(2)}, u32[]{:S(2)}) async-start(s32[8,6,1]{1,2,0:T(1,128)} %bitcast), calls=%async_computation | async-start | bytes 8192 | tf_op jit(solution)/shard_map/all_to_all | solution.py:45
  132.3 9.3 %copy-start.1 = (s32[8]{0:T(128)S(1)}, s32[8]{0:T(128)}, u32[]{:S(2)}) copy-start(s32[8]{0:T(128)} %param.13) | copy-start | bytes 100
  135.8 76.9 %all-to-all-start.1 = ((bf16[48,128,256]{2,1,0:T(8,128)(2,1)}), bf16[48,128,256]{2,1,0:T(8,128)(2,1)S(1)}, u32[]{:S(2)}, u32[]{:S(2)}) async-start(bf16[48,128,256]{2,1,0:T(8,128)(2,1)} %bitcast.17), calls=%async_computation.1 | async-start | bytes 6291456 | tf_op jit(solution)/shard_map/all_to_all | solution.py:44
Sparse Core Ops, SparseCore 0:
  95.8 32.8 all-reduce.1
where the time goes:
time: 223 us; the launch traced here: 222 us
  waiting for transfers between devices  94.4 us (42%)
  matrix products  86.3 us (39%)
  between operations  13.5 us (6%)
  starting transfers between devices  13.1 us (6%)
  local copies, waits for them, and re-layouts  9.94 us (4%)
  other arithmetic  5.14 us (2%)
    all_to_all x1, waiting for transfers between devices, body(): lax.all_to_all(packed, 'sector', split_axis=0, concat_axis=0, tiled=True)  69.8 us
    dot_general x1, matrix products, body(): jnp.einsum('cws,wsik->csik', weights, terms, precision=lax.Precision.HIGH...  53 us
    psum x1, waiting for transfers between devices, body(): lax.psum(partial_sum.astype(jnp.bfloat16), 'mpo').astype(jnp.float32)  24.6 us
    dot_general x1, matrix products, body(): jnp.einsum('wsij,wsjk->wsik', inner, right_env, preferred_element_type=jn...  20 us
    dot_general x1, matrix products, body(): jnp.einsum('wsij,sjk->wsik', left_env, masked, preferred_element_type=jnp...  10.2 us
    all_to_all x1, starting transfers between devices, body(): lax.all_to_all(slot_target, 'sector', split_axis=0, concat_axis=0, tiled=...  7.28 us
    all_to_all x1, starting transfers between devices, body(): lax.all_to_all(packed, 'sector', split_axis=0, concat_axis=0, tiled=True)  5.78 us
  transfers between devices with their start and end apart: 3, of which 2 were waited for; matrix products, arithmetic and copies ran while one was open for 4% of the time, Pallas kernels for 0%

commit v1 on v0

v1 whole, which is shorter than its diff:
```python
import functools

import jax
import jax.numpy as jnp
from jax import lax
from jax.experimental import pallas as pl
from jax.experimental.pallas import tpu as pltpu
from jax.sharding import PartitionSpec as P

SMEM = pl.BlockSpec(memory_space=pltpu.SMEM)
ANY = pl.BlockSpec(memory_space=pl.ANY)
VMEM = pl.BlockSpec(memory_space=pltpu.VMEM)
DEPTH = 12
CHUNKS = 1
Y = 2


def shifts_kernel(chunk, tc, act, rows, psi, left, right, send, keep, lbuf, rbuf, acc, masked, w_of, s_of, c_of, first, sems):
    s = pl.program_id(0)
    n_w, n_s = left.shape[0], left.shape[1]
    classes = send.shape[0]
    blk = left.shape[2]
    half = blk // 2
    hr = send.shape[2]
    me = lax.axis_index("mpo")

    def copies(j):
        slot = lax.rem(j, DEPTH)
        w, sec = w_of[j], s_of[j]
        parts = [(right.at[w, sec], rbuf.at[slot])]
        if hr == half:
            parts.append((left.at[w, sec], lbuf.at[slot]))
        else:
            for h in range(2):
                parts.append((left.at[w, sec, pl.ds(h * half + chunk * hr, hr)], lbuf.at[slot, pl.ds(h * hr, hr)]))
        return [pltpu.make_async_copy(a, b, sems.at[slot, i]) for i, (a, b) in enumerate(parts)]

    def fetch(j):
        for c in copies(j):
            c.start()

    @pl.when(s == 0)
    def _():
        first[0] = 0

        def sector(sec, n):
            def term(w, n):
                on = act[w, sec]
                w_of[n] = w
                s_of[n] = sec
                c_of[n] = tc[w]

                @pl.when((on == 1) & (n < DEPTH))
                def _():
                    fetch(n)

                return n + on

            n = lax.fori_loop(0, n_w, term, n)
            odd = lax.rem(n, 2)

            @pl.when(odd == 1)
            def _():
                w_of[n] = w_of[n - 1]
                s_of[n] = sec
                c_of[n] = classes

                @pl.when(n < DEPTH)
                def _():
                    fetch(n)

            first[sec + 1] = n + odd
            return n + odd

        lax.fori_loop(0, n_s, sector, jnp.int32(0))

    total = first[n_s]
    line = lax.broadcasted_iota(jnp.int32, (blk, blk), 0)
    masked[...] = jnp.where(line < rows[s], psi[0].astype(jnp.float32), 0.0).astype(jnp.bfloat16)
    for c in range(classes):
        acc[c] = jnp.zeros(acc.shape[1:], jnp.float32)

    begin = first[s]

    def pair(t, _):
        j = begin + 2 * t
        for i in range(2):
            for c in copies(j + i):
                c.wait()
        slots = [lax.rem(j + i, DEPTH) for i in range(2)]
        inner = [
            jnp.dot(lbuf[slots[i]], masked[...], preferred_element_type=jnp.float32).astype(jnp.bfloat16)
            for i in range(2)
        ]
        terms = [jnp.dot(inner[i], rbuf[slots[i]], preferred_element_type=jnp.float32) for i in range(2)]
        for i in range(2):
            acc[c_of[j + i]] += terms[i]
        for i in range(2):

            @pl.when(j + i + DEPTH < total)
            def _():
                fetch(j + i + DEPTH)

        return 0

    lax.fori_loop(0, (first[s + 1] - begin) // 2, pair, 0)
    mine = pl.multiple_of(me * hr, hr)
    other = pl.multiple_of((1 - me) * hr, hr)
    for c in range(classes):
        keep[c, 0] = acc[c, pl.ds(mine, hr), :].astype(jnp.bfloat16)
        send[c, 0] = acc[c, pl.ds(other, hr), :].astype(jnp.bfloat16)


def shift_sums(chunk, hr, psi, left_env, right_env, term_class, active, sector_rows, classes):
    n_w, n_s, blk = left_env.shape[:3]
    out = jax.ShapeDtypeStruct((classes, n_s, hr, blk), jnp.bfloat16)
    block = pl.BlockSpec((classes, 1, hr, blk), lambda s: (0, s, 0, 0))
    most = n_s * (n_w + 1) + 1
    return pl.pallas_call(
        functools.partial(shifts_kernel, chunk),
        grid=(n_s,),
        out_shape=(out, out),
        in_specs=[SMEM, SMEM, SMEM, pl.BlockSpec((1, blk, blk), lambda s: (s, 0, 0)), ANY, ANY],
        out_specs=(block, block),
        scratch_shapes=[
            pltpu.VMEM((DEPTH, 2 * hr, blk), jnp.bfloat16),
            pltpu.VMEM((DEPTH, blk, blk), jnp.bfloat16),
            pltpu.VMEM((classes + 1, 2 * hr, blk), jnp.float32),
            pltpu.VMEM((blk, blk), jnp.bfloat16),
            pltpu.SMEM((most,), jnp.int32),
            pltpu.SMEM((most,), jnp.int32),
            pltpu.SMEM((most,), jnp.int32),
            pltpu.SMEM((n_s + 1,), jnp.int32),
            pltpu.SemaphoreType.DMA((DEPTH, 3)),
        ],
        compiler_params=pltpu.CompilerParams(vmem_limit_bytes=40 * 2**20, dimension_semantics=("arbitrary",)),
        cost_estimate=pl.CostEstimate(
            flops=4 * n_w * n_s * 2 * hr * blk * blk, bytes_accessed=2 * n_w * n_s * blk * (blk + 2 * hr), transcendentals=0
        ),
    )(term_class, active, sector_rows, psi, left_env, right_env)


def place(n, q):
    d = lax.axis_index("sector")
    z, y = d // Y, lax.rem(d, Y)
    line = n // Y
    m = jnp.where(lax.rem(z, 2) == 0, line - 1 - q, q + 1) if q < line - 1 else jnp.int32(0)
    return d, z, y, m


def scan_shift(dest, n, n_s, d, k, found):
    classes = dest.shape[0]

    def step(j, rank):
        t = dest[j // n_s, lax.rem(j, n_s)]
        hit = lax.rem(t // n_s - d + n, n) == k

        @pl.when(hit)
        def _():
            found(rank, j, lax.rem(t, n_s))

        return rank + hit.astype(jnp.int32)

    return lax.fori_loop(0, classes * n_s, step, jnp.int32(0))


def pack_kernel(n, qs, dest, keep, recv, *rest):
    outs, (a, b, sems) = rest[: len(qs)], rest[len(qs):]
    n_s = dest.shape[1]
    cap = outs[0].shape[0]
    counts = []
    for i, q in enumerate(qs):
        d, z, y, m = place(n, q)
        k = lax.rem(2 * m + 1 - 2 * y + n, n)

        def found(rank, j, p, i=i):
            pltpu.make_async_copy(keep.at[j], a.at[i, rank], sems.at[i, 0, rank]).start()
            pltpu.make_async_copy(recv.at[j], b.at[i, rank], sems.at[i, 1, rank]).start()

        counts.append(scan_shift(dest, n, n_s, d, k, found))
    for i in range(len(qs)):
        for slot in range(cap):

            @pl.when(slot < counts[i])
            def _(i=i, slot=slot):
                pltpu.make_async_copy(keep.at[0], a.at[i, slot], sems.at[i, 0, slot]).wait()
                pltpu.make_async_copy(recv.at[0], b.at[i, slot], sems.at[i, 1, slot]).wait()
                outs[i][slot] = (a[i, slot].astype(jnp.float32) + b[i, slot].astype(jnp.float32)).astype(jnp.bfloat16)


def pack(n, qs, cap, dest, keep, recv, after=()):
    hr, blk = keep.shape[1:]
    out = jax.ShapeDtypeStruct((cap, hr, blk), jnp.bfloat16)

    def body(dest, keep, recv, *rest):
        pack_kernel(n, qs, dest, keep, recv, *rest[len(after):])

    return pl.pallas_call(
        body,
        out_shape=(out,) * len(qs),
        in_specs=[SMEM, ANY, ANY] + [ANY] * len(after),
        out_specs=(VMEM,) * len(qs),
        scratch_shapes=[
            pltpu.VMEM((len(qs), cap, hr, blk), jnp.bfloat16),
            pltpu.VMEM((len(qs), cap, hr, blk), jnp.bfloat16),
            pltpu.SemaphoreType.DMA((len(qs), 2, cap)),
        ],
        compiler_params=pltpu.CompilerParams(vmem_limit_bytes=16 * 2**20),
        cost_estimate=pl.CostEstimate(flops=0, bytes_accessed=6 * len(qs) * cap * hr * blk, transcendentals=0),
    )(dest, keep, recv, *after)


def gather_kernel(n, q, chunk, dest, rows, keep, recv, crossed, *rest):
    extra, (out, a, b, total, where, sems) = rest[:-6], rest[-6:]
    n_s = dest.shape[1]
    cap = crossed.shape[0]
    hr = out.shape[1]
    d, z, y, m = place(n, q)

    def found(rank, j, p):
        where[rank] = p
        pltpu.make_async_copy(keep.at[j], a.at[rank], sems.at[0, rank]).start()
        pltpu.make_async_copy(recv.at[j], b.at[rank], sems.at[1, rank]).start()

    own = scan_shift(dest, n, n_s, d, lax.rem(2 * m, n), found)
    if extra:
        total[...] = sum(e[...].astype(jnp.float32) for e in extra)
    else:
        total[...] = jnp.zeros_like(total)

    def cross(rank, j, p):
        total[p] += crossed[rank].astype(jnp.float32)

    scan_shift(dest, n, n_s, d, lax.rem(2 * m + 2 * y - 1 + n, n), cross)
    for slot in range(cap):

        @pl.when(slot < own)
        def _(slot=slot):
            pltpu.make_async_copy(keep.at[0], a.at[slot], sems.at[0, slot]).wait()
            pltpu.make_async_copy(recv.at[0], b.at[slot], sems.at[1, slot]).wait()
            block = (a[slot].astype(jnp.float32) + b[slot].astype(jnp.float32)).astype(jnp.bfloat16)
            total[where[slot]] += block.astype(jnp.float32)

    if q == n // Y - 1:
        line = lax.broadcasted_iota(jnp.int32, total.shape[1:], 0) + (lax.axis_index("mpo") * hr * CHUNKS + chunk * hr)
        for p in range(n_s):
            out[p] = jnp.where(line < rows[p], total[p], 0.0).astype(jnp.bfloat16)
    else:
        out[...] = total[...].astype(jnp.bfloat16)


def gather(n, q, chunk, dest, rows, keep, recv, crossed, extra=()):
    hr, blk = keep.shape[1:]
    n_s = dest.shape[1]
    cap = crossed.shape[0]
    return pl.pallas_call(
        functools.partial(gather_kernel, n, q, chunk),
        out_shape=jax.ShapeDtypeStruct((n_s, hr, blk), jnp.bfloat16),
        in_specs=[SMEM, SMEM, ANY, ANY, VMEM] + [VMEM] * len(extra),
        out_specs=VMEM,
        scratch_shapes=[
            pltpu.VMEM((cap, hr, blk), jnp.bfloat16),
            pltpu.VMEM((cap, hr, blk), jnp.bfloat16),
            pltpu.VMEM((n_s, hr, blk), jnp.float32),
            pltpu.SMEM((cap,), jnp.int32),
            pltpu.SemaphoreType.DMA((2, cap)),
        ],
        compiler_params=pltpu.CompilerParams(vmem_limit_bytes=16 * 2**20),
        cost_estimate=pl.CostEstimate(flops=0, bytes_accessed=2 * (3 * cap + 2 * n_s) * hr * blk, transcendentals=0),
    )(dest, rows, keep, recv, crossed, *extra)


def body(psi, left_env, right_env, term_class, active, dest, sector_rows):
    n = lax.axis_size("sector")
    line = n // Y
    classes, n_s = dest.shape
    blk = psi.shape[1]
    half = blk // 2
    hr = half // CHUNKS
    cap = (classes * n_s + n - 1) // n + 1
    across = [(d, d ^ 1) for d in range(n)]
    near = [(z * Y + y, (z ^ 1) * Y + y) for z in range(line) for y in range(Y)]
    far = [(z * Y + y, (((z + 1) ^ 1) - 1) * Y + y) for z in range(1, line - 1) for y in range(Y)]

    outs = []
    for chunk in range(CHUNKS):
        send, keep = shift_sums(chunk, hr, psi, left_env, right_env, term_class, active, sector_rows, classes)
        send, keep = (x.reshape(classes * n_s, hr, blk) for x in (send, keep))
        recv = lax.ppermute(send, "mpo", [(0, 1), (1, 0)])
        crossed = []
        for q in range(line):
            (packed,) = pack(n, [q], cap, dest, keep, recv, crossed[-1:])
            crossed.append(lax.ppermute(packed, "sector", across))
        acc = [None] * line
        near_in, far_in = None, None
        for step in range(1, line):
            extra = () if far_in is None else (far_in,)
            acc[step - 1] = gather(n, step - 1, chunk, dest, sector_rows, keep, recv, crossed[step - 1])
            near_out = acc[step - 1]
            if far_in is not None:
                near_out = near_out + far_in
            far_out = None
            if step > 1:
                back = line - 1 - step
                if acc[back] is None:
                    acc[back] = gather(n, back, chunk, dest, sector_rows, keep, recv, crossed[back])
                far_out = acc[back] + near_in
            near_in = lax.ppermute(near_out, "sector", near)
            far_in = None if far_out is None else lax.ppermute(far_out, "sector", far)
        outs.append(gather(n, line - 1, chunk, dest, sector_rows, keep, recv, crossed[line - 1], (near_in, far_in)))
    return outs[0] if CHUNKS == 1 else jnp.concatenate(outs, axis=1)


def solution(mesh):
    placed = (
        P(("groups", "sector"), None, None),
        P(("groups", "mpo"), "sector", None, None),
        P(("groups", "mpo"), "sector", None, None),
        P(("groups", "mpo")),
        P(("groups", "mpo"), "sector"),
        P("groups", "sector"),
        P(("groups", "sector")),
    )
    return jax.shard_map(
        body,
        mesh=mesh,
        in_specs=placed,
        out_specs=P(("groups", "sector"), "mpo", None),
        check_vma=False,
    )
```

time: 223 us -> 111 us (0.50)
  matrix products: 86.3 us -> 0 us
  waiting for transfers between devices: 94.4 us -> 38 us
  Pallas kernels: 0 us -> 51.8 us
  between operations: 13.5 us -> 0.12 us
  local copies, waits for them, and re-layouts: 9.94 us -> 3.31 us
  other arithmetic: 5.14 us -> 0.45 us
  starting transfers between devices: 13.1 us -> 17.3 us
    dot_general x5 -> x0, matrix products: 86.3 us -> none  [the longest x1 53 us: body(): jnp.einsum('cws,wsik->csik', weights, terms, precision=lax.Precision.HIGH...]
    all_to_all x2 -> x0, waiting for transfers between devices: 69.8 us -> none  [the longest x1 69.8 us: body(): lax.all_to_all(packed, 'sector', split_axis=0, concat_axis=0, tiled=True)]
    pallas_call x0 -> x9, Pallas kernels: none -> 51.8 us  [the longest x1 21.5 us: shift_sums(): pl.pallas_call(functools.partial(shifts_kernel, chunk), grid=(n_s,), out_...]
    ppermute x0 -> x10, waiting for transfers between devices: none -> 38 us  [the longest x4 33.4 us: body(): crossed.append(lax.ppermute(packed, 'sector', across))]
    psum x1 -> x0, waiting for transfers between devices: 24.6 us -> none  [body(): lax.psum(partial_sum.astype(jnp.bfloat16), 'mpo').astype(jnp.float32)]
    ppermute x0 -> x10, starting transfers between devices: none -> 17.3 us  [the longest x3 7.61 us: body(): near_in = lax.ppermute(near_out, 'sector', near)]
    all_to_all x2 -> x0, starting transfers between devices: 13.1 us -> none  [the longest x1 7.28 us: body(): lax.all_to_all(slot_target, 'sector', split_axis=0, concat_axis=0, tiled=...]
    dot_general x1 -> x0, local copies, waits for them, and re-layouts: 3.7 us -> none  [body(): jnp.einsum('cws,wsik->csik', weights, terms, precision=lax.Precision.HIGH...]
  transfers between devices with their start and end apart: 3 -> 10, of which waited for: 2 -> 5; matrix products, arithmetic and copies ran while one was open for 4% -> 0% of each run, Pallas kernels for 0% -> 15%
where the time goes in v1:
time: 111 us
  Pallas kernels  51.8 us (47%)
  waiting for transfers between devices  38 us (34%)
  starting transfers between devices  17.3 us (16%)
  local copies, waits for them, and re-layouts  3.31 us (3%)
    ppermute x4, waiting for transfers between devices, body(): crossed.append(lax.ppermute(packed, 'sector', across))  33.4 us
    pallas_call x1, Pallas kernels, shift_sums(): pl.pallas_call(functools.partial(shifts_kernel, chunk), grid=(n_s,), out_...  21.5 us
    pallas_call x4, Pallas kernels, gather(): pl.pallas_call(functools.partial(gather_kernel, n, q, chunk), out_shape=j...  19.4 us
    pallas_call x4, Pallas kernels, pack(): pl.pallas_call(body, out_shape=(out,) * len(qs), in_specs=[SMEM, ANY, ANY...  11 us
    ppermute x3, starting transfers between devices, body(): near_in = lax.ppermute(near_out, 'sector', near)  7.61 us
    ppermute x4, starting transfers between devices, body(): crossed.append(lax.ppermute(packed, 'sector', across))  6.96 us
    ppermute x1, waiting for transfers between devices, body(): recv = lax.ppermute(send, 'mpo', [(0, 1), (1, 0)])  4.54 us
    unnamed x9, local copies, waits for them, and re-layouts  3.31 us
  transfers between devices with their start and end apart: 10, of which 5 were waited for; matrix products, arithmetic and copies ran while one was open for 0% of the time, Pallas kernels for 15%

profile of v1, /device:TPU:0, one launch (start us, length us, event | category | flops | bytes accessed | tf_op | source)
XLA Modules:
  0.0 111.0 jit_solution(733320513145294739)
XLA Ops:
  0.0 0.8 copy.8.act
  0.8 0.0 copy-start
  0.8 1.2 %copy-done = bf16[8,256,256]{2,1,0:T(8,128)(2,1)S(1)} copy-done((bf16[8,256,256]{2,1,0:T(8,128)(2,1)S(1)}, bf16[8,256,256]{2,1,0:T(8,128)(2,1)}, u32[]{:S(2)}) %copy-start) | copy-done | bytes 1048600
  2.0 0.0 copy-start.2
  2.0 0.7 copy-done.2
  2.7 0.0 copy-start.3
  2.7 0.7 copy-done.3
  3.3 0.0 copy-start.1
  3.3 21.5 %shard_map.73 = (bf16[5,8,128,256]{3,2,1,0:T(8,128)(2,1)S(1)}, bf16[5,8,128,256]{3,2,1,0:T(8,128)(2,1)S(1)}) custom-call(s32[13]{0:T(128)S(1)} %copy-done.3, s32[13,8]{1,0:T(8,128)S(1)} %copy.8.act, s32[8]{0:T(128)S(1)} %copy-done.2, bf16[8,256,256]{2,1,0:T(8,128)(2,1)S(1)} %copy-done, bf16[13,8,256,256]{3,2,1,0:T(8,128)(2,1)} %left.1, ...), custom_call_target="tpu_custom_call" | custom-call | flops 6979321856 | bytes 27262976 | tf_op jit(solution)/shard_map/pallas_call | solution.py:119
  24.8 1.3 %collective-permute-start = (bf16[40,128,256]{2,1,0:T(8,128)(2,1)S(1)}, bf16[40,128,256]{2,1,0:T(8,128)(2,1)S(1)}, u32[]{:S(2)}, u32[]{:S(2)}) collective-permute-start(bf16[40,128,256]{2,1,0:T(8,128)(2,1)S(1)} %bitcast.10), channel_id=1, source_target_pairs={{0,1},{1,0},{2,3},{3,2},{4,5},{5,4},{6,7},{7,6},{8,9},{9,8},{10,11... | collective-permute-start | bytes 7864328 | tf_op jit(solution)/shard_map/ppermute | solution.py:289
  26.1 4.5 %collective-permute-done.recv = bf16[40,128,256]{2,1,0:T(8,128)(2,1)S(1)} collective-permute-done((bf16[40,128,256]{2,1,0:T(8,128)(2,1)S(1)}, bf16[40,128,256]{2,1,0:T(8,128)(2,1)S(1)}, u32[]{:S(2)}, u32[]{:S(2)}) %collective-permute-start) | collective-permute-done | bytes 2621472 | tf_op jit(solution)/shard_map/ppermute | solution.py:289
  30.6 0.0 copy-done.1
  30.6 3.1 %shard_map.74 = bf16[6,128,256]{2,1,0:T(8,128)(2,1)S(1)} custom-call(s32[5,8]{1,0:T(8,128)S(1)} %copy-done.1, bf16[40,128,256]{2,1,0:T(8,128)(2,1)S(1)} %bitcast.2, bf16[40,128,256]{2,1,0:T(8,128)(2,1)S(1)} %collective-permute-done.recv), custom_call_target="tpu_custom_call" | custom-call | bytes 1179648 | tf_op jit(solution)/shard_map/pallas_call | solution.py:198
  33.8 2.9 %collective-permute-start.1 = (bf16[6,128,256]{2,1,0:T(8,128)(2,1)S(1)}, bf16[6,128,256]{2,1,0:T(8,128)(2,1)S(1)}, u32[]{:S(2)}, u32[]{:S(2)}) collective-permute-start(bf16[6,128,256]{2,1,0:T(8,128)(2,1)S(1)} %shard_map.74), channel_id=1, source_target_pairs={{0,2},{2,0},{4,6},{6,4},{8,10},{10,8},{12,14},{14,12},{1,3},{3,1},... | collective-permute-start | bytes 1179656 | tf_op jit(solution)/shard_map/ppermute | solution.py:293
  36.6 9.6 %collective-permute-done.1.rest_0_.crossed = bf16[6,128,256]{2,1,0:T(8,128)(2,1)S(1)} collective-permute-done((bf16[6,128,256]{2,1,0:T(8,128)(2,1)S(1)}, bf16[6,128,256]{2,1,0:T(8,128)(2,1)S(1)}, u32[]{:S(2)}, u32[]{:S(2)}) %collective-permute-start.1) | collective-permute-done | bytes 393248 | tf_op jit(solution)/shard_map/ppermute | solution.py:293
  46.3 4.6 %shard_map.80 = bf16[8,128,256]{2,1,0:T(8,128)(2,1)S(1)} custom-call(s32[5,8]{1,0:T(8,128)S(1)} %copy-done.1, s32[8]{0:T(128)S(1)} %copy-done.2, bf16[40,128,256]{2,1,0:T(8,128)(2,1)S(1)} %bitcast.3, bf16[40,128,256]{2,1,0:T(8,128)(2,1)S(1)} %collective-permute-done.recv, bf16[6,128,256]{2,1,0:T(8,128)(2,1)S(1)} %collective-permute-done.1.rest_0_.crossed), custom_call_target="tpu_custom_call" | custom-call | bytes 2228224 | tf_op jit(solution)/shard_map/pallas_call | solution.py:256
  50.9 0.3 collective-permute-start.5
  51.2 2.7 %shard_map.75 = bf16[6,128,256]{2,1,0:T(8,128)(2,1)S(1)} custom-call(s32[5,8]{1,0:T(8,128)S(1)} %copy-done.1, bf16[40,128,256]{2,1,0:T(8,128)(2,1)S(1)} %bitcast.4, bf16[40,128,256]{2,1,0:T(8,128)(2,1)S(1)} %collective-permute-done.recv, bf16[6,128,256]{2,1,0:T(8,128)(2,1)S(1)} %collective-permute-done.1.rest_0_.crossed), custom_call_target="tpu_custom_call" | custom-call | bytes 1179648 | tf_op jit(solution)/shard_map/pallas_call | solution.py:198
  54.0 1.0 collective-permute-start.2
  55.0 9.6 %collective-permute-done.2.rest_0_.crossed = bf16[6,128,256]{2,1,0:T(8,128)(2,1)S(1)} collective-permute-done((bf16[6,128,256]{2,1,0:T(8,128)(2,1)S(1)}, bf16[6,128,256]{2,1,0:T(8,128)(2,1)S(1)}, u32[]{:S(2)}, u32[]{:S(2)}) %collective-permute-start.2) | collective-permute-done | bytes 393248 | tf_op jit(solution)/shard_map/ppermute | solution.py:293
  64.6 4.6 %shard_map.79 = bf16[8,128,256]{2,1,0:T(8,128)(2,1)S(1)} custom-call(s32[5,8]{1,0:T(8,128)S(1)} %copy-done.1, s32[8]{0:T(128)S(1)} %copy-done.2, bf16[40,128,256]{2,1,0:T(8,128)(2,1)S(1)} %bitcast.5, bf16[40,128,256]{2,1,0:T(8,128)(2,1)S(1)} %collective-permute-done.recv, bf16[6,128,256]{2,1,0:T(8,128)(2,1)S(1)} %collective-permute-done.2.rest_0_.crossed), custom_call_target="tpu_custom_call" | custom-call | bytes 2228224 | tf_op jit(solution)/shard_map/pallas_call | solution.py:256
  69.2 1.8 %collective-permute-start.8 = (bf16[8,128,256]{2,1,0:T(8,128)(2,1)S(1)}, bf16[8,128,256]{2,1,0:T(8,128)(2,1)S(1)}, u32[]{:S(2)}, u32[]{:S(2)}) collective-permute-start(bf16[8,128,256]{2,1,0:T(8,128)(2,1)S(1)} %shard_map.79), channel_id=1, source_target_pairs={{0,4},{2,6},{4,0},{6,2},{8,12},{10,14},{12,8},{14,10},{1,5},{3,7},... | collective-permute-start | bytes 1572872 | tf_op jit(solution)/shard_map/ppermute | solution.py:308
  71.0 0.0 collective-permute-done.5
  71.0 0.1 add.9
  71.2 0.7 collective-permute-start.6
  71.9 2.0 %shard_map.76 = bf16[6,128,256]{2,1,0:T(8,128)(2,1)S(1)} custom-call(s32[5,8]{1,0:T(8,128)S(1)} %copy-done.1, bf16[40,128,256]{2,1,0:T(8,128)(2,1)S(1)} %bitcast.6, bf16[40,128,256]{2,1,0:T(8,128)(2,1)S(1)} %collective-permute-done.recv, bf16[6,128,256]{2,1,0:T(8,128)(2,1)S(1)} %collective-permute-done.2.rest_0_.crossed), custom_call_target="tpu_custom_call" | custom-call | bytes 1179648 | tf_op jit(solution)/shard_map/pallas_call | solution.py:198
  73.9 2.0 %collective-permute-start.3 = (bf16[6,128,256]{2,1,0:T(8,128)(2,1)S(1)}, bf16[6,128,256]{2,1,0:T(8,128)(2,1)S(1)}, u32[]{:S(2)}, u32[]{:S(2)}) collective-permute-start(bf16[6,128,256]{2,1,0:T(8,128)(2,1)S(1)} %shard_map.76), channel_id=1, source_target_pairs={{0,2},{2,0},{4,6},{6,4},{8,10},{10,8},{12,14},{14,12},{1,3},{3,1},... | collective-permute-start | bytes 1179656 | tf_op jit(solution)/shard_map/ppermute | solution.py:293
  75.9 7.4 %collective-permute-done.3.rest_0_.crossed = bf16[6,128,256]{2,1,0:T(8,128)(2,1)S(1)} collective-permute-done((bf16[6,128,256]{2,1,0:T(8,128)(2,1)S(1)}, bf16[6,128,256]{2,1,0:T(8,128)(2,1)S(1)}, u32[]{:S(2)}, u32[]{:S(2)}) %collective-permute-start.3) | collective-permute-done | bytes 393248 | tf_op jit(solution)/shard_map/ppermute | solution.py:293
  83.3 4.7 %shard_map.78 = bf16[8,128,256]{2,1,0:T(8,128)(2,1)S(1)} custom-call(s32[5,8]{1,0:T(8,128)S(1)} %copy-done.1, s32[8]{0:T(128)S(1)} %copy-done.2, bf16[40,128,256]{2,1,0:T(8,128)(2,1)S(1)} %bitcast.7, bf16[40,128,256]{2,1,0:T(8,128)(2,1)S(1)} %collective-permute-done.recv, bf16[6,128,256]{2,1,0:T(8,128)(2,1)S(1)} %collective-permute-done.3.rest_0_.crossed), custom_call_target="tpu_custom_call" | custom-call | bytes 2228224 | tf_op jit(solution)/shard_map/pallas_call | solution.py:256
  88.0 0.0 collective-permute-done.8
  88.0 0.1 add.11
  88.1 0.7 collective-permute-start.9
  88.8 0.0 collective-permute-done.6
  88.8 0.1 add.10
  89.0 5.5 %collective-permute-start.7 = (bf16[8,128,256]{2,1,0:T(8,128)(2,1)S(1)}, bf16[8,128,256]{2,1,0:T(8,128)(2,1)S(1)}, u32[]{:S(2)}, u32[]{:S(2)}) collective-permute-start(bf16[8,128,256]{2,1,0:T(8,128)(2,1)S(1)} %add.10), channel_id=1, source_target_pairs={{0,4},{2,6},{4,0},{6,2},{8,12},{10,14},{12,8},{14,10},{1,5},{3,7},... | collective-permute-start | bytes 1572872 | tf_op jit(solution)/shard_map/ppermute | solution.py:308
  94.5 3.1 %shard_map.77 = bf16[6,128,256]{2,1,0:T(8,128)(2,1)S(1)} custom-call(s32[5,8]{1,0:T(8,128)S(1)} %copy-done.1, bf16[40,128,256]{2,1,0:T(8,128)(2,1)S(1)} %bitcast.8, bf16[40,128,256]{2,1,0:T(8,128)(2,1)S(1)} %collective-permute-done.recv, bf16[6,128,256]{2,1,0:T(8,128)(2,1)S(1)} %collective-permute-done.3.rest_0_.crossed), custom_call_target="tpu_custom_call" | custom-call | bytes 1179648 | tf_op jit(solution)/shard_map/pallas_call | solution.py:198
  97.6 1.1 collective-permute-start.4
  98.7 6.7 %collective-permute-done.4.crossed = bf16[6,128,256]{2,1,0:T(8,128)(2,1)S(1)} collective-permute-done((bf16[6,128,256]{2,1,0:T(8,128)(2,1)S(1)}, bf16[6,128,256]{2,1,0:T(8,128)(2,1)S(1)}, u32[]{:S(2)}, u32[]{:S(2)}) %collective-permute-start.4) | collective-permute-done | bytes 393248 | tf_op jit(solution)/shard_map/ppermute | solution.py:293
  105.5 0.0 collective-permute-done.9.rest_1_
  105.5 0.0 collective-permute-done.7.rest_0_
  105.5 5.5 %shard_map.81 = bf16[8,128,256]{2,1,0:T(8,128)(2,1)} custom-call(s32[5,8]{1,0:T(8,128)S(1)} %copy-done.1, s32[8]{0:T(128)S(1)} %copy-done.2, bf16[40,128,256]{2,1,0:T(8,128)(2,1)S(1)} %bitcast.9, bf16[40,128,256]{2,1,0:T(8,128)(2,1)S(1)} %collective-permute-done.recv, bf16[6,128,256]{2,1,0:T(8,128)(2,1)S(1)} %collective-permute-done.4.crossed, ...), custom_call_target="tpu_custom_call" | custom-call | bytes 2228224 | tf_op jit(solution)/shard_map/pallas_call | solution.py:256
Async XLA Ops:
  0.8 1.2 %copy-start = (bf16[8,256,256]{2,1,0:T(8,128)(2,1)S(1)}, bf16[8,256,256]{2,1,0:T(8,128)(2,1)}, u32[]{:S(2)}) copy-start(bf16[8,256,256]{2,1,0:T(8,128)(2,1)} %psi.1) | copy-start | bytes 3145732
  2.0 0.7 copy-start.2
  2.7 0.7 copy-start.3
  3.3 27.3 %copy-start.1 = (s32[5,8]{1,0:T(8,128)S(1)}, s32[5,8]{1,0:T(8,128)}, u32[]{:S(2)}) copy-start(s32[5,8]{1,0:T(8,128)} %dest.15) | copy-start | bytes 484
  24.8 5.9 %collective-permute-start = (bf16[40,128,256]{2,1,0:T(8,128)(2,1)S(1)}, bf16[40,128,256]{2,1,0:T(8,128)(2,1)S(1)}, u32[]{:S(2)}, u32[]{:S(2)}) collective-permute-start(bf16[40,128,256]{2,1,0:T(8,128)(2,1)S(1)} %bitcast.10), channel_id=1, source_target_pairs={{0,1},{1,0},{2,3},{3,2},{4,5},{5,4},{6,7},{7,6},{8,9},{9,8},{10,11... | collective-permute-start | bytes 7864328 | tf_op jit(solution)/shard_map/ppermute | solution.py:289
  33.8 12.5 %collective-permute-start.1 = (bf16[6,128,256]{2,1,0:T(8,128)(2,1)S(1)}, bf16[6,128,256]{2,1,0:T(8,128)(2,1)S(1)}, u32[]{:S(2)}, u32[]{:S(2)}) collective-permute-start(bf16[6,128,256]{2,1,0:T(8,128)(2,1)S(1)} %shard_map.74), channel_id=1, source_target_pairs={{0,2},{2,0},{4,6},{6,4},{8,10},{10,8},{12,14},{14,12},{1,3},{3,1},... | collective-permute-start | bytes 1179656 | tf_op jit(solution)/shard_map/ppermute | solution.py:293
  50.9 20.1 %collective-permute-start.5 = (bf16[8,128,256]{2,1,0:T(8,128)(2,1)S(1)}, bf16[8,128,256]{2,1,0:T(8,128)(2,1)S(1)}, u32[]{:S(2)}, u32[]{:S(2)}) collective-permute-start(bf16[8,128,256]{2,1,0:T(8,128)(2,1)S(1)} %shard_map.80), channel_id=1, source_target_pairs={{0,4},{2,6},{4,0},{6,2},{8,12},{10,14},{12,8},{14,10},{1,5},{3,7},... | collective-permute-start | bytes 1572872 | tf_op jit(solution)/shard_map/ppermute | solution.py:308
  54.0 10.6 %collective-permute-start.2 = (bf16[6,128,256]{2,1,0:T(8,128)(2,1)S(1)}, bf16[6,128,256]{2,1,0:T(8,128)(2,1)S(1)}, u32[]{:S(2)}, u32[]{:S(2)}) collective-permute-start(bf16[6,128,256]{2,1,0:T(8,128)(2,1)S(1)} %shard_map.75), channel_id=1, source_target_pairs={{0,2},{2,0},{4,6},{6,4},{8,10},{10,8},{12,14},{14,12},{1,3},{3,1},... | collective-permute-start | bytes 1179656 | tf_op jit(solution)/shard_map/ppermute | solution.py:293
  69.2 18.8 %collective-permute-start.8 = (bf16[8,128,256]{2,1,0:T(8,128)(2,1)S(1)}, bf16[8,128,256]{2,1,0:T(8,128)(2,1)S(1)}, u32[]{:S(2)}, u32[]{:S(2)}) collective-permute-start(bf16[8,128,256]{2,1,0:T(8,128)(2,1)S(1)} %shard_map.79), channel_id=1, source_target_pairs={{0,4},{2,6},{4,0},{6,2},{8,12},{10,14},{12,8},{14,10},{1,5},{3,7},... | collective-permute-start | bytes 1572872 | tf_op jit(solution)/shard_map/ppermute | solution.py:308
  71.2 17.7 %collective-permute-start.6 = (bf16[8,128,256]{2,1,0:T(8,128)(2,1)S(1)}, bf16[8,128,256]{2,1,0:T(8,128)(2,1)S(1)}, u32[]{:S(2)}, u32[]{:S(2)}) collective-permute-start(bf16[8,128,256]{2,1,0:T(8,128)(2,1)S(1)} %add.9), channel_id=1, source_target_pairs={{4,8},{6,10},{8,4},{10,6},{5,9},{7,11},{9,5},{11,7},{20,24},{22,26... | collective-permute-start | bytes 1572872 | tf_op jit(solution)/shard_map/ppermute | solution.py:309
  73.9 9.4 %collective-permute-start.3 = (bf16[6,128,256]{2,1,0:T(8,128)(2,1)S(1)}, bf16[6,128,256]{2,1,0:T(8,128)(2,1)S(1)}, u32[]{:S(2)}, u32[]{:S(2)}) collective-permute-start(bf16[6,128,256]{2,1,0:T(8,128)(2,1)S(1)} %shard_map.76), channel_id=1, source_target_pairs={{0,2},{2,0},{4,6},{6,4},{8,10},{10,8},{12,14},{14,12},{1,3},{3,1},... | collective-permute-start | bytes 1179656 | tf_op jit(solution)/shard_map/ppermute | solution.py:293
  88.1 17.3 %collective-permute-start.9 = (bf16[8,128,256]{2,1,0:T(8,128)(2,1)S(1)}, bf16[8,128,256]{2,1,0:T(8,128)(2,1)S(1)}, u32[]{:S(2)}, u32[]{:S(2)}) collective-permute-start(bf16[8,128,256]{2,1,0:T(8,128)(2,1)S(1)} %add.11), channel_id=1, source_target_pairs={{4,8},{6,10},{8,4},{10,6},{5,9},{7,11},{9,5},{11,7},{20,24},{22,26... | collective-permute-start | bytes 1572872 | tf_op jit(solution)/shard_map/ppermute | solution.py:309
  89.0 16.5 %collective-permute-start.7 = (bf16[8,128,256]{2,1,0:T(8,128)(2,1)S(1)}, bf16[8,128,256]{2,1,0:T(8,128)(2,1)S(1)}, u32[]{:S(2)}, u32[]{:S(2)}) collective-permute-start(bf16[8,128,256]{2,1,0:T(8,128)(2,1)S(1)} %add.10), channel_id=1, source_target_pairs={{0,4},{2,6},{4,0},{6,2},{8,12},{10,14},{12,8},{14,10},{1,5},{3,7},... | collective-permute-start | bytes 1572872 | tf_op jit(solution)/shard_map/ppermute | solution.py:308
  97.6 7.8 %collective-permute-start.4 = (bf16[6,128,256]{2,1,0:T(8,128)(2,1)S(1)}, bf16[6,128,256]{2,1,0:T(8,128)(2,1)S(1)}, u32[]{:S(2)}, u32[]{:S(2)}) collective-permute-start(bf16[6,128,256]{2,1,0:T(8,128)(2,1)S(1)} %shard_map.77), channel_id=1, source_target_pairs={{0,2},{2,0},{4,6},{6,4},{8,10},{10,8},{12,14},{14,12},{1,3},{3,1},... | collective-permute-start | bytes 1179656 | tf_op jit(solution)/shard_map/ppermute | solution.py:293

commit v2 on v0

v2 whole, which is shorter than its diff:
```python
import functools

import jax
import jax.numpy as jnp
from jax import lax
from jax.experimental import pallas as pl
from jax.experimental.pallas import tpu as pltpu
from jax.sharding import PartitionSpec as P

SMEM = pl.BlockSpec(memory_space=pltpu.SMEM)
VMEM = pl.BlockSpec(memory_space=pltpu.VMEM)
Y = 2
OWN, SEND, CROSS = range(3)


def split(x, by):
    if by & (by - 1) == 0:
        return lax.shift_right_logical(x, by.bit_length() - 1), x & (by - 1)
    return x // by, lax.rem(x, by)


def wrap(x, by):
    x = jnp.where(x < 0, x + by, x)
    return jnp.where(x >= by, x - by, x)


def shifts_kernel(tc, act, rows, psi, left, right, send, keep, inner, acc):
    s = pl.program_id(0)
    n_w, blk = right.shape[0], right.shape[2]
    classes, _, half = send.shape[:3]
    me = lax.axis_index("mpo")
    line = lax.broadcasted_iota(jnp.int32, (blk, blk), 0)
    masked = jnp.where(line < rows[s], psi[0].astype(jnp.float32), 0.0).astype(jnp.bfloat16)
    for c in range(classes):
        acc[c] = jnp.zeros(acc.shape[1:], jnp.float32)
    lhs = left[...].reshape(n_w * blk, blk)
    inner[...] = jnp.dot(lhs, masked, preferred_element_type=jnp.float32).astype(jnp.bfloat16)
    for w in range(n_w):
        c = jnp.where(act[w, s] == 1, tc[w], classes)
        acc[c] += jnp.dot(inner[w * blk:(w + 1) * blk], right[w, 0], preferred_element_type=jnp.float32)
    mine = pl.multiple_of(me * half, half)
    other = pl.multiple_of((1 - me) * half, half)
    for c in range(classes):
        keep[c, 0] = acc[c, pl.ds(mine, half), :].astype(jnp.bfloat16)
        send[c, 0] = acc[c, pl.ds(other, half), :].astype(jnp.bfloat16)


def shift_sums(psi, left_env, right_env, term_class, active, sector_rows, classes):
    n_w, n_s, blk = left_env.shape[:3]
    half = blk // 2
    out = jax.ShapeDtypeStruct((classes, n_s, half, blk), jnp.bfloat16)
    block = pl.BlockSpec((classes, 1, half, blk), lambda s: (0, s, 0, 0))
    env = pl.BlockSpec((n_w, 1, blk, blk), lambda s: (0, s, 0, 0))
    return pl.pallas_call(
        shifts_kernel,
        grid=(n_s,),
        out_shape=(out, out),
        in_specs=[SMEM, SMEM, SMEM, pl.BlockSpec((1, blk, blk), lambda s: (s, 0, 0)), env, env],
        out_specs=(block, block),
        scratch_shapes=[
            pltpu.VMEM((n_w * blk, blk), jnp.bfloat16),
            pltpu.VMEM((classes + 1, blk, blk), jnp.float32),
        ],
        compiler_params=pltpu.CompilerParams(vmem_limit_bytes=40 * 2**20, dimension_semantics=("arbitrary",)),
        cost_estimate=pl.CostEstimate(
            flops=4 * n_w * n_s * blk**3, bytes_accessed=4 * n_w * n_s * blk * blk, transcendentals=0
        ),
    )(term_class, active, sector_rows, psi, left_env, right_env)


def table_at(cap, q, kind):
    return (q * 3 + kind) * (1 + 2 * cap)


def table_kernel(n, cap, dest, table):
    classes, n_s = dest.shape
    line = n // Y
    d = lax.axis_index("sector")
    z, y = split(d, Y)
    even = (z & 1) == 0

    def clear(i, _):
        table[i * (1 + 2 * cap)] = 0
        return 0

    lax.fori_loop(0, 3 * line, clear, 0)

    def position(twice):
        m = wrap(lax.shift_right_arithmetic(twice, 1), line)
        return jnp.where(m == 0, line - 1, jnp.where(even, line - 1 - m, m - 1))

    def note(q, kind, j, p):
        at = table_at(cap, q, kind)
        count = table[at]
        table[at + 1 + count] = j
        table[at + 1 + cap + count] = p
        table[at] = count + 1

    for c in range(classes):

        def step(i, _, c=c):
            t, p = split(dest[c, i], n_s)
            k = wrap(t - d, n)
            j = c * n_s + i

            @pl.when((k & 1) == 0)
            def _():
                note(position(k), OWN, j, p)

            @pl.when((k & 1) == 1)
            def _():
                note(position(k - 1 + 2 * y), SEND, j, p)
                note(position(k + 1 - 2 * y), CROSS, j, p)

            return 0

        lax.fori_loop(0, n_s, step, 0)


def make_table(n, cap, dest):
    return pl.pallas_call(
        functools.partial(table_kernel, n, cap),
        out_shape=jax.ShapeDtypeStruct((3 * (n // Y) * (1 + 2 * cap),), jnp.int32),
        in_specs=[SMEM],
        out_specs=SMEM,
        cost_estimate=pl.CostEstimate(flops=4000, bytes_accessed=4000, transcendentals=0),
    )(dest)


def joined(keep, recv, j):
    return keep[j].astype(jnp.float32) + recv[j].astype(jnp.float32)


def pack_into(out, cap, q, start, table, keep, recv):
    at = table_at(cap, q, SEND)
    rows = pl.ds(start, out.shape[1])

    def step(slot, _):
        j = table[at + 1 + slot]
        out[slot] = (keep[j, rows].astype(jnp.float32) + recv[j, rows].astype(jnp.float32)).astype(jnp.bfloat16)
        return 0

    lax.fori_loop(0, table[at], step, 0)


def pack(cap, q, pieces, table, keep, recv):
    blk = keep.shape[2]

    def kernel(table, keep, recv, *outs):
        for out, (start, size) in zip(outs, pieces):
            pack_into(out, cap, q, start, table, keep, recv)

    return pl.pallas_call(
        kernel,
        out_shape=[jax.ShapeDtypeStruct((cap, size, blk), jnp.bfloat16) for _, size in pieces],
        in_specs=[SMEM, VMEM, VMEM],
        out_specs=[VMEM] * len(pieces),
        compiler_params=pltpu.CompilerParams(vmem_limit_bytes=16 * 2**20),
        cost_estimate=pl.CostEstimate(flops=0, bytes_accessed=1000, transcendentals=0),
    )(table, keep, recv)


def pack_rest(cap, line, pieces, table, keep, recv, after):
    blk = keep.shape[2]
    flat = [(q, piece) for q in range(1, line) for piece in pieces[q]]

    def kernel(table, keep, recv, after, *packed):
        for (q, (start, _)), out in zip(flat, packed):
            pack_into(out, cap, q, start, table, keep, recv)

    outs = pl.pallas_call(
        kernel,
        out_shape=[jax.ShapeDtypeStruct((cap, size, blk), jnp.bfloat16) for _, (_, size) in flat],
        in_specs=[SMEM, VMEM, VMEM, pl.BlockSpec(memory_space=pl.ANY)],
        out_specs=[VMEM] * len(flat),
        compiler_params=pltpu.CompilerParams(vmem_limit_bytes=16 * 2**20),
        cost_estimate=pl.CostEstimate(flops=0, bytes_accessed=1000, transcendentals=0),
    )(table, keep, recv, after)
    return [[x for (at, _), x in zip(flat, outs) if at == q] for q in range(1, line)]


def add_own(cap, line, n_s, table, keep, recv, firsts):
    half, blk = keep.shape[1:]

    def kernel(table, keep, recv, *refs):
        own = refs[len(firsts):]
        for q in range(line):
            own[q][...] = jnp.zeros(own[q].shape, jnp.float32)
            at = table_at(cap, q, OWN)

            def step(slot, _, q=q, at=at):
                block = joined(keep, recv, table[at + 1 + slot]).astype(jnp.bfloat16)
                own[q][table[at + 1 + cap + slot]] += block.astype(jnp.float32)
                return 0

            lax.fori_loop(0, table[at], step, 0)

    return pl.pallas_call(
        kernel,
        out_shape=[jax.ShapeDtypeStruct((n_s, half, blk), jnp.float32)] * line,
        in_specs=[SMEM, VMEM, VMEM] + [pl.BlockSpec(memory_space=pl.ANY)] * len(firsts),
        out_specs=[VMEM] * line,
        compiler_params=pltpu.CompilerParams(vmem_limit_bytes=24 * 2**20),
        cost_estimate=pl.CostEstimate(flops=0, bytes_accessed=1000, transcendentals=0),
    )(table, keep, recv, *firsts)


def gather(cap, q, piece, table, own, crossed):
    n_s, _, blk = own.shape
    start, size = piece
    at = table_at(cap, q, CROSS)

    def kernel(table, own, crossed, out, total):
        total[...] = own[:, start:start + size]

        def step(slot, _):
            total[table[at + 1 + cap + slot]] += crossed[slot].astype(jnp.float32)
            return 0

        lax.fori_loop(0, table[at], step, 0)
        out[...] = total[...].astype(jnp.bfloat16)

    return pl.pallas_call(
        kernel,
        out_shape=jax.ShapeDtypeStruct((n_s, size, blk), jnp.bfloat16),
        in_specs=[SMEM, VMEM, VMEM],
        out_specs=VMEM,
        scratch_shapes=[pltpu.VMEM((n_s, size, blk), jnp.float32)],
        compiler_params=pltpu.CompilerParams(vmem_limit_bytes=16 * 2**20),
        cost_estimate=pl.CostEstimate(flops=0, bytes_accessed=1000, transcendentals=0),
    )(table, own, crossed)


def finish(cap, q, table, rows, own, crossed, arrived):
    n_s, half, blk = own.shape
    at = table_at(cap, q, CROSS)
    spots = [start for start, _ in arrived]

    def kernel(table, rows, own, crossed, *rest):
        parts, (out, total) = rest[:-2], rest[-2:]
        total[...] = own[...]

        def step(slot, _):
            total[table[at + 1 + cap + slot]] += crossed[slot].astype(jnp.float32)
            return 0

        lax.fori_loop(0, table[at], step, 0)
        for start, part in zip(spots, parts):
            total[:, start:start + part.shape[1]] += part[...].astype(jnp.float32)
        line = lax.broadcasted_iota(jnp.int32, (half, blk), 0) + lax.axis_index("mpo") * half
        for p in range(n_s):
            out[p] = jnp.where(line < rows[p], total[p], 0.0).astype(jnp.bfloat16)

    return pl.pallas_call(
        kernel,
        out_shape=jax.ShapeDtypeStruct((n_s, half, blk), jnp.bfloat16),
        in_specs=[SMEM, SMEM, VMEM, VMEM] + [VMEM] * len(arrived),
        out_specs=VMEM,
        scratch_shapes=[pltpu.VMEM((n_s, half, blk), jnp.float32)],
        compiler_params=pltpu.CompilerParams(vmem_limit_bytes=16 * 2**20),
        cost_estimate=pl.CostEstimate(flops=0, bytes_accessed=1000, transcendentals=0),
    )(table, rows, own, crossed, *[part for _, part in arrived])


def plus(a, a_start, b, b_start, size):
    def kernel(a, b, out):
        total = a[:, a_start:a_start + size].astype(jnp.float32) + b[:, b_start:b_start + size].astype(jnp.float32)
        out[...] = total.astype(jnp.bfloat16)

    return pl.pallas_call(
        kernel,
        out_shape=jax.ShapeDtypeStruct((a.shape[0], size, a.shape[2]), jnp.bfloat16),
        in_specs=[VMEM, VMEM],
        out_specs=VMEM,
        compiler_params=pltpu.CompilerParams(vmem_limit_bytes=16 * 2**20),
        cost_estimate=pl.CostEstimate(flops=0, bytes_accessed=1000, transcendentals=0),
    )(a, b)


def sums(a_parts, b_parts, piece):
    start, size = piece

    def holder(parts):
        for first, x in parts:
            if first <= start and start + size <= first + x.shape[1]:
                return x, start - first
        return some_rows(parts, piece), 0

    return plus(*holder(a_parts), *holder(b_parts), size)


def some_rows(parts, piece):
    start, size = piece
    got = []
    for first, part in parts:
        low, high = max(first, start), min(first + part.shape[1], start + size)
        if low < high:
            got.append(part if (low, high) == (first, first + part.shape[1]) else part[:, low - first:high - first])
    return got[0] if len(got) == 1 else jnp.concatenate(got, axis=1)


def body(psi, left_env, right_env, term_class, active, dest, sector_rows):
    n = lax.axis_size("sector")
    line = n // Y
    classes, n_s = dest.shape
    blk = psi.shape[1]
    half = blk // 2
    cap = (classes * n_s + n - 1) // n + 1
    whole = [(0, half)]
    halves = [(0, half // 2), (half // 2, half // 2)]
    across = [(d, d ^ 1) for d in range(n)]
    near = [(z * Y + y, (z ^ 1) * Y + y) for z in range(line) for y in range(Y)]
    far = [(z * Y + y, (((z + 1) ^ 1) - 1) * Y + y) for z in range(1, line - 1) for y in range(Y)]

    send, keep = shift_sums(psi, left_env, right_env, term_class, active, sector_rows, classes)
    send, keep = (x.reshape(classes * n_s, half, blk) for x in (send, keep))
    recv = lax.ppermute(send, "mpo", [(0, 1), (1, 0)])
    table = make_table(n, cap, dest)
    pieces = [halves] * (line - 1) + [whole]
    firsts = pack(cap, 0, pieces[0], table, keep, recv)
    crossed = [[lax.ppermute(x, "sector", across) for x in firsts]]
    own = add_own(cap, line, n_s, table, keep, recv, firsts)
    packed = pack_rest(cap, line, pieces, table, keep, recv, crossed[0][0])
    crossed += [[lax.ppermute(x, "sector", across) for x in xs] for xs in packed]

    acc = []
    for q in range(line - 1):
        acc.append([(piece[0], gather(cap, q, piece, table, own[q], x)) for piece, x in zip(pieces[q], crossed[q])])
    near_in, far_in = None, None
    for step in range(1, line):
        near_out, far_out = [], []
        for piece in halves:
            if far_in is None:
                near_out.append((piece[0], some_rows(acc[step - 1], piece)))
            else:
                near_out.append((piece[0], sums(acc[step - 1], far_in, piece)))
        if step > 1:
            for piece in halves:
                far_out.append((piece[0], sums(acc[line - 1 - step], near_in, piece)))
        near_in = [(start, lax.ppermute(x, "sector", near)) for start, x in near_out]
        far_in = [(start, lax.ppermute(x, "sector", far)) for start, x in far_out] if far_out else None
    return finish(cap, line - 1, table, sector_rows, own[line - 1], crossed[line - 1][0], near_in + (far_in or []))


def solution(mesh):
    placed = (
        P(("groups", "sector"), None, None),
        P(("groups", "mpo"), "sector", None, None),
        P(("groups", "mpo"), "sector", None, None),
        P(("groups", "mpo")),
        P(("groups", "mpo"), "sector"),
        P("groups", "sector"),
        P(("groups", "sector")),
    )
    return jax.shard_map(
        body,
        mesh=mesh,
        in_specs=placed,
        out_specs=P(("groups", "sector"), "mpo", None),
        check_vma=False,
    )
```

time: 223 us -> 80.7 us (0.36)
  matrix products: 86.3 us -> 0 us
  waiting for transfers between devices: 94.4 us -> 20 us
  Pallas kernels: 0 us -> 31.7 us
  between operations: 13.5 us -> 0.2 us
  starting transfers between devices: 13.1 us -> 24.4 us
  local copies, waits for them, and re-layouts: 9.94 us -> 3.99 us
  other arithmetic: 5.14 us -> 0 us
    dot_general x5 -> x0, matrix products: 86.3 us -> none  [the longest x1 53 us: body(): jnp.einsum('cws,wsik->csik', weights, terms, precision=lax.Precision.HIGH...]
    all_to_all x2 -> x0, waiting for transfers between devices: 69.8 us -> none  [the longest x1 69.8 us: body(): lax.all_to_all(packed, 'sector', split_axis=0, concat_axis=0, tiled=True)]
    pallas_call x0 -> x18, Pallas kernels: none -> 31.7 us  [the longest x1 15.9 us: shift_sums(): pl.pallas_call(shifts_kernel, grid=(n_s,), out_shape=(out, out), in_specs...]
    psum x1 -> x0, waiting for transfers between devices: 24.6 us -> none  [body(): lax.psum(partial_sum.astype(jnp.bfloat16), 'mpo').astype(jnp.float32)]
    ppermute x0 -> x18, starting transfers between devices: none -> 24.4 us  [the longest x6 12.2 us: body(): lax.ppermute(x, 'sector', near)]
    ppermute x0 -> x18, waiting for transfers between devices: none -> 20 us  [the longest x6 10.5 us: body(): lax.ppermute(x, 'sector', near)]
    all_to_all x2 -> x0, starting transfers between devices: 13.1 us -> none  [the longest x1 7.28 us: body(): lax.all_to_all(slot_target, 'sector', split_axis=0, concat_axis=0, tiled=...]
    dot_general x1 -> x0, local copies, waits for them, and re-layouts: 3.7 us -> none  [body(): jnp.einsum('cws,wsik->csik', weights, terms, precision=lax.Precision.HIGH...]
  transfers between devices with their start and end apart: 3 -> 18, of which waited for: 2 -> 8; matrix products, arithmetic and copies ran while one was open for 4% -> 0% of each run, Pallas kernels for 0% -> 15%
where the time goes in v2:
time: 80.7 us; the launch traced here: 80.2 us
  Pallas kernels  31.7 us (39%)
  starting transfers between devices  24.4 us (30%)
  waiting for transfers between devices  20 us (25%)
  local copies, waits for them, and re-layouts  3.99 us (5%)
    pallas_call x1, Pallas kernels, shift_sums(): pl.pallas_call(shifts_kernel, grid=(n_s,), out_shape=(out, out), in_specs...  15.9 us
    ppermute x6, starting transfers between devices, body(): lax.ppermute(x, 'sector', near)  12.2 us
    ppermute x6, waiting for transfers between devices, body(): lax.ppermute(x, 'sector', near)  10.5 us
    ppermute x5, starting transfers between devices, body(): lax.ppermute(x, 'sector', across)  6 us
    ppermute x5, waiting for transfers between devices, body(): lax.ppermute(x, 'sector', across)  4.6 us
    unnamed x13, local copies, waits for them, and re-layouts  3.99 us
    pallas_call x6, Pallas kernels, gather(): pl.pallas_call(kernel, out_shape=jax.ShapeDtypeStruct((n_s, size, blk), j...  3.92 us
    ppermute x2, starting transfers between devices, body(): crossed = [[lax.ppermute(x, 'sector', across) for x in firsts]]  3.03 us
  transfers between devices with their start and end apart: 18, of which 8 were waited for; matrix products, arithmetic and copies ran while one was open for 0% of the time, Pallas kernels for 15%

profile of v2, /device:TPU:0, one launch (start us, length us, event | category | flops | bytes accessed | tf_op | source)
XLA Modules:
  0.0 80.2 jit_solution(570973684110281510)
XLA Ops:
  0.0 0.8 copy.8.act
  0.8 0.0 copy-start
  0.8 1.2 %copy-done = bf16[8,256,256]{2,1,0:T(8,128)(2,1)S(1)} copy-done((bf16[8,256,256]{2,1,0:T(8,128)(2,1)S(1)}, bf16[8,256,256]{2,1,0:T(8,128)(2,1)}, u32[]{:S(2)}) %copy-start) | copy-done | bytes 1048600
  2.0 0.0 copy-start.3
  2.0 0.7 copy-done.3
  2.7 0.7 copy-done.5
  3.3 15.9 %shard_map.74 = (bf16[5,8,128,256]{3,2,1,0:T(8,128)(2,1)}, bf16[5,8,128,256]{3,2,1,0:T(8,128)(2,1)S(1)}) custom-call(s32[13]{0:T(128)S(1)} %copy-done.5, s32[13,8]{1,0:T(8,128)S(1)} %copy.8.act, s32[8]{0:T(128)S(1)} %copy-done.3, bf16[8,256,256]{2,1,0:T(8,128)(2,1)S(1)} %copy-done, bf16[13,8,256,256]{3,2,1,0:T(8,128)(2,1)} %left.1, ...), custom_call_target="tpu_custom_call" | custom-call | flops 6979321856 | bytes 27262976 | tf_op jit(solution)/shard_map/pallas_call | solution.py:54
  19.2 0.5 collective-permute-start
  19.6 2.9 %shard_map.73.table = s32[156]{0:T(256)} custom-call(s32[5,8]{1,0:T(8,128)} %dest.1), custom_call_target="tpu_custom_call" | custom-call | flops 4000 | bytes 4000 | tf_op jit(solution)/shard_map/pallas_call | solution.py:121
  22.6 1.9 %collective-permute-done.recv = bf16[40,128,256]{2,1,0:T(8,128)(2,1)} collective-permute-done((bf16[40,128,256]{2,1,0:T(8,128)(2,1)}, bf16[40,128,256]{2,1,0:T(8,128)(2,1)}, u32[]{:S(2)}, u32[]{:S(2)}) %collective-permute-start) | collective-permute-done | bytes 2621472 | tf_op jit(solution)/shard_map/ppermute | solution.py:317
  24.5 0.7 copy-done.1
  25.2 2.0 %shard_map.75 = (bf16[6,64,256]{2,1,0:T(8,128)(2,1)S(1)}, bf16[6,64,256]{2,1,0:T(8,128)(2,1)S(1)}) custom-call(s32[156]{0:T(256)S(1)} %copy-done.1, bf16[40,128,256]{2,1,0:T(8,128)(2,1)S(1)} %bitcast.2, bf16[40,128,256]{2,1,0:T(8,128)(2,1)} %collective-permute-done.recv), custom_call_target="tpu_custom_call" | custom-call | bytes 1000 | tf_op jit(solution)/shard_map/pallas_call | solution.py:153
  27.2 3.0 %collective-permute-start.1 = (bf16[6,64,256]{2,1,0:T(8,128)(2,1)S(1)}, bf16[6,64,256]{2,1,0:T(8,128)(2,1)S(1)}, u32[]{:S(2)}, u32[]{:S(2)}) collective-permute-start(bf16[6,64,256]{2,1,0:T(8,128)(2,1)S(1)} %get-tuple-element.20.refs_0_), channel_id=1, source_target_pairs={{0,2},{2,0},{4,6},{6,4},{8,10},{10,8},{12,14},{14,12},{1,3},{3,1},... | collective-permute-start | bytes 589832 | tf_op jit(solution)/shard_map/ppermute | solution.py:321
  30.1 0.1 collective-permute-start.10
  30.2 0.0 copy-done.2
  30.2 2.7 %shard_map.76 = (f32[8,128,256]{2,1,0:T(8,128)S(1)}, f32[8,128,256]{2,1,0:T(8,128)S(1)}, f32[8,128,256]{2,1,0:T(8,128)S(1)}, f32[8,128,256]{2,1,0:T(8,128)S(1)}) custom-call(s32[156]{0:T(256)S(1)} %copy-done.2, bf16[40,128,256]{2,1,0:T(8,128)(2,1)S(1)} %bitcast.3, bf16[40,128,256]{2,1,0:T(8,128)(2,1)} %collective-permute-done.recv, ...), custom_call_target="tpu_custom_call" | custom-call | bytes 1000 | tf_op jit(solution)/shard_map/pallas_call | solution.py:198
  32.9 2.9 %collective-permute-done.1.after.crossed = bf16[6,64,256]{2,1,0:T(8,128)(2,1)S(1)} collective-permute-done((bf16[6,64,256]{2,1,0:T(8,128)(2,1)S(1)}, bf16[6,64,256]{2,1,0:T(8,128)(2,1)S(1)}, u32[]{:S(2)}, u32[]{:S(2)}) %collective-permute-start.1) | collective-permute-done | bytes 196640 | tf_op jit(solution)/shard_map/ppermute | solution.py:321
  35.8 2.1 %shard_map.77 = (bf16[6,64,256]{2,1,0:T(8,128)(2,1)S(1)}, bf16[6,64,256]{2,1,0:T(8,128)(2,1)S(1)}, bf16[6,64,256]{2,1,0:T(8,128)(2,1)S(1)}, bf16[6,64,256]{2,1,0:T(8,128)(2,1)S(1)}, bf16[6,128,256]{2,1,0:T(8,128)(2,1)S(1)}) custom-call(s32[156]{0:T(256)S(1)} %copy-done.2, bf16[40,128,256]{2,1,0:T(8,128)(2,1)S(1)} %bitcast.4, ...), custom_call_target="tpu_custom_call" | custom-call | bytes 1000 | tf_op jit(solution)/shard_map/pallas_call | solution.py:171
  37.9 2.1 %collective-permute-start.4 = (bf16[6,64,256]{2,1,0:T(8,128)(2,1)S(1)}, bf16[6,64,256]{2,1,0:T(8,128)(2,1)S(1)}, u32[]{:S(2)}, u32[]{:S(2)}) collective-permute-start(bf16[6,64,256]{2,1,0:T(8,128)(2,1)S(1)} %get-tuple-element.27), channel_id=1, source_target_pairs={{0,2},{2,0},{4,6},{6,4},{8,10},{10,8},{12,14},{14,12},{1,3},{3,1},... | collective-permute-start | bytes 589832 | tf_op jit(solution)/shard_map/ppermute | solution.py:324
  40.0 0.7 shard_map.80.a
  40.7 1.6 %collective-permute-start.5 = (bf16[8,64,256]{2,1,0:T(8,128)(2,1)S(1)}, bf16[8,64,256]{2,1,0:T(8,128)(2,1)S(1)}, u32[]{:S(2)}, u32[]{:S(2)}) collective-permute-start(bf16[8,64,256]{2,1,0:T(8,128)(2,1)S(1)} %shard_map.80.a), channel_id=1, source_target_pairs={{0,4},{2,6},{4,0},{6,2},{8,12},{10,14},{12,8},{14,10},{1,5},{3,7},... | collective-permute-start | bytes 786440 | tf_op jit(solution)/shard_map/ppermute | solution.py:340
  42.4 0.0 collective-permute-done.10.crossed
  42.4 0.7 shard_map.85.a
  43.0 0.5 collective-permute-start.11
  43.6 0.1 collective-permute-start.9
  43.6 2.0 %collective-permute-start.3 = (bf16[6,64,256]{2,1,0:T(8,128)(2,1)S(1)}, bf16[6,64,256]{2,1,0:T(8,128)(2,1)S(1)}, u32[]{:S(2)}, u32[]{:S(2)}) collective-permute-start(bf16[6,64,256]{2,1,0:T(8,128)(2,1)S(1)} %get-tuple-element.25), channel_id=1, source_target_pairs={{0,2},{2,0},{4,6},{6,4},{8,10},{10,8},{12,14},{14,12},{1,3},{3,1},... | collective-permute-start | bytes 589832 | tf_op jit(solution)/shard_map/ppermute | solution.py:324
  45.6 0.0 collective-permute-done.4.crossed
  45.6 0.6 collective-permute-start.8
  46.2 0.6 shard_map.79.a
  46.8 4.6 %collective-permute-done.9.crossed = bf16[6,64,256]{2,1,0:T(8,128)(2,1)S(1)} collective-permute-done((bf16[6,64,256]{2,1,0:T(8,128)(2,1)S(1)}, bf16[6,64,256]{2,1,0:T(8,128)(2,1)S(1)}, u32[]{:S(2)}, u32[]{:S(2)}) %collective-permute-start.9) | collective-permute-done | bytes 196640 | tf_op jit(solution)/shard_map/ppermute | solution.py:324
  51.4 1.6 %collective-permute-start.14 = (bf16[8,64,256]{2,1,0:T(8,128)(2,1)S(1)}, bf16[8,64,256]{2,1,0:T(8,128)(2,1)S(1)}, u32[]{:S(2)}, u32[]{:S(2)}) collective-permute-start(bf16[8,64,256]{2,1,0:T(8,128)(2,1)S(1)} %shard_map.79.a), channel_id=1, source_target_pairs={{0,4},{2,6},{4,0},{6,2},{8,12},{10,14},{12,8},{14,10},{1,5},{3,7},... | collective-permute-start | bytes 786440 | tf_op jit(solution)/shard_map/ppermute | solution.py:340
  53.0 0.6 shard_map.84.a
  53.6 0.0 collective-permute-done.5.b
  53.6 0.5 collective-permute-start.16
  54.1 0.1 shard_map.81
  54.2 1.5 %collective-permute-done.11.b = bf16[8,64,256]{2,1,0:T(8,128)(2,1)S(1)} collective-permute-done((bf16[8,64,256]{2,1,0:T(8,128)(2,1)S(1)}, bf16[8,64,256]{2,1,0:T(8,128)(2,1)S(1)}, u32[]{:S(2)}, u32[]{:S(2)}) %collective-permute-start.11) | collective-permute-done | bytes 262176 | tf_op jit(solution)/shard_map/ppermute | solution.py:340
  55.6 0.7 collective-permute-start.6
  56.3 0.1 shard_map.86
  56.4 0.0 collective-permute-done.3.crossed
  56.4 0.7 collective-permute-start.12
  57.1 0.0 collective-permute-done.8.crossed
  57.1 1.3 %collective-permute-start.2 = (bf16[6,128,256]{2,1,0:T(8,128)(2,1)S(1)}, bf16[6,128,256]{2,1,0:T(8,128)(2,1)S(1)}, u32[]{:S(2)}, u32[]{:S(2)}) collective-permute-start(bf16[6,128,256]{2,1,0:T(8,128)(2,1)S(1)} %get-tuple-element.23), channel_id=1, source_target_pairs={{0,2},{2,0},{4,6},{6,4},{8,10},{10,8},{12,14},{14,12},{1,3},{3,1},... | collective-permute-start | bytes 1179656 | tf_op jit(solution)/shard_map/ppermute | solution.py:324
  58.3 0.7 shard_map.78.a
  59.0 0.0 copy-start.4
  59.0 0.7 shard_map.83.a
  59.7 1.5 %collective-permute-done.14.b = bf16[8,64,256]{2,1,0:T(8,128)(2,1)S(1)} collective-permute-done((bf16[8,64,256]{2,1,0:T(8,128)(2,1)S(1)}, bf16[8,64,256]{2,1,0:T(8,128)(2,1)S(1)}, u32[]{:S(2)}, u32[]{:S(2)}) %collective-permute-start.14) | collective-permute-done | bytes 262176 | tf_op jit(solution)/shard_map/ppermute | solution.py:340
  61.3 0.1 shard_map.88
  61.3 0.7 collective-permute-start.15
  62.0 2.1 %collective-permute-done.16.b = bf16[8,64,256]{2,1,0:T(8,128)(2,1)S(1)} collective-permute-done((bf16[8,64,256]{2,1,0:T(8,128)(2,1)S(1)}, bf16[8,64,256]{2,1,0:T(8,128)(2,1)S(1)}, u32[]{:S(2)}, u32[]{:S(2)}) %collective-permute-start.16) | collective-permute-done | bytes 262176 | tf_op jit(solution)/shard_map/ppermute | solution.py:340
  64.1 0.1 shard_map.89
  64.1 0.7 collective-permute-start.17
  64.8 0.0 collective-permute-done.6.b
  64.8 0.1 shard_map.82
  64.9 6.0 %collective-permute-start.7 = (bf16[8,64,256]{2,1,0:T(8,128)(2,1)S(1)}, bf16[8,64,256]{2,1,0:T(8,128)(2,1)S(1)}, u32[]{:S(2)}, u32[]{:S(2)}) collective-permute-start(bf16[8,64,256]{2,1,0:T(8,128)(2,1)S(1)} %shard_map.82), channel_id=1, source_target_pairs={{0,4},{2,6},{4,0},{6,2},{8,12},{10,14},{12,8},{14,10},{1,5},{3,7},... | collective-permute-start | bytes 786440 | tf_op jit(solution)/shard_map/ppermute | solution.py:340
  70.9 0.0 collective-permute-done.12.b
  70.9 0.1 shard_map.87
  71.0 1.9 %collective-permute-start.13 = (bf16[8,64,256]{2,1,0:T(8,128)(2,1)S(1)}, bf16[8,64,256]{2,1,0:T(8,128)(2,1)S(1)}, u32[]{:S(2)}, u32[]{:S(2)}) collective-permute-start(bf16[8,64,256]{2,1,0:T(8,128)(2,1)S(1)} %shard_map.87), channel_id=1, source_target_pairs={{0,4},{2,6},{4,0},{6,2},{8,12},{10,14},{12,8},{14,10},{1,5},{3,7},... | collective-permute-start | bytes 786440 | tf_op jit(solution)/shard_map/ppermute | solution.py:340
  72.9 0.0 collective-permute-done.2.crossed
  72.9 0.0 collective-permute-done.15.rest_2_
  72.9 0.0 collective-permute-done.17.rest_3_
  72.9 2.7 %collective-permute-done.7.rest_0_ = bf16[8,64,256]{2,1,0:T(8,128)(2,1)S(1)} collective-permute-done((bf16[8,64,256]{2,1,0:T(8,128)(2,1)S(1)}, bf16[8,64,256]{2,1,0:T(8,128)(2,1)S(1)}, u32[]{:S(2)}, u32[]{:S(2)}) %collective-permute-start.7) | collective-permute-done | bytes 262176 | tf_op jit(solution)/shard_map/ppermute | solution.py:340
  75.6 2.8 %collective-permute-done.13.rest_1_ = bf16[8,64,256]{2,1,0:T(8,128)(2,1)S(1)} collective-permute-done((bf16[8,64,256]{2,1,0:T(8,128)(2,1)S(1)}, bf16[8,64,256]{2,1,0:T(8,128)(2,1)S(1)}, u32[]{:S(2)}, u32[]{:S(2)}) %collective-permute-start.13) | collective-permute-done | bytes 262176 | tf_op jit(solution)/shard_map/ppermute | solution.py:340
  78.4 0.0 copy-done.4
  78.4 1.8 %shard_map.90 = bf16[8,128,256]{2,1,0:T(8,128)(2,1)} custom-call(s32[156]{0:T(256)S(1)} %copy-done.2, s32[8]{0:T(128)S(1)} %copy-done.4, f32[8,128,256]{2,1,0:T(8,128)S(1)} %get-tuple-element.22.own, bf16[6,128,256]{2,1,0:T(8,128)(2,1)S(1)} %collective-permute-done.2.crossed, bf16[8,64,256]{2,1,0:T(8,128)(2,1)S(1)} %collective-permute-done.7.rest_0_, ...), custom_call_target="tpu_custom_call" | custom-call | bytes 1000 | tf_op jit(solution)/shard_map/pallas_call | solution.py:254
  (3 shorter events, 0.0 us)
Async XLA Ops:
  0.8 1.2 %copy-start = (bf16[8,256,256]{2,1,0:T(8,128)(2,1)S(1)}, bf16[8,256,256]{2,1,0:T(8,128)(2,1)}, u32[]{:S(2)}) copy-start(bf16[8,256,256]{2,1,0:T(8,128)(2,1)} %psi.1) | copy-start | bytes 3145732
  2.0 0.7 copy-start.3
  2.7 0.7 copy-start.5
  19.2 5.3 %collective-permute-start = (bf16[40,128,256]{2,1,0:T(8,128)(2,1)}, bf16[40,128,256]{2,1,0:T(8,128)(2,1)}, u32[]{:S(2)}, u32[]{:S(2)}) collective-permute-start(bf16[40,128,256]{2,1,0:T(8,128)(2,1)} %bitcast.1), channel_id=1, source_target_pairs={{0,1},{1,0},{2,3},{3,2},{4,5},{5,4},{6,7},{7,6},{8,9},{9,8},{10,11... | collective-permute-start | bytes 7864328 | tf_op jit(solution)/shard_map/ppermute | solution.py:317
  24.5 0.7 copy-start.1
  25.2 5.0 %copy-start.2 = (s32[156]{0:T(256)S(1)}, s32[156]{0:T(256)}, u32[]{:S(2)}) copy-start(s32[156]{0:T(256)} %shard_map.73.table) | copy-start | bytes 1876
  27.2 8.6 %collective-permute-start.1 = (bf16[6,64,256]{2,1,0:T(8,128)(2,1)S(1)}, bf16[6,64,256]{2,1,0:T(8,128)(2,1)S(1)}, u32[]{:S(2)}, u32[]{:S(2)}) collective-permute-start(bf16[6,64,256]{2,1,0:T(8,128)(2,1)S(1)} %get-tuple-element.20.refs_0_), channel_id=1, source_target_pairs={{0,2},{2,0},{4,6},{6,4},{8,10},{10,8},{12,14},{14,12},{1,3},{3,1},... | collective-permute-start | bytes 589832 | tf_op jit(solution)/shard_map/ppermute | solution.py:321
  30.1 12.2 %collective-permute-start.10 = (bf16[6,64,256]{2,1,0:T(8,128)(2,1)S(1)}, bf16[6,64,256]{2,1,0:T(8,128)(2,1)S(1)}, u32[]{:S(2)}, u32[]{:S(2)}) collective-permute-start(bf16[6,64,256]{2,1,0:T(8,128)(2,1)S(1)} %get-tuple-element.21.refs_1_), channel_id=1, source_target_pairs={{0,2},{2,0},{4,6},{6,4},{8,10},{10,8},{12,14},{14,12},{1,3},{3,1},... | collective-permute-start | bytes 589832 | tf_op jit(solution)/shard_map/ppermute | solution.py:321
  37.9 7.7 %collective-permute-start.4 = (bf16[6,64,256]{2,1,0:T(8,128)(2,1)S(1)}, bf16[6,64,256]{2,1,0:T(8,128)(2,1)S(1)}, u32[]{:S(2)}, u32[]{:S(2)}) collective-permute-start(bf16[6,64,256]{2,1,0:T(8,128)(2,1)S(1)} %get-tuple-element.27), channel_id=1, source_target_pairs={{0,2},{2,0},{4,6},{6,4},{8,10},{10,8},{12,14},{14,12},{1,3},{3,1},... | collective-permute-start | bytes 589832 | tf_op jit(solution)/shard_map/ppermute | solution.py:324
  40.7 12.9 %collective-permute-start.5 = (bf16[8,64,256]{2,1,0:T(8,128)(2,1)S(1)}, bf16[8,64,256]{2,1,0:T(8,128)(2,1)S(1)}, u32[]{:S(2)}, u32[]{:S(2)}) collective-permute-start(bf16[8,64,256]{2,1,0:T(8,128)(2,1)S(1)} %shard_map.80.a), channel_id=1, source_target_pairs={{0,4},{2,6},{4,0},{6,2},{8,12},{10,14},{12,8},{14,10},{1,5},{3,7},... | collective-permute-start | bytes 786440 | tf_op jit(solution)/shard_map/ppermute | solution.py:340
  43.0 12.6 %collective-permute-start.11 = (bf16[8,64,256]{2,1,0:T(8,128)(2,1)S(1)}, bf16[8,64,256]{2,1,0:T(8,128)(2,1)S(1)}, u32[]{:S(2)}, u32[]{:S(2)}) collective-permute-start(bf16[8,64,256]{2,1,0:T(8,128)(2,1)S(1)} %shard_map.85.a), channel_id=1, source_target_pairs={{0,4},{2,6},{4,0},{6,2},{8,12},{10,14},{12,8},{14,10},{1,5},{3,7},... | collective-permute-start | bytes 786440 | tf_op jit(solution)/shard_map/ppermute | solution.py:340
  43.6 7.8 %collective-permute-start.9 = (bf16[6,64,256]{2,1,0:T(8,128)(2,1)S(1)}, bf16[6,64,256]{2,1,0:T(8,128)(2,1)S(1)}, u32[]{:S(2)}, u32[]{:S(2)}) collective-permute-start(bf16[6,64,256]{2,1,0:T(8,128)(2,1)S(1)} %get-tuple-element.30), channel_id=1, source_target_pairs={{0,2},{2,0},{4,6},{6,4},{8,10},{10,8},{12,14},{14,12},{1,3},{3,1},... | collective-permute-start | bytes 589832 | tf_op jit(solution)/shard_map/ppermute | solution.py:324
  43.6 12.8 %collective-permute-start.3 = (bf16[6,64,256]{2,1,0:T(8,128)(2,1)S(1)}, bf16[6,64,256]{2,1,0:T(8,128)(2,1)S(1)}, u32[]{:S(2)}, u32[]{:S(2)}) collective-permute-start(bf16[6,64,256]{2,1,0:T(8,128)(2,1)S(1)} %get-tuple-element.25), channel_id=1, source_target_pairs={{0,2},{2,0},{4,6},{6,4},{8,10},{10,8},{12,14},{14,12},{1,3},{3,1},... | collective-permute-start | bytes 589832 | tf_op jit(solution)/shard_map/ppermute | solution.py:324
  45.6 11.5 %collective-permute-start.8 = (bf16[6,64,256]{2,1,0:T(8,128)(2,1)S(1)}, bf16[6,64,256]{2,1,0:T(8,128)(2,1)S(1)}, u32[]{:S(2)}, u32[]{:S(2)}) collective-permute-start(bf16[6,64,256]{2,1,0:T(8,128)(2,1)S(1)} %get-tuple-element.29), channel_id=1, source_target_pairs={{0,2},{2,0},{4,6},{6,4},{8,10},{10,8},{12,14},{14,12},{1,3},{3,1},... | collective-permute-start | bytes 589832 | tf_op jit(solution)/shard_map/ppermute | solution.py:324
  51.4 9.9 %collective-permute-start.14 = (bf16[8,64,256]{2,1,0:T(8,128)(2,1)S(1)}, bf16[8,64,256]{2,1,0:T(8,128)(2,1)S(1)}, u32[]{:S(2)}, u32[]{:S(2)}) collective-permute-start(bf16[8,64,256]{2,1,0:T(8,128)(2,1)S(1)} %shard_map.79.a), channel_id=1, source_target_pairs={{0,4},{2,6},{4,0},{6,2},{8,12},{10,14},{12,8},{14,10},{1,5},{3,7},... | collective-permute-start | bytes 786440 | tf_op jit(solution)/shard_map/ppermute | solution.py:340
  53.6 10.5 %collective-permute-start.16 = (bf16[8,64,256]{2,1,0:T(8,128)(2,1)S(1)}, bf16[8,64,256]{2,1,0:T(8,128)(2,1)S(1)}, u32[]{:S(2)}, u32[]{:S(2)}) collective-permute-start(bf16[8,64,256]{2,1,0:T(8,128)(2,1)S(1)} %shard_map.84.a), channel_id=1, source_target_pairs={{0,4},{2,6},{4,0},{6,2},{8,12},{10,14},{12,8},{14,10},{1,5},{3,7},... | collective-permute-start | bytes 786440 | tf_op jit(solution)/shard_map/ppermute | solution.py:340
  55.6 9.2 %collective-permute-start.6 = (bf16[8,64,256]{2,1,0:T(8,128)(2,1)S(1)}, bf16[8,64,256]{2,1,0:T(8,128)(2,1)S(1)}, u32[]{:S(2)}, u32[]{:S(2)}) collective-permute-start(bf16[8,64,256]{2,1,0:T(8,128)(2,1)S(1)} %shard_map.81), channel_id=1, source_target_pairs={{4,8},{6,10},{8,4},{10,6},{5,9},{7,11},{9,5},{11,7},{20,24},{22,26... | collective-permute-start | bytes 786440 | tf_op jit(solution)/shard_map/ppermute | solution.py:341
  56.4 14.5 %collective-permute-start.12 = (bf16[8,64,256]{2,1,0:T(8,128)(2,1)S(1)}, bf16[8,64,256]{2,1,0:T(8,128)(2,1)S(1)}, u32[]{:S(2)}, u32[]{:S(2)}) collective-permute-start(bf16[8,64,256]{2,1,0:T(8,128)(2,1)S(1)} %shard_map.86), channel_id=1, source_target_pairs={{4,8},{6,10},{8,4},{10,6},{5,9},{7,11},{9,5},{11,7},{20,24},{22,26... | collective-permute-start | bytes 786440 | tf_op jit(solution)/shard_map/ppermute | solution.py:341
  57.1 15.8 %collective-permute-start.2 = (bf16[6,128,256]{2,1,0:T(8,128)(2,1)S(1)}, bf16[6,128,256]{2,1,0:T(8,128)(2,1)S(1)}, u32[]{:S(2)}, u32[]{:S(2)}) collective-permute-start(bf16[6,128,256]{2,1,0:T(8,128)(2,1)S(1)} %get-tuple-element.23), channel_id=1, source_target_pairs={{0,2},{2,0},{4,6},{6,4},{8,10},{10,8},{12,14},{14,12},{1,3},{3,1},... | collective-permute-start | bytes 1179656 | tf_op jit(solution)/shard_map/ppermute | solution.py:324
  59.0 19.4 %copy-start.4 = (s32[8]{0:T(128)S(1)}, s32[8]{0:T(128)}, u32[]{:S(2)}) copy-start(s32[8]{0:T(128)} %rows.3) | copy-start | bytes 100
  61.3 11.6 %collective-permute-start.15 = (bf16[8,64,256]{2,1,0:T(8,128)(2,1)S(1)}, bf16[8,64,256]{2,1,0:T(8,128)(2,1)S(1)}, u32[]{:S(2)}, u32[]{:S(2)}) collective-permute-start(bf16[8,64,256]{2,1,0:T(8,128)(2,1)S(1)} %shard_map.88), channel_id=1, source_target_pairs={{4,8},{6,10},{8,4},{10,6},{5,9},{7,11},{9,5},{11,7},{20,24},{22,26... | collective-permute-start | bytes 786440 | tf_op jit(solution)/shard_map/ppermute | solution.py:341
  64.1 8.8 %collective-permute-start.17 = (bf16[8,64,256]{2,1,0:T(8,128)(2,1)S(1)}, bf16[8,64,256]{2,1,0:T(8,128)(2,1)S(1)}, u32[]{:S(2)}, u32[]{:S(2)}) collective-permute-start(bf16[8,64,256]{2,1,0:T(8,128)(2,1)S(1)} %shard_map.89), channel_id=1, source_target_pairs={{4,8},{6,10},{8,4},{10,6},{5,9},{7,11},{9,5},{11,7},{20,24},{22,26... | collective-permute-start | bytes 786440 | tf_op jit(solution)/shard_map/ppermute | solution.py:341
  64.9 10.7 %collective-permute-start.7 = (bf16[8,64,256]{2,1,0:T(8,128)(2,1)S(1)}, bf16[8,64,256]{2,1,0:T(8,128)(2,1)S(1)}, u32[]{:S(2)}, u32[]{:S(2)}) collective-permute-start(bf16[8,64,256]{2,1,0:T(8,128)(2,1)S(1)} %shard_map.82), channel_id=1, source_target_pairs={{0,4},{2,6},{4,0},{6,2},{8,12},{10,14},{12,8},{14,10},{1,5},{3,7},... | collective-permute-start | bytes 786440 | tf_op jit(solution)/shard_map/ppermute | solution.py:340
  71.0 7.4 %collective-permute-start.13 = (bf16[8,64,256]{2,1,0:T(8,128)(2,1)S(1)}, bf16[8,64,256]{2,1,0:T(8,128)(2,1)S(1)}, u32[]{:S(2)}, u32[]{:S(2)}) collective-permute-start(bf16[8,64,256]{2,1,0:T(8,128)(2,1)S(1)} %shard_map.87), channel_id=1, source_target_pairs={{0,4},{2,6},{4,0},{6,2},{8,12},{10,14},{12,8},{14,10},{1,5},{3,7},... | collective-permute-start | bytes 786440 | tf_op jit(solution)/shard_map/ppermute | solution.py:340

commit v3 on v2

--- a/solution.py
+++ b/solution.py
@@ -9,6 +9,7 @@
 
 SMEM = pl.BlockSpec(memory_space=pltpu.SMEM)
 VMEM = pl.BlockSpec(memory_space=pltpu.VMEM)
+HBM = pl.BlockSpec(memory_space=pltpu.HBM)
 Y = 2
 OWN, SEND, CROSS = range(3)
 
@@ -24,48 +25,77 @@
     return jnp.where(x >= by, x - by, x)
 
 
-def shifts_kernel(tc, act, rows, psi, left, right, send, keep, inner, acc):
-    s = pl.program_id(0)
-    n_w, blk = right.shape[0], right.shape[2]
+def shifts_kernel(slots, masked, left, right, send, keep, lbuf, rbuf, inner, acc, sems):
+    n_w, n_s, blk = right.shape[:3]
     classes, _, half = send.shape[:3]
+    depth = lbuf.shape[0]
     me = lax.axis_index("mpo")
-    line = lax.broadcasted_iota(jnp.int32, (blk, blk), 0)
-    masked = jnp.where(line < rows[s], psi[0].astype(jnp.float32), 0.0).astype(jnp.bfloat16)
-    for c in range(classes):
-        acc[c] = jnp.zeros(acc.shape[1:], jnp.float32)
-    lhs = left[...].reshape(n_w * blk, blk)
-    inner[...] = jnp.dot(lhs, masked, preferred_element_type=jnp.float32).astype(jnp.bfloat16)
-    for w in range(n_w):
-        c = jnp.where(act[w, s] == 1, tc[w], classes)
-        acc[c] += jnp.dot(inner[w * blk:(w + 1) * blk], right[w, 0], preferred_element_type=jnp.float32)
+
+    def copies(s):
+        at = lax.rem(s, depth)
+        return (
+            pltpu.make_async_copy(left.at[:, s], lbuf.at[at], sems.at[0, at]),
+            pltpu.make_async_copy(right.at[:, s], rbuf.at[at], sems.at[1, at]),
+        )
+
+    for s in range(min(depth, n_s)):
+        for c in copies(jnp.int32(s)):
+            c.start()
     mine = pl.multiple_of(me * half, half)
     other = pl.multiple_of((1 - me) * half, half)
-    for c in range(classes):
-        keep[c, 0] = acc[c, pl.ds(mine, half), :].astype(jnp.bfloat16)
-        send[c, 0] = acc[c, pl.ds(other, half), :].astype(jnp.bfloat16)
+
+    def sector(s, _):
+        at = lax.rem(s, depth)
+        here = copies(s)
+        here[0].wait()
+        for c in range(classes):
+            acc[c] = jnp.zeros(acc.shape[1:], jnp.float32)
+        lhs = lbuf[at].reshape(n_w * blk, blk)
+        inner[...] = jnp.dot(lhs, masked[s], preferred_element_type=jnp.float32).astype(jnp.bfloat16)
+        here[1].wait()
+        for w in range(n_w):
+            acc[slots[s, w]] += jnp.dot(
+                inner[w * blk:(w + 1) * blk], rbuf[at, w], preferred_element_type=jnp.float32
+            )
+
+        @pl.when(s + depth < n_s)
+        def _():
+            for c in copies(s + depth):
+                c.start()
+
+        for c in range(classes):
+            keep[c, s] = acc[c, pl.ds(mine, half), :].astype(jnp.bfloat16)
+            send[c, s] = acc[c, pl.ds(other, half), :].astype(jnp.bfloat16)
+        return 0
+
+    lax.fori_loop(0, n_s, sector, 0)
 
 
 def shift_sums(psi, left_env, right_env, term_class, active, sector_rows, classes):
     n_w, n_s, blk = left_env.shape[:3]
     half = blk // 2
+    depth = 3
+    line = jnp.arange(blk, dtype=jnp.int32)
+    masked = jnp.where(line[None, :, None] < sector_rows[:, None, None], psi, jnp.zeros_like(psi))
+    slots = jnp.where(active.T == 1, term_class[None, :], classes)
     out = jax.ShapeDtypeStruct((classes, n_s, half, blk), jnp.bfloat16)
-    block = pl.BlockSpec((classes, 1, half, blk), lambda s: (0, s, 0, 0))
-    env = pl.BlockSpec((n_w, 1, blk, blk), lambda s: (0, s, 0, 0))
     return pl.pallas_call(
         shifts_kernel,
-        grid=(n_s,),
         out_shape=(out, out),
-        in_specs=[SMEM, SMEM, SMEM, pl.BlockSpec((1, blk, blk), lambda s: (s, 0, 0)), env, env],
-        out_specs=(block, block),
+        in_specs=[SMEM, VMEM, HBM, HBM],
+        out_specs=(VMEM, VMEM),
         scratch_shapes=[
+            pltpu.VMEM((depth, n_w, blk, blk), jnp.bfloat16),
+            pltpu.VMEM((depth, n_w, blk, blk), jnp.bfloat16),
             pltpu.VMEM((n_w * blk, blk), jnp.bfloat16),
             pltpu.VMEM((classes + 1, blk, blk), jnp.float32),
+            pltpu.SemaphoreType.DMA((2, depth)),
         ],
-        compiler_params=pltpu.CompilerParams(vmem_limit_bytes=40 * 2**20, dimension_semantics=("arbitrary",)),
+        compiler_params=pltpu.CompilerParams(vmem_limit_bytes=40 * 2**20),
         cost_estimate=pl.CostEstimate(
             flops=4 * n_w * n_s * blk**3, bytes_accessed=4 * n_w * n_s * blk * blk, transcendentals=0
         ),
-    )(term_class, active, sector_rows, psi, left_env, right_env)
+    )(slots, masked, left_env, right_env)
 
 
 def table_at(cap, q, kind):
@@ -79,11 +109,11 @@
     z, y = split(d, Y)
     even = (z & 1) == 0
 
-    def clear(i, _):
+    for i in range(3 * line):
         table[i * (1 + 2 * cap)] = 0
-        return 0
-
-    lax.fori_loop(0, 3 * line, clear, 0)
+        for slot in range(cap):
+            table[i * (1 + 2 * cap) + 1 + slot] = 0
+            table[i * (1 + 2 * cap) + 1 + cap + slot] = n_s
 
     def position(twice):
         m = wrap(lax.shift_right_arithmetic(twice, 1), line)
@@ -127,20 +157,13 @@
     )(dest)
 
 
-def joined(keep, recv, j):
-    return keep[j].astype(jnp.float32) + recv[j].astype(jnp.float32)
-
-
 def pack_into(out, cap, q, start, table, keep, recv):
     at = table_at(cap, q, SEND)
     rows = pl.ds(start, out.shape[1])
 
-    def step(slot, _):
+    for slot in range(cap):
         j = table[at + 1 + slot]
-        out[slot] = (keep[j, rows].astype(jnp.float32) + recv[j, rows].astype(jnp.float32)).astype(jnp.bfloat16)
-        return 0
-
-    lax.fori_loop(0, table[at], step, 0)
+        out[slot] = keep[j, rows] + recv[j, rows]
 
 
 def pack(cap, q, pieces, table, keep, recv):
@@ -188,16 +211,13 @@
             own[q][...] = jnp.zeros(own[q].shape, jnp.float32)
             at = table_at(cap, q, OWN)
 
-            def step(slot, _, q=q, at=at):
-                block = joined(keep, recv, table[at + 1 + slot]).astype(jnp.bfloat16)
-                own[q][table[at + 1 + cap + slot]] += block.astype(jnp.float32)
-                return 0
-
-            lax.fori_loop(0, table[at], step, 0)
-
-    return pl.pallas_call(
-        kernel,
-        out_shape=[jax.ShapeDtypeStruct((n_s, half, blk), jnp.float32)] * line,
+            for slot in range(cap):
+                j = table[at + 1 + slot]
+                own[q][table[at + 1 + cap + slot]] += (keep[j] + recv[j]).astype(jnp.float32)
+
+    return pl.pallas_call(
+        kernel,
+        out_shape=[jax.ShapeDtypeStruct((n_s + 1, half, blk), jnp.float32)] * line,
         in_specs=[SMEM, VMEM, VMEM] + [pl.BlockSpec(memory_space=pl.ANY)] * len(firsts),
         out_specs=[VMEM] * line,
         compiler_params=pltpu.CompilerParams(vmem_limit_bytes=24 * 2**20),
@@ -206,48 +226,40 @@
 
 
 def gather(cap, q, piece, table, own, crossed):
-    n_s, _, blk = own.shape
+    n_s, blk = own.shape[0] - 1, own.shape[2]
     start, size = piece
     at = table_at(cap, q, CROSS)
 
     def kernel(table, own, crossed, out, total):
-        total[...] = own[:, start:start + size]
-
-        def step(slot, _):
+        total[:n_s] = own[:n_s, start:start + size]
+        for slot in range(cap):
             total[table[at + 1 + cap + slot]] += crossed[slot].astype(jnp.float32)
-            return 0
-
-        lax.fori_loop(0, table[at], step, 0)
-        out[...] = total[...].astype(jnp.bfloat16)
+        out[...] = total[:n_s].astype(jnp.bfloat16)
 
     return pl.pallas_call(
         kernel,
         out_shape=jax.ShapeDtypeStruct((n_s, size, blk), jnp.bfloat16),
         in_specs=[SMEM, VMEM, VMEM],
         out_specs=VMEM,
-        scratch_shapes=[pltpu.VMEM((n_s, size, blk), jnp.float32)],
+        scratch_shapes=[pltpu.VMEM((n_s + 1, size, blk), jnp.float32)],
         compiler_params=pltpu.CompilerParams(vmem_limit_bytes=16 * 2**20),
         cost_estimate=pl.CostEstimate(flops=0, bytes_accessed=1000, transcendentals=0),
     )(table, own, crossed)
 
 
 def finish(cap, q, table, rows, own, crossed, arrived):
-    n_s, half, blk = own.shape
+    n_s, half, blk = own.shape[0] - 1, own.shape[1], own.shape[2]
     at = table_at(cap, q, CROSS)
     spots = [start for start, _ in arrived]
 
     def kernel(table, rows, own, crossed, *rest):
         parts, (out, total) = rest[:-2], rest[-2:]
-        total[...] = own[...]
-
-        def step(slot, _):
+        total[:n_s] = own[:n_s]
+        for slot in range(cap):
             total[table[at + 1 + cap + slot]] += crossed[slot].astype(jnp.float32)
-            return 0
-
-        lax.fori_loop(0, table[at], step, 0)
+        line = lax.broadcasted_iota(jnp.int32, (half, blk), 0) + lax.axis_index("mpo") * half
         for start, part in zip(spots, parts):
-            total[:, start:start + part.shape[1]] += part[...].astype(jnp.float32)
-        line = lax.broadcasted_iota(jnp.int32, (half, blk), 0) + lax.axis_index("mpo") * half
+            total[:n_s, start:start + part.shape[1]] += part[...].astype(jnp.float32)
         for p in range(n_s):
             out[p] = jnp.where(line < rows[p], total[p], 0.0).astype(jnp.bfloat16)
 
@@ -256,7 +268,7 @@
         out_shape=jax.ShapeDtypeStruct((n_s, half, blk), jnp.bfloat16),
         in_specs=[SMEM, SMEM, VMEM, VMEM] + [VMEM] * len(arrived),
         out_specs=VMEM,
-        scratch_shapes=[pltpu.VMEM((n_s, half, blk), jnp.float32)],
+        scratch_shapes=[pltpu.VMEM((n_s + 1, half, blk), jnp.float32)],
         compiler_params=pltpu.CompilerParams(vmem_limit_bytes=16 * 2**20),
         cost_estimate=pl.CostEstimate(flops=0, bytes_accessed=1000, transcendentals=0),
     )(table, rows, own, crossed, *[part for _, part in arrived])
@@ -320,7 +332,7 @@
     firsts = pack(cap, 0, pieces[0], table, keep, recv)
     crossed = [[lax.ppermute(x, "sector", across) for x in firsts]]
     own = add_own(cap, line, n_s, table, keep, recv, firsts)
-    packed = pack_rest(cap, line, pieces, table, keep, recv, crossed[0][0])
+    packed = pack_rest(cap, line, pieces, table, keep, recv, firsts[0])
     crossed += [[lax.ppermute(x, "sector", across) for x in xs] for xs in packed]
 
     acc = []

time: 80.7 us -> 83.8 us (1.038)
  Pallas kernels: 31.7 us -> 35.9 us
  waiting for transfers between devices: 20 us -> 16.7 us
  local copies, waits for them, and re-layouts: 3.99 us -> 0.69 us
  other arithmetic: 0 us -> 2.91 us
  starting transfers between devices: 24.4 us -> 26.9 us
    pallas_call x2, Pallas kernels: 18.6 us -> 23.2 us  [the longest x1 20.8 us: shift_sums(): pl.pallas_call(shifts_kernel, out_shape=(out, out), in_specs=[SMEM, VMEM,...]
    unnamed x13 -> x6, local copies, waits for them, and re-layouts: 3.99 us -> 0.69 us
    select_n x0 -> x2, other arithmetic: none -> 2.18 us  [the longest x1 1.49 us: shift_sums(): jnp.where(line[None, :, None] < sector_rows[:, None, None], psi, jnp.zero...]
    ppermute x6, waiting for transfers between devices: 10.5 us -> 8.61 us  [body(): lax.ppermute(x, 'sector', near)]
    ppermute x2, waiting for transfers between devices: 2.87 us -> 1.18 us  [body(): crossed = [[lax.ppermute(x, 'sector', across) for x in firsts]]]
    ppermute x5, starting transfers between devices: 6 us -> 7.34 us  [body(): lax.ppermute(x, 'sector', across)]
    ppermute x6, starting transfers between devices: 12.2 us -> 13.3 us  [body(): lax.ppermute(x, 'sector', near)]
  transfers between devices with their start and end apart: 18 -> 18, of which waited for: 8 -> 7; matrix products, arithmetic and copies ran while one was open for 0% -> 0% of each run, Pallas kernels for 15% -> 14%
where the time goes in v3:
time: 83.8 us; the launch traced here: 83.4 us
  Pallas kernels  35.9 us (43%)
  starting transfers between devices  26.9 us (32%)
  waiting for transfers between devices  16.7 us (20%)
  other arithmetic  2.91 us (3%)
    pallas_call x1, Pallas kernels, shift_sums(): pl.pallas_call(shifts_kernel, out_shape=(out, out), in_specs=[SMEM, VMEM,...  20.8 us
    ppermute x6, starting transfers between devices, body(): lax.ppermute(x, 'sector', near)  13.3 us
    ppermute x6, waiting for transfers between devices, body(): lax.ppermute(x, 'sector', near)  8.61 us
    ppermute x5, starting transfers between devices, body(): lax.ppermute(x, 'sector', across)  7.34 us
    ppermute x5, waiting for transfers between devices, body(): lax.ppermute(x, 'sector', across)  4.96 us
    pallas_call x6, Pallas kernels, gather(): pl.pallas_call(kernel, out_shape=jax.ShapeDtypeStruct((n_s, size, blk), j...  3.96 us
    ppermute x2, starting transfers between devices, body(): crossed = [[lax.ppermute(x, 'sector', across) for x in firsts]]  3.04 us
    pallas_call x1, Pallas kernels, make_table(): pl.pallas_call(functools.partial(table_kernel, n, cap), out_shape=jax.Sha...  2.92 us
  transfers between devices with their start and end apart: 18, of which 7 were waited for; matrix products, arithmetic and copies ran while one was open for 0% of the time, Pallas kernels for 14%

profile of v3, /device:TPU:0, one launch (start us, length us, event | category | flops | bytes accessed | tf_op | source)
XLA Modules:
  0.0 83.4 jit_solution(15553558732764462170)
XLA Ops:
  0.0 0.7 iota_compare_fusion
  0.7 0.7 select_bitcast_fusion.slots
  1.4 1.5 %broadcast_select_fusion.masked = bf16[8,256,256]{2,1,0:T(8,128)(2,1)S(1)} fusion(bf16[8,256,256]{2,1,0:T(8,128)(2,1)} %param.7, pred[8,256]{1,0:T(8,128)(4,1)S(1)} %iota_compare_fusion), kind=kLoop, calls=%fused_computation | loop fusion | flops 524288 | bytes 2099200 | tf_op jit(solution)/shard_map/jit(_where)/select_n | solution.py:79
  2.9 20.8 %shard_map.74 = (bf16[5,8,128,256]{3,2,1,0:T(8,128)(2,1)}, bf16[5,8,128,256]{3,2,1,0:T(8,128)(2,1)S(1)}) custom-call(s32[8,13]{1,0:T(8,128)S(1)} %select_bitcast_fusion.slots, bf16[8,256,256]{2,1,0:T(8,128)(2,1)S(1)} %broadcast_select_fusion.masked, bf16[13,8,256,256]{3,2,1,0:T(8,128)(2,1)} %left.1, bf16[13,8,256,256]{3,2,1,0:T(8,128)(2,1)} %right.1), custom_call_target="tpu_custom_call" | custom-call | flops 6979321856 | bytes 27262976 | tf_op jit(solution)/shard_map/pallas_call | solution.py:82
  23.7 0.5 collective-permute-start
  24.2 2.9 %shard_map.73.table = s32[156]{0:T(256)} custom-call(s32[5,8]{1,0:T(8,128)} %dest.1), custom_call_target="tpu_custom_call" | custom-call | flops 4000 | bytes 4000 | tf_op jit(solution)/shard_map/pallas_call | solution.py:151
  27.2 1.9 %collective-permute-done.recv = bf16[40,128,256]{2,1,0:T(8,128)(2,1)} collective-permute-done((bf16[40,128,256]{2,1,0:T(8,128)(2,1)}, bf16[40,128,256]{2,1,0:T(8,128)(2,1)}, u32[]{:S(2)}, u32[]{:S(2)}) %collective-permute-start) | collective-permute-done | bytes 2621472 | tf_op jit(solution)/shard_map/ppermute | solution.py:329
  29.1 0.0 copy-start
  29.1 0.7 copy-done
  29.8 1.8 %shard_map.75 = (bf16[6,64,256]{2,1,0:T(8,128)(2,1)S(1)}, bf16[6,64,256]{2,1,0:T(8,128)(2,1)S(1)}) custom-call(s32[156]{0:T(256)S(1)} %copy-done, bf16[40,128,256]{2,1,0:T(8,128)(2,1)S(1)} %bitcast.4, bf16[40,128,256]{2,1,0:T(8,128)(2,1)} %collective-permute-done.recv), custom_call_target="tpu_custom_call" | custom-call | bytes 1000 | tf_op jit(solution)/shard_map/pallas_call | solution.py:176
  31.6 3.0 %collective-permute-start.4 = (bf16[6,64,256]{2,1,0:T(8,128)(2,1)S(1)}, bf16[6,64,256]{2,1,0:T(8,128)(2,1)S(1)}, u32[]{:S(2)}, u32[]{:S(2)}) collective-permute-start(bf16[6,64,256]{2,1,0:T(8,128)(2,1)S(1)} %get-tuple-element.20.refs_0_.after), channel_id=1, source_target_pairs={{0,2},{2,0},{4,6},{6,4},{8,10},{10,8},{12,14},{14,12},{1,3},{3,1},... | collective-permute-start | bytes 589832 | tf_op jit(solution)/shard_map/ppermute | solution.py:333
  34.5 0.0 copy-start.1
  34.5 0.1 collective-permute-start.10
  34.6 1.9 %shard_map.77 = (bf16[6,64,256]{2,1,0:T(8,128)(2,1)S(1)}, bf16[6,64,256]{2,1,0:T(8,128)(2,1)S(1)}, bf16[6,64,256]{2,1,0:T(8,128)(2,1)S(1)}, bf16[6,64,256]{2,1,0:T(8,128)(2,1)S(1)}, bf16[6,128,256]{2,1,0:T(8,128)(2,1)S(1)}) custom-call(s32[156]{0:T(256)S(1)} %copy-done, bf16[40,128,256]{2,1,0:T(8,128)(2,1)S(1)} %bitcast.5, ...), custom_call_target="tpu_custom_call" | custom-call | bytes 1000 | tf_op jit(solution)/shard_map/pallas_call | solution.py:194
  36.5 2.0 %collective-permute-start.3 = (bf16[6,64,256]{2,1,0:T(8,128)(2,1)S(1)}, bf16[6,64,256]{2,1,0:T(8,128)(2,1)S(1)}, u32[]{:S(2)}, u32[]{:S(2)}) collective-permute-start(bf16[6,64,256]{2,1,0:T(8,128)(2,1)S(1)} %get-tuple-element.27), channel_id=1, source_target_pairs={{0,2},{2,0},{4,6},{6,4},{8,10},{10,8},{12,14},{14,12},{1,3},{3,1},... | collective-permute-start | bytes 589832 | tf_op jit(solution)/shard_map/ppermute | solution.py:336
  38.5 0.0 copy-done.1
  38.5 2.4 %shard_map.76 = (f32[9,128,256]{2,1,0:T(8,128)S(1)}, f32[9,128,256]{2,1,0:T(8,128)S(1)}, f32[9,128,256]{2,1,0:T(8,128)S(1)}, f32[9,128,256]{2,1,0:T(8,128)S(1)}) custom-call(s32[156]{0:T(256)S(1)} %copy-done.1, bf16[40,128,256]{2,1,0:T(8,128)(2,1)S(1)} %bitcast.6, bf16[40,128,256]{2,1,0:T(8,128)(2,1)} %collective-permute-done.recv, ...), custom_call_target="tpu_custom_call" | custom-call | bytes 1000 | tf_op jit(solution)/shard_map/pallas_call | solution.py:218
  40.9 0.0 collective-permute-done.4.crossed
  40.9 0.7 shard_map.80.a
  41.6 1.7 %collective-permute-start.5 = (bf16[8,64,256]{2,1,0:T(8,128)(2,1)S(1)}, bf16[8,64,256]{2,1,0:T(8,128)(2,1)S(1)}, u32[]{:S(2)}, u32[]{:S(2)}) collective-permute-start(bf16[8,64,256]{2,1,0:T(8,128)(2,1)S(1)} %shard_map.80.a), channel_id=1, source_target_pairs={{0,4},{2,6},{4,0},{6,2},{8,12},{10,14},{12,8},{14,10},{1,5},{3,7},... | collective-permute-start | bytes 786440 | tf_op jit(solution)/shard_map/ppermute | solution.py:352
  43.3 1.2 %collective-permute-done.10.crossed = bf16[6,64,256]{2,1,0:T(8,128)(2,1)S(1)} collective-permute-done((bf16[6,64,256]{2,1,0:T(8,128)(2,1)S(1)}, bf16[6,64,256]{2,1,0:T(8,128)(2,1)S(1)}, u32[]{:S(2)}, u32[]{:S(2)}) %collective-permute-start.10) | collective-permute-done | bytes 196640 | tf_op jit(solution)/shard_map/ppermute | solution.py:333
  44.4 0.7 shard_map.85.a
  45.1 2.2 %collective-permute-start.11 = (bf16[8,64,256]{2,1,0:T(8,128)(2,1)S(1)}, bf16[8,64,256]{2,1,0:T(8,128)(2,1)S(1)}, u32[]{:S(2)}, u32[]{:S(2)}) collective-permute-start(bf16[8,64,256]{2,1,0:T(8,128)(2,1)S(1)} %shard_map.85.a), channel_id=1, source_target_pairs={{0,4},{2,6},{4,0},{6,2},{8,12},{10,14},{12,8},{14,10},{1,5},{3,7},... | collective-permute-start | bytes 786440 | tf_op jit(solution)/shard_map/ppermute | solution.py:352
  47.3 1.6 %collective-permute-start.9 = (bf16[6,64,256]{2,1,0:T(8,128)(2,1)S(1)}, bf16[6,64,256]{2,1,0:T(8,128)(2,1)S(1)}, u32[]{:S(2)}, u32[]{:S(2)}) collective-permute-start(bf16[6,64,256]{2,1,0:T(8,128)(2,1)S(1)} %get-tuple-element.30), channel_id=1, source_target_pairs={{0,2},{2,0},{4,6},{6,4},{8,10},{10,8},{12,14},{14,12},{1,3},{3,1},... | collective-permute-start | bytes 589832 | tf_op jit(solution)/shard_map/ppermute | solution.py:336
  48.9 0.5 collective-permute-start.2
  49.3 0.0 collective-permute-done.3.crossed
  49.3 1.6 %collective-permute-start.8 = (bf16[6,64,256]{2,1,0:T(8,128)(2,1)S(1)}, bf16[6,64,256]{2,1,0:T(8,128)(2,1)S(1)}, u32[]{:S(2)}, u32[]{:S(2)}) collective-permute-start(bf16[6,64,256]{2,1,0:T(8,128)(2,1)S(1)} %get-tuple-element.29), channel_id=1, source_target_pairs={{0,2},{2,0},{4,6},{6,4},{8,10},{10,8},{12,14},{14,12},{1,3},{3,1},... | collective-permute-start | bytes 589832 | tf_op jit(solution)/shard_map/ppermute | solution.py:336
  50.9 0.7 shard_map.79.a
  51.5 3.6 %collective-permute-done.9.crossed = bf16[6,64,256]{2,1,0:T(8,128)(2,1)S(1)} collective-permute-done((bf16[6,64,256]{2,1,0:T(8,128)(2,1)S(1)}, bf16[6,64,256]{2,1,0:T(8,128)(2,1)S(1)}, u32[]{:S(2)}, u32[]{:S(2)}) %collective-permute-start.9) | collective-permute-done | bytes 196640 | tf_op jit(solution)/shard_map/ppermute | solution.py:336
  55.1 0.1 collective-permute-start.14
  55.2 0.7 shard_map.84.a
  55.9 0.0 collective-permute-done.5.b
  55.9 2.0 %collective-permute-start.16 = (bf16[8,64,256]{2,1,0:T(8,128)(2,1)S(1)}, bf16[8,64,256]{2,1,0:T(8,128)(2,1)S(1)}, u32[]{:S(2)}, u32[]{:S(2)}) collective-permute-start(bf16[8,64,256]{2,1,0:T(8,128)(2,1)S(1)} %shard_map.84.a), channel_id=1, source_target_pairs={{0,4},{2,6},{4,0},{6,2},{8,12},{10,14},{12,8},{14,10},{1,5},{3,7},... | collective-permute-start | bytes 786440 | tf_op jit(solution)/shard_map/ppermute | solution.py:352
  57.9 0.1 shard_map.81
  58.0 0.0 collective-permute-done.11.b
  58.0 0.7 collective-permute-start.6
  58.6 0.1 shard_map.86
  58.7 0.0 collective-permute-done.2.crossed
  58.7 0.7 collective-permute-start.12
  59.4 1.4 %collective-permute-done.8.crossed = bf16[6,64,256]{2,1,0:T(8,128)(2,1)S(1)} collective-permute-done((bf16[6,64,256]{2,1,0:T(8,128)(2,1)S(1)}, bf16[6,64,256]{2,1,0:T(8,128)(2,1)S(1)}, u32[]{:S(2)}, u32[]{:S(2)}) %collective-permute-start.8) | collective-permute-done | bytes 196640 | tf_op jit(solution)/shard_map/ppermute | solution.py:336
  60.8 1.7 %collective-permute-start.1 = (bf16[6,128,256]{2,1,0:T(8,128)(2,1)S(1)}, bf16[6,128,256]{2,1,0:T(8,128)(2,1)S(1)}, u32[]{:S(2)}, u32[]{:S(2)}) collective-permute-start(bf16[6,128,256]{2,1,0:T(8,128)(2,1)S(1)} %get-tuple-element.23), channel_id=1, source_target_pairs={{0,2},{2,0},{4,6},{6,4},{8,10},{10,8},{12,14},{14,12},{1,3},{3,1},... | collective-permute-start | bytes 1179656 | tf_op jit(solution)/shard_map/ppermute | solution.py:336
  62.5 0.7 shard_map.78.a
  63.2 0.0 copy-start.2
  63.2 0.7 shard_map.83.a
  63.9 0.0 collective-permute-done.14.b
  63.9 0.1 shard_map.88
  64.0 0.7 collective-permute-start.15
  64.7 1.4 %collective-permute-done.16.b = bf16[8,64,256]{2,1,0:T(8,128)(2,1)S(1)} collective-permute-done((bf16[8,64,256]{2,1,0:T(8,128)(2,1)S(1)}, bf16[8,64,256]{2,1,0:T(8,128)(2,1)S(1)}, u32[]{:S(2)}, u32[]{:S(2)}) %collective-permute-start.16) | collective-permute-done | bytes 262176 | tf_op jit(solution)/shard_map/ppermute | solution.py:352
  66.0 0.1 shard_map.89
  66.1 0.7 collective-permute-start.17
  66.8 0.0 collective-permute-done.6.b
  66.8 0.1 shard_map.82
  66.9 7.3 %collective-permute-start.7 = (bf16[8,64,256]{2,1,0:T(8,128)(2,1)S(1)}, bf16[8,64,256]{2,1,0:T(8,128)(2,1)S(1)}, u32[]{:S(2)}, u32[]{:S(2)}) collective-permute-start(bf16[8,64,256]{2,1,0:T(8,128)(2,1)S(1)} %shard_map.82), channel_id=1, source_target_pairs={{0,4},{2,6},{4,0},{6,2},{8,12},{10,14},{12,8},{14,10},{1,5},{3,7},... | collective-permute-start | bytes 786440 | tf_op jit(solution)/shard_map/ppermute | solution.py:352
  74.2 0.0 collective-permute-done.12.b
  74.2 0.1 shard_map.87
  74.3 0.1 collective-permute-start.13
  74.4 0.0 collective-permute-done.1.crossed
  74.4 0.0 collective-permute-done.15.rest_2_
  74.4 0.0 collective-permute-done.17.rest_3_
  74.4 4.4 %collective-permute-done.7.rest_0_ = bf16[8,64,256]{2,1,0:T(8,128)(2,1)S(1)} collective-permute-done((bf16[8,64,256]{2,1,0:T(8,128)(2,1)S(1)}, bf16[8,64,256]{2,1,0:T(8,128)(2,1)S(1)}, u32[]{:S(2)}, u32[]{:S(2)}) %collective-permute-start.7) | collective-permute-done | bytes 262176 | tf_op jit(solution)/shard_map/ppermute | solution.py:352
  78.8 2.8 %collective-permute-done.13.rest_1_ = bf16[8,64,256]{2,1,0:T(8,128)(2,1)S(1)} collective-permute-done((bf16[8,64,256]{2,1,0:T(8,128)(2,1)S(1)}, bf16[8,64,256]{2,1,0:T(8,128)(2,1)S(1)}, u32[]{:S(2)}, u32[]{:S(2)}) %collective-permute-start.13) | collective-permute-done | bytes 262176 | tf_op jit(solution)/shard_map/ppermute | solution.py:352
  81.6 0.0 copy-done.2
  81.6 1.8 %shard_map.90 = bf16[8,128,256]{2,1,0:T(8,128)(2,1)} custom-call(s32[156]{0:T(256)S(1)} %copy-done.1, s32[8]{0:T(128)S(1)} %copy-done.2, f32[9,128,256]{2,1,0:T(8,128)S(1)} %get-tuple-element.22.own, bf16[6,128,256]{2,1,0:T(8,128)(2,1)S(1)} %collective-permute-done.1.crossed, bf16[8,64,256]{2,1,0:T(8,128)(2,1)S(1)} %collective-permute-done.7.rest_0_, ...), custom_call_target="tpu_custom_call" | custom-call | bytes 1000 | tf_op jit(solution)/shard_map/pallas_call | solution.py:266
Async XLA Ops:
  23.7 5.4 %collective-permute-start = (bf16[40,128,256]{2,1,0:T(8,128)(2,1)}, bf16[40,128,256]{2,1,0:T(8,128)(2,1)}, u32[]{:S(2)}, u32[]{:S(2)}) collective-permute-start(bf16[40,128,256]{2,1,0:T(8,128)(2,1)} %bitcast.2), channel_id=1, source_target_pairs={{0,1},{1,0},{2,3},{3,2},{4,5},{5,4},{6,7},{7,6},{8,9},{9,8},{10,11... | collective-permute-start | bytes 7864328 | tf_op jit(solution)/shard_map/ppermute | solution.py:329
  29.1 0.7 copy-start
  31.6 9.3 %collective-permute-start.4 = (bf16[6,64,256]{2,1,0:T(8,128)(2,1)S(1)}, bf16[6,64,256]{2,1,0:T(8,128)(2,1)S(1)}, u32[]{:S(2)}, u32[]{:S(2)}) collective-permute-start(bf16[6,64,256]{2,1,0:T(8,128)(2,1)S(1)} %get-tuple-element.20.refs_0_.after), channel_id=1, source_target_pairs={{0,2},{2,0},{4,6},{6,4},{8,10},{10,8},{12,14},{14,12},{1,3},{3,1},... | collective-permute-start | bytes 589832 | tf_op jit(solution)/shard_map/ppermute | solution.py:333
  34.5 4.0 %copy-start.1 = (s32[156]{0:T(256)S(1)}, s32[156]{0:T(256)}, u32[]{:S(2)}) copy-start(s32[156]{0:T(256)} %shard_map.73.table) | copy-start | bytes 1876
  34.5 9.9 %collective-permute-start.10 = (bf16[6,64,256]{2,1,0:T(8,128)(2,1)S(1)}, bf16[6,64,256]{2,1,0:T(8,128)(2,1)S(1)}, u32[]{:S(2)}, u32[]{:S(2)}) collective-permute-start(bf16[6,64,256]{2,1,0:T(8,128)(2,1)S(1)} %get-tuple-element.21.refs_1_), channel_id=1, source_target_pairs={{0,2},{2,0},{4,6},{6,4},{8,10},{10,8},{12,14},{14,12},{1,3},{3,1},... | collective-permute-start | bytes 589832 | tf_op jit(solution)/shard_map/ppermute | solution.py:333
  36.5 12.8 %collective-permute-start.3 = (bf16[6,64,256]{2,1,0:T(8,128)(2,1)S(1)}, bf16[6,64,256]{2,1,0:T(8,128)(2,1)S(1)}, u32[]{:S(2)}, u32[]{:S(2)}) collective-permute-start(bf16[6,64,256]{2,1,0:T(8,128)(2,1)S(1)} %get-tuple-element.27), channel_id=1, source_target_pairs={{0,2},{2,0},{4,6},{6,4},{8,10},{10,8},{12,14},{14,12},{1,3},{3,1},... | collective-permute-start | bytes 589832 | tf_op jit(solution)/shard_map/ppermute | solution.py:336
  41.6 14.3 %collective-permute-start.5 = (bf16[8,64,256]{2,1,0:T(8,128)(2,1)S(1)}, bf16[8,64,256]{2,1,0:T(8,128)(2,1)S(1)}, u32[]{:S(2)}, u32[]{:S(2)}) collective-permute-start(bf16[8,64,256]{2,1,0:T(8,128)(2,1)S(1)} %shard_map.80.a), channel_id=1, source_target_pairs={{0,4},{2,6},{4,0},{6,2},{8,12},{10,14},{12,8},{14,10},{1,5},{3,7},... | collective-permute-start | bytes 786440 | tf_op jit(solution)/shard_map/ppermute | solution.py:352
  45.1 12.9 %collective-permute-start.11 = (bf16[8,64,256]{2,1,0:T(8,128)(2,1)S(1)}, bf16[8,64,256]{2,1,0:T(8,128)(2,1)S(1)}, u32[]{:S(2)}, u32[]{:S(2)}) collective-permute-start(bf16[8,64,256]{2,1,0:T(8,128)(2,1)S(1)} %shard_map.85.a), channel_id=1, source_target_pairs={{0,4},{2,6},{4,0},{6,2},{8,12},{10,14},{12,8},{14,10},{1,5},{3,7},... | collective-permute-start | bytes 786440 | tf_op jit(solution)/shard_map/ppermute | solution.py:352
  47.3 7.8 %collective-permute-start.9 = (bf16[6,64,256]{2,1,0:T(8,128)(2,1)S(1)}, bf16[6,64,256]{2,1,0:T(8,128)(2,1)S(1)}, u32[]{:S(2)}, u32[]{:S(2)}) collective-permute-start(bf16[6,64,256]{2,1,0:T(8,128)(2,1)S(1)} %get-tuple-element.30), channel_id=1, source_target_pairs={{0,2},{2,0},{4,6},{6,4},{8,10},{10,8},{12,14},{14,12},{1,3},{3,1},... | collective-permute-start | bytes 589832 | tf_op jit(solution)/shard_map/ppermute | solution.py:336
  48.9 9.9 %collective-permute-start.2 = (bf16[6,64,256]{2,1,0:T(8,128)(2,1)S(1)}, bf16[6,64,256]{2,1,0:T(8,128)(2,1)S(1)}, u32[]{:S(2)}, u32[]{:S(2)}) collective-permute-start(bf16[6,64,256]{2,1,0:T(8,128)(2,1)S(1)} %get-tuple-element.25), channel_id=1, source_target_pairs={{0,2},{2,0},{4,6},{6,4},{8,10},{10,8},{12,14},{14,12},{1,3},{3,1},... | collective-permute-start | bytes 589832 | tf_op jit(solution)/shard_map/ppermute | solution.py:336
  49.3 11.5 %collective-permute-start.8 = (bf16[6,64,256]{2,1,0:T(8,128)(2,1)S(1)}, bf16[6,64,256]{2,1,0:T(8,128)(2,1)S(1)}, u32[]{:S(2)}, u32[]{:S(2)}) collective-permute-start(bf16[6,64,256]{2,1,0:T(8,128)(2,1)S(1)} %get-tuple-element.29), channel_id=1, source_target_pairs={{0,2},{2,0},{4,6},{6,4},{8,10},{10,8},{12,14},{14,12},{1,3},{3,1},... | collective-permute-start | bytes 589832 | tf_op jit(solution)/shard_map/ppermute | solution.py:336
  55.1 8.8 %collective-permute-start.14 = (bf16[8,64,256]{2,1,0:T(8,128)(2,1)S(1)}, bf16[8,64,256]{2,1,0:T(8,128)(2,1)S(1)}, u32[]{:S(2)}, u32[]{:S(2)}) collective-permute-start(bf16[8,64,256]{2,1,0:T(8,128)(2,1)S(1)} %shard_map.79.a), channel_id=1, source_target_pairs={{0,4},{2,6},{4,0},{6,2},{8,12},{10,14},{12,8},{14,10},{1,5},{3,7},... | collective-permute-start | bytes 786440 | tf_op jit(solution)/shard_map/ppermute | solution.py:352
  55.9 10.2 %collective-permute-start.16 = (bf16[8,64,256]{2,1,0:T(8,128)(2,1)S(1)}, bf16[8,64,256]{2,1,0:T(8,128)(2,1)S(1)}, u32[]{:S(2)}, u32[]{:S(2)}) collective-permute-start(bf16[8,64,256]{2,1,0:T(8,128)(2,1)S(1)} %shard_map.84.a), channel_id=1, source_target_pairs={{0,4},{2,6},{4,0},{6,2},{8,12},{10,14},{12,8},{14,10},{1,5},{3,7},... | collective-permute-start | bytes 786440 | tf_op jit(solution)/shard_map/ppermute | solution.py:352
  58.0 8.8 %collective-permute-start.6 = (bf16[8,64,256]{2,1,0:T(8,128)(2,1)S(1)}, bf16[8,64,256]{2,1,0:T(8,128)(2,1)S(1)}, u32[]{:S(2)}, u32[]{:S(2)}) collective-permute-start(bf16[8,64,256]{2,1,0:T(8,128)(2,1)S(1)} %shard_map.81), channel_id=1, source_target_pairs={{4,8},{6,10},{8,4},{10,6},{5,9},{7,11},{9,5},{11,7},{20,24},{22,26... | collective-permute-start | bytes 786440 | tf_op jit(solution)/shard_map/ppermute | solution.py:353
  58.7 15.5 %collective-permute-start.12 = (bf16[8,64,256]{2,1,0:T(8,128)(2,1)S(1)}, bf16[8,64,256]{2,1,0:T(8,128)(2,1)S(1)}, u32[]{:S(2)}, u32[]{:S(2)}) collective-permute-start(bf16[8,64,256]{2,1,0:T(8,128)(2,1)S(1)} %shard_map.86), channel_id=1, source_target_pairs={{4,8},{6,10},{8,4},{10,6},{5,9},{7,11},{9,5},{11,7},{20,24},{22,26... | collective-permute-start | bytes 786440 | tf_op jit(solution)/shard_map/ppermute | solution.py:353
  60.8 13.6 %collective-permute-start.1 = (bf16[6,128,256]{2,1,0:T(8,128)(2,1)S(1)}, bf16[6,128,256]{2,1,0:T(8,128)(2,1)S(1)}, u32[]{:S(2)}, u32[]{:S(2)}) collective-permute-start(bf16[6,128,256]{2,1,0:T(8,128)(2,1)S(1)} %get-tuple-element.23), channel_id=1, source_target_pairs={{0,2},{2,0},{4,6},{6,4},{8,10},{10,8},{12,14},{14,12},{1,3},{3,1},... | collective-permute-start | bytes 1179656 | tf_op jit(solution)/shard_map/ppermute | solution.py:336
  63.2 18.4 %copy-start.2 = (s32[8]{0:T(128)S(1)}, s32[8]{0:T(128)}, u32[]{:S(2)}) copy-start(s32[8]{0:T(128)} %rows.1) | copy-start | bytes 100
  64.0 10.4 %collective-permute-start.15 = (bf16[8,64,256]{2,1,0:T(8,128)(2,1)S(1)}, bf16[8,64,256]{2,1,0:T(8,128)(2,1)S(1)}, u32[]{:S(2)}, u32[]{:S(2)}) collective-permute-start(bf16[8,64,256]{2,1,0:T(8,128)(2,1)S(1)} %shard_map.88), channel_id=1, source_target_pairs={{4,8},{6,10},{8,4},{10,6},{5,9},{7,11},{9,5},{11,7},{20,24},{22,26... | collective-permute-start | bytes 786440 | tf_op jit(solution)/shard_map/ppermute | solution.py:353
  66.1 8.3 %collective-permute-start.17 = (bf16[8,64,256]{2,1,0:T(8,128)(2,1)S(1)}, bf16[8,64,256]{2,1,0:T(8,128)(2,1)S(1)}, u32[]{:S(2)}, u32[]{:S(2)}) collective-permute-start(bf16[8,64,256]{2,1,0:T(8,128)(2,1)S(1)} %shard_map.89), channel_id=1, source_target_pairs={{4,8},{6,10},{8,4},{10,6},{5,9},{7,11},{9,5},{11,7},{20,24},{22,26... | collective-permute-start | bytes 786440 | tf_op jit(solution)/shard_map/ppermute | solution.py:353
  66.9 11.9 %collective-permute-start.7 = (bf16[8,64,256]{2,1,0:T(8,128)(2,1)S(1)}, bf16[8,64,256]{2,1,0:T(8,128)(2,1)S(1)}, u32[]{:S(2)}, u32[]{:S(2)}) collective-permute-start(bf16[8,64,256]{2,1,0:T(8,128)(2,1)S(1)} %shard_map.82), channel_id=1, source_target_pairs={{0,4},{2,6},{4,0},{6,2},{8,12},{10,14},{12,8},{14,10},{1,5},{3,7},... | collective-permute-start | bytes 786440 | tf_op jit(solution)/shard_map/ppermute | solution.py:352
  74.3 7.3 %collective-permute-start.13 = (bf16[8,64,256]{2,1,0:T(8,128)(2,1)S(1)}, bf16[8,64,256]{2,1,0:T(8,128)(2,1)S(1)}, u32[]{:S(2)}, u32[]{:S(2)}) collective-permute-start(bf16[8,64,256]{2,1,0:T(8,128)(2,1)S(1)} %shard_map.87), channel_id=1, source_target_pairs={{0,4},{2,6},{4,0},{6,2},{8,12},{10,14},{12,8},{14,10},{1,5},{3,7},... | collective-permute-start | bytes 786440 | tf_op jit(solution)/shard_map/ppermute | solution.py:352

commit v4 on v3

v4 whole, which is shorter than its diff:
```python
import functools

import jax
import jax.numpy as jnp
from jax import lax
from jax.experimental import pallas as pl
from jax.experimental.pallas import tpu as pltpu
from jax.sharding import PartitionSpec as P

SMEM = pl.BlockSpec(memory_space=pltpu.SMEM)
VMEM = pl.BlockSpec(memory_space=pltpu.VMEM)
HBM = pl.BlockSpec(memory_space=pltpu.HBM)
Y = 2
OWN, SEND, CROSS = range(3)


def split(x, by):
    if by & (by - 1) == 0:
        return lax.shift_right_logical(x, by.bit_length() - 1), x & (by - 1)
    return x // by, lax.rem(x, by)


def wrap(x, by):
    x = jnp.where(x < 0, x + by, x)
    return jnp.where(x >= by, x - by, x)


def shifts_kernel(slots, masked, left, right, *refs):
    pieces = (len(refs) - 5) // 2
    send, keep = refs[:pieces], refs[pieces:2 * pieces]
    lbuf, rbuf, inner, acc, sems = refs[2 * pieces:]
    n_w, n_s, blk = right.shape[:3]
    classes, _, size = send[0].shape[:3]
    depth = lbuf.shape[0]
    me = lax.axis_index("mpo")

    def copies(s):
        at = lax.rem(s, depth)
        return (
            pltpu.make_async_copy(left.at[:, s], lbuf.at[at], sems.at[0, at]),
            pltpu.make_async_copy(right.at[:, s], rbuf.at[at], sems.at[1, at]),
        )

    for s in range(min(depth, n_s)):
        for c in copies(jnp.int32(s)):
            c.start()

    def sector(s, _):
        at = lax.rem(s, depth)
        for c in copies(s):
            c.wait()
        for c in range(classes):
            acc[c] = jnp.zeros(acc.shape[1:], jnp.float32)
        for w in range(n_w):
            inner[w * blk:(w + 1) * blk] = jnp.dot(
                lbuf[at, w], masked[s], preferred_element_type=jnp.float32
            ).astype(jnp.bfloat16)
        for w in range(n_w):
            acc[slots[s, w]] += jnp.dot(
                inner[w * blk:(w + 1) * blk], rbuf[at, w], preferred_element_type=jnp.float32
            )

        @pl.when(s + depth < n_s)
        def _():
            for c in copies(s + depth):
                c.start()

        for piece in range(pieces):
            mine = pl.multiple_of(me * (blk // 2) + piece * size, size)
            other = pl.multiple_of((1 - me) * (blk // 2) + piece * size, size)
            for c in range(classes):
                keep[piece][c, s] = acc[c, pl.ds(mine, size), :].astype(jnp.bfloat16)
                send[piece][c, s] = acc[c, pl.ds(other, size), :].astype(jnp.bfloat16)
        return 0

    lax.fori_loop(0, n_s, sector, 0)


def shift_sums(psi, left_env, right_env, term_class, active, sector_rows, classes, pieces):
    n_w, n_s, blk = left_env.shape[:3]
    size = blk // 2 // pieces
    depth = 3
    line = jnp.arange(blk, dtype=jnp.int32)
    masked = jnp.where(line[None, :, None] < sector_rows[:, None, None], psi, jnp.zeros_like(psi))
    slots = jnp.where(active.T == 1, term_class[None, :], classes)
    outs = pl.pallas_call(
        shifts_kernel,
        out_shape=[jax.ShapeDtypeStruct((classes, n_s, size, blk), jnp.bfloat16)] * (2 * pieces),
        in_specs=[SMEM, VMEM, HBM, HBM],
        out_specs=[VMEM] * (2 * pieces),
        scratch_shapes=[
            pltpu.VMEM((depth, n_w, blk, blk), jnp.bfloat16),
            pltpu.VMEM((depth, n_w, blk, blk), jnp.bfloat16),
            pltpu.VMEM((n_w * blk, blk), jnp.bfloat16),
            pltpu.VMEM((classes + 1, blk, blk), jnp.float32),
            pltpu.SemaphoreType.DMA((2, depth)),
        ],
        compiler_params=pltpu.CompilerParams(vmem_limit_bytes=40 * 2**20),
        cost_estimate=pl.CostEstimate(
            flops=4 * n_w * n_s * blk**3, bytes_accessed=4 * n_w * n_s * blk * blk, transcendentals=0
        ),
    )(slots, masked, left_env, right_env)
    outs = [x.reshape(classes * n_s, size, blk) for x in outs]
    return outs[:pieces], outs[pieces:]


def table_at(cap, q, kind):
    return (q * 3 + kind) * (1 + 2 * cap)


def table_kernel(n, cap, dest, table):
    classes, n_s = dest.shape
    line = n // Y
    d = lax.axis_index("sector")
    z, y = split(d, Y)
    even = (z & 1) == 0

    for i in range(3 * line):
        table[i * (1 + 2 * cap)] = 0
        for slot in range(cap):
            table[i * (1 + 2 * cap) + 1 + slot] = 0
            table[i * (1 + 2 * cap) + 1 + cap + slot] = n_s

    def position(twice):
        m = wrap(lax.shift_right_arithmetic(twice, 1), line)
        return jnp.where(m == 0, line - 1, jnp.where(even, line - 1 - m, m - 1))

    def note(q, kind, j, p):
        at = table_at(cap, q, kind)
        count = table[at]
        table[at + 1 + count] = j
        table[at + 1 + cap + count] = p
        table[at] = count + 1

    for c in range(classes):

        def step(i, _, c=c):
            t, p = split(dest[c, i], n_s)
            k = wrap(t - d, n)
            j = c * n_s + i

            @pl.when((k & 1) == 0)
            def _():
                note(position(k), OWN, j, p)

            @pl.when((k & 1) == 1)
            def _():
                note(position(k - 1 + 2 * y), SEND, j, p)
                note(position(k + 1 - 2 * y), CROSS, j, p)

            return 0

        lax.fori_loop(0, n_s, step, 0)


def make_table(n, cap, dest):
    return pl.pallas_call(
        functools.partial(table_kernel, n, cap),
        out_shape=jax.ShapeDtypeStruct((3 * (n // Y) * (1 + 2 * cap),), jnp.int32),
        in_specs=[SMEM],
        out_specs=SMEM,
        cost_estimate=pl.CostEstimate(flops=4000, bytes_accessed=4000, transcendentals=0),
    )(dest)


def small_call(kernel, outs, table, ins, after=(), scratch=()):
    spare = len(after)

    def body(table, *refs):
        kernel(table, *refs[:len(ins)], *refs[len(ins) + spare:])

    return pl.pallas_call(
        body,
        out_shape=outs,
        in_specs=[SMEM] + [VMEM] * len(ins) + [pl.BlockSpec(memory_space=pl.ANY)] * spare,
        out_specs=[VMEM] * len(outs),
        scratch_shapes=scratch,
        compiler_params=pltpu.CompilerParams(vmem_limit_bytes=16 * 2**20),
        cost_estimate=pl.CostEstimate(flops=0, bytes_accessed=1000, transcendentals=0),
    )(table, *ins, *after)


def pack(cap, qs, table, keep, recv, after):
    _, size, blk = keep.shape

    def kernel(table, keep, recv, *outs):
        for q, out in zip(qs, outs):
            for slot in range(cap):
                j = table[table_at(cap, q, SEND) + 1 + slot]
                out[slot] = keep[j] + recv[j]

    return small_call(kernel, [jax.ShapeDtypeStruct((cap, size, blk), jnp.bfloat16)] * len(qs), table, (keep, recv), after)


def gather(cap, q, n_s, table, keep, recv, crossed, after, dtype=jnp.bfloat16):
    _, size, blk = keep.shape

    def kernel(table, keep, recv, crossed, out, total):
        total[...] = jnp.zeros_like(total)
        at = table_at(cap, q, OWN) + 1
        for slot in range(cap):
            j = table[at + slot]
            total[table[at + cap + slot]] += (keep[j] + recv[j]).astype(jnp.float32)
        at = table_at(cap, q, CROSS) + 1
        for slot in range(cap):
            total[table[at + cap + slot]] += crossed[slot].astype(jnp.float32)
        out[...] = total[:n_s].astype(dtype)

    (out,) = small_call(
        kernel,
        [jax.ShapeDtypeStruct((n_s, size, blk), dtype)],
        table,
        (keep, recv, crossed),
        after,
        [pltpu.VMEM((n_s + 1, size, blk), jnp.float32)],
    )
    return out


def plus(table, a, b, after):
    def kernel(table, a, b, out):
        out[...] = a[...] + b[...]

    (out,) = small_call(kernel, [jax.ShapeDtypeStruct(a.shape, a.dtype)], table, (a, b), after)
    return out


def finish(rows, bases, arrived):
    n_s, size, blk = bases[0].shape
    pieces = len(bases)

    def kernel(rows, *refs):
        out = refs[-1]
        line = lax.broadcasted_iota(jnp.int32, (size, blk), 0) + lax.axis_index("mpo") * (size * pieces)
        for piece in range(pieces):
            for p in range(n_s):
                total = refs[piece][p]
                for part in refs[pieces + piece:-1:pieces]:
                    total += part[p].astype(jnp.float32)
                total = jnp.where(line + piece * size < rows[p], total, 0.0)
                out[p, piece * size:(piece + 1) * size] = total.astype(jnp.bfloat16)

    flat = list(bases) + [x for parts in arrived for x in parts]
    return pl.pallas_call(
        kernel,
        out_shape=jax.ShapeDtypeStruct((n_s, size * pieces, blk), jnp.bfloat16),
        in_specs=[SMEM] + [VMEM] * len(flat),
        out_specs=VMEM,
        compiler_params=pltpu.CompilerParams(vmem_limit_bytes=16 * 2**20),
        cost_estimate=pl.CostEstimate(flops=0, bytes_accessed=1000, transcendentals=0),
    )(rows, *flat)


def body(psi, left_env, right_env, term_class, active, dest, sector_rows):
    n = lax.axis_size("sector")
    line = n // Y
    classes, n_s = dest.shape
    cap = (classes * n_s + n - 1) // n + 1
    pieces = range(2)
    across = [(d, d ^ 1) for d in range(n)]
    near = [(z * Y + y, (z ^ 1) * Y + y) for z in range(line) for y in range(Y)]
    far = [(z * Y + y, (((z + 1) ^ 1) - 1) * Y + y) for z in range(1, line - 1) for y in range(Y)]

    def cross(x):
        return lax.ppermute(x, "sector", across)

    send, keep = shift_sums(psi, left_env, right_env, term_class, active, sector_rows, classes, len(pieces))
    recv = [lax.ppermute(x, "mpo", [(0, 1), (1, 0)]) for x in send]
    table = make_table(n, cap, dest)
    last = ()
    crossed = [[None] * len(pieces) for _ in range(line)]
    for qs in ([0], [1], list(range(2, line))):
        for i in pieces:
            packed = pack(cap, qs, table, keep[i], recv[i], last)
            last = (packed[0],)
            for q, x in zip(qs, packed):
                crossed[q][i] = cross(x)

    acc = [[None] * len(pieces) for _ in range(line)]

    def sums(q, i):
        if acc[q][i] is None:
            dtype = jnp.float32 if q == line - 1 else jnp.bfloat16
            acc[q][i] = gather(cap, q, n_s, table, keep[i], recv[i], crossed[q][i], last, dtype)
        return acc[q][i], (acc[q][i],)

    near_in, far_in = [None] * len(pieces), [None] * len(pieces)
    for step in range(1, line):
        near_out, far_out = [None] * len(pieces), [None] * len(pieces)
        for i in pieces:
            near_out[i], last = sums(step - 1, i)
            if far_in[i] is not None:
                near_out[i] = plus(table, near_out[i], far_in[i], last)
                last = (near_out[i],)
            if step > 1:
                base, last = sums(line - 1 - step, i)
                far_out[i] = plus(table, base, near_in[i], last)
                last = (far_out[i],)
        near_in = [lax.ppermute(x, "sector", near) for x in near_out]
        far_in = [None if x is None else lax.ppermute(x, "sector", far) for x in far_out]
    bases = [sums(line - 1, i)[0] for i in pieces]
    return finish(sector_rows, bases, [x for x in (near_in, far_in) if x[0] is not None])


def solution(mesh):
    placed = (
        P(("groups", "sector"), None, None),
        P(("groups", "mpo"), "sector", None, None),
        P(("groups", "mpo"), "sector", None, None),
        P(("groups", "mpo")),
        P(("groups", "mpo"), "sector"),
        P("groups", "sector"),
        P(("groups", "sector")),
    )
    return jax.shard_map(
        body,
        mesh=mesh,
        in_specs=placed,
        out_specs=P(("groups", "sector"), "mpo", None),
        check_vma=False,
    )
```

time: 83.8 us -> 81 us (0.967)
  waiting for transfers between devices: 16.7 us -> 10.9 us
  starting transfers between devices: 26.9 us -> 28.1 us
  local copies, waits for them, and re-layouts: 0.69 us -> 1.77 us
    ppermute x14 -> x16, waiting for transfers between devices: 16.7 us -> 10.9 us  [the longest x8 7.8 us: cross(): return lax.ppermute(x, 'sector', across)]
    ppermute x14 -> x16, starting transfers between devices: 24.2 us -> 25.4 us  [the longest x6 15 us: body(): near_in = [lax.ppermute(x, 'sector', near) for x in near_out]]
    unnamed x6 -> x10, local copies, waits for them, and re-layouts: 0.69 us -> 1.77 us
    pallas_call x17 -> x22, Pallas kernels: 33 us -> 33.6 us  [the longest x20 18.1 us: small_call(): pl.pallas_call(body, out_shape=outs, in_specs=[SMEM] + [VMEM] * len(ins)...]
  transfers between devices with their start and end apart: 18 -> 20, of which waited for: 7 -> 7; matrix products, arithmetic and copies ran while one was open for 0% -> 0% of each run, Pallas kernels for 14% -> 26%
where the time goes in v4:
time: 81 us; the launch traced here: 80.4 us
  Pallas kernels  36.5 us (45%)
  starting transfers between devices  28.1 us (35%)
  waiting for transfers between devices  10.9 us (13%)
  other arithmetic  2.91 us (4%)
  local copies, waits for them, and re-layouts  1.77 us (2%)
    pallas_call x20, Pallas kernels, small_call(): pl.pallas_call(body, out_shape=outs, in_specs=[SMEM] + [VMEM] * len(ins)...  18.1 us
    ppermute x6, starting transfers between devices, body(): near_in = [lax.ppermute(x, 'sector', near) for x in near_out]  15 us
    pallas_call x1, Pallas kernels, shift_sums(): pl.pallas_call(shifts_kernel, out_shape=[jax.ShapeDtypeStruct((classes, n...  13.9 us
    ppermute x8, starting transfers between devices, cross(): return lax.ppermute(x, 'sector', across)  9.91 us
    ppermute x8, waiting for transfers between devices, cross(): return lax.ppermute(x, 'sector', across)  7.8 us
    pallas_call x1, Pallas kernels, make_table(): pl.pallas_call(functools.partial(table_kernel, n, cap), out_shape=jax.Sha...  2.92 us
    ppermute x4, starting transfers between devices, body(): lax.ppermute(x, 'sector', far)  2.69 us
    unnamed x10, local copies, waits for them, and re-layouts  1.77 us
  transfers between devices with their start and end apart: 20, of which 7 were waited for; matrix products, arithmetic and copies ran while one was open for 0% of the time, Pallas kernels for 26%

profile of v4, /device:TPU:0, one launch (start us, length us, event | category | flops | bytes accessed | tf_op | source)
XLA Modules:
  0.0 80.4 jit_solution(10337003470990025734)
XLA Ops:
  0.0 0.7 iota_compare_fusion
  0.7 0.7 select_bitcast_fusion.slots
  1.4 1.5 %broadcast_select_fusion.masked = bf16[8,256,256]{2,1,0:T(8,128)(2,1)S(1)} fusion(bf16[8,256,256]{2,1,0:T(8,128)(2,1)} %param.7, pred[8,256]{1,0:T(8,128)(4,1)S(1)} %iota_compare_fusion), kind=kLoop, calls=%fused_computation | loop fusion | flops 524288 | bytes 2099200 | tf_op jit(solution)/shard_map/jit(_where)/select_n | solution.py:84
  2.9 13.9 %shard_map.74 = (bf16[5,8,64,256]{3,2,1,0:T(8,128)(2,1)}, bf16[5,8,64,256]{3,2,1,0:T(8,128)(2,1)}, bf16[5,8,64,256]{3,2,1,0:T(8,128)(2,1)S(1)}, bf16[5,8,64,256]{3,2,1,0:T(8,128)(2,1)S(1)}) custom-call(s32[8,13]{1,0:T(8,128)S(1)} %select_bitcast_fusion.slots, bf16[8,256,256]{2,1,0:T(8,128)(2,1)S(1)} %broadcast_select_fusion.masked, ...), custom_call_target="tpu_custom_call" | custom-call | flops 6979321856 | bytes 27262976 | tf_op jit(solution)/shard_map/pallas_call | solution.py:86
  16.8 1.1 %copy-done = bf16[5,8,64,256]{3,2,1,0:T(8,128)(2,1)} copy-done((bf16[5,8,64,256]{3,2,1,0:T(8,128)(2,1)}, bf16[5,8,64,256]{3,2,1,0:T(8,128)(2,1)S(1)}, u32[]{:S(2)}) %copy-start) | copy-done | bytes 1310744
  17.9 0.5 collective-permute-start
  18.4 0.0 collective-permute-start.1
  18.4 2.9 %shard_map.73.table = s32[156]{0:T(256)} custom-call(s32[5,8]{1,0:T(8,128)} %dest.1), custom_call_target="tpu_custom_call" | custom-call | flops 4000 | bytes 4000 | tf_op jit(solution)/shard_map/pallas_call | solution.py:157
  21.3 1.3 %collective-permute-done.refs_1_ = bf16[40,64,256]{2,1,0:T(8,128)(2,1)S(1)} collective-permute-done((bf16[40,64,256]{2,1,0:T(8,128)(2,1)}, bf16[40,64,256]{2,1,0:T(8,128)(2,1)S(1)}, u32[]{:S(2)}, u32[]{:S(2)}) %collective-permute-start) | collective-permute-done | bytes 1310752 | tf_op jit(solution)/shard_map/ppermute | solution.py:268
  22.7 0.7 copy-done.2
  23.4 0.6 shard_map.75.refs_2_
  24.0 3.0 %collective-permute-start.4 = (bf16[6,64,256]{2,1,0:T(8,128)(2,1)S(1)}, bf16[6,64,256]{2,1,0:T(8,128)(2,1)S(1)}, u32[]{:S(2)}, u32[]{:S(2)}) collective-permute-start(bf16[6,64,256]{2,1,0:T(8,128)(2,1)S(1)} %shard_map.75.refs_2_), channel_id=1, source_target_pairs={{0,2},{2,0},{4,6},{6,4},{8,10},{10,8},{12,14},{14,12},{1,3},{3,1},... | collective-permute-start | bytes 589832 | tf_op jit(solution)/shard_map/ppermute | solution.py:265
  27.0 0.0 collective-permute-done.1.refs_1_
  27.0 1.4 %shard_map.76.refs_2_ = bf16[6,64,256]{2,1,0:T(8,128)(2,1)S(1)} custom-call(s32[156]{0:T(256)S(1)} %copy-done.3, bf16[40,64,256]{2,1,0:T(8,128)(2,1)S(1)} %bitcast.13, bf16[40,64,256]{2,1,0:T(8,128)(2,1)} %collective-permute-done.1.refs_1_, bf16[6,64,256]{2,1,0:T(8,128)(2,1)S(1)} %shard_map.75.refs_2_), custom_call_target="tpu_custom_call" | custom-call | bytes 1000 | tf_op jit(solution)/shard_map/pallas_call | solution.py:172
  28.3 0.7 collective-permute-start.3
  29.0 0.6 shard_map.77.refs_2_
  29.6 1.4 %collective-permute-start.6 = (bf16[6,64,256]{2,1,0:T(8,128)(2,1)S(1)}, bf16[6,64,256]{2,1,0:T(8,128)(2,1)S(1)}, u32[]{:S(2)}, u32[]{:S(2)}) collective-permute-start(bf16[6,64,256]{2,1,0:T(8,128)(2,1)S(1)} %shard_map.77.refs_2_), channel_id=1, source_target_pairs={{0,2},{2,0},{4,6},{6,4},{8,10},{10,8},{12,14},{14,12},{1,3},{3,1},... | collective-permute-start | bytes 589832 | tf_op jit(solution)/shard_map/ppermute | solution.py:265
  31.1 1.3 %shard_map.78.refs_2_ = bf16[6,64,256]{2,1,0:T(8,128)(2,1)S(1)} custom-call(s32[156]{0:T(256)S(1)} %copy-done.3, bf16[40,64,256]{2,1,0:T(8,128)(2,1)S(1)} %bitcast.14, bf16[40,64,256]{2,1,0:T(8,128)(2,1)} %collective-permute-done.1.refs_1_, bf16[6,64,256]{2,1,0:T(8,128)(2,1)S(1)} %shard_map.77.refs_2_), custom_call_target="tpu_custom_call" | custom-call | bytes 1000 | tf_op jit(solution)/shard_map/pallas_call | solution.py:172
  32.4 0.6 shard_map.79
  33.0 1.4 %shard_map.80 = (bf16[6,64,256]{2,1,0:T(8,128)(2,1)S(1)}, bf16[6,64,256]{2,1,0:T(8,128)(2,1)S(1)}) custom-call(s32[156]{0:T(256)S(1)} %copy-done.3, bf16[40,64,256]{2,1,0:T(8,128)(2,1)S(1)} %bitcast.15, bf16[40,64,256]{2,1,0:T(8,128)(2,1)} %collective-permute-done.1.refs_1_, bf16[6,64,256]{2,1,0:T(8,128)(2,1)S(1)} %get-tuple-element.18.refs_2_), custom_call_target="tpu_custom_call" | custom-call | bytes 1000 | tf_op jit(solution)/shard_map/pallas_call | solution.py:172
  34.4 0.0 collective-permute-done.4.refs_2_
  34.4 0.7 shard_map.81.refs_3_.refs_0_.refs_2_
  35.1 1.7 %collective-permute-start.7 = (bf16[8,64,256]{2,1,0:T(8,128)(2,1)S(1)}, bf16[8,64,256]{2,1,0:T(8,128)(2,1)S(1)}, u32[]{:S(2)}, u32[]{:S(2)}) collective-permute-start(bf16[8,64,256]{2,1,0:T(8,128)(2,1)S(1)} %shard_map.81.refs_3_.refs_0_.refs_2_), channel_id=1, source_target_pairs={{0,4},{2,6},{4,0},{6,2},{8,12},{10,14},{12,8},{14,10},{1,5},{3,7},... | collective-permute-start | bytes 786440 | tf_op jit(solution)/shard_map/ppermute | solution.py:299
  36.8 0.1 collective-permute-done.3.refs_2_
  36.9 1.5 %shard_map.82.refs_3_.refs_0_.refs_2_ = bf16[8,64,256]{2,1,0:T(8,128)(2,1)S(1)} custom-call(s32[156]{0:T(256)S(1)} %copy-done.3, bf16[40,64,256]{2,1,0:T(8,128)(2,1)S(1)} %bitcast.16, bf16[40,64,256]{2,1,0:T(8,128)(2,1)} %collective-permute-done.1.refs_1_, bf16[6,64,256]{2,1,0:T(8,128)(2,1)S(1)} %collective-permute-done.3.refs_2_, ...), custom_call_target="tpu_custom_call" | custom-call | bytes 1000 | tf_op jit(solution)/shard_map/pallas_call | solution.py:172
  38.3 2.2 %collective-permute-start.11 = (bf16[8,64,256]{2,1,0:T(8,128)(2,1)S(1)}, bf16[8,64,256]{2,1,0:T(8,128)(2,1)S(1)}, u32[]{:S(2)}, u32[]{:S(2)}) collective-permute-start(bf16[8,64,256]{2,1,0:T(8,128)(2,1)S(1)} %shard_map.82.refs_3_.refs_0_.refs_2_), channel_id=1, source_target_pairs={{0,4},{2,6},{4,0},{6,2},{8,12},{10,14},{12,8},{14,10},{1,5},{3,7},... | collective-permute-start | bytes 786440 | tf_op jit(solution)/shard_map/ppermute | solution.py:299
  40.5 1.5 %collective-permute-start.5 = (bf16[6,64,256]{2,1,0:T(8,128)(2,1)S(1)}, bf16[6,64,256]{2,1,0:T(8,128)(2,1)S(1)}, u32[]{:S(2)}, u32[]{:S(2)}) collective-permute-start(bf16[6,64,256]{2,1,0:T(8,128)(2,1)S(1)} %shard_map.78.refs_2_), channel_id=1, source_target_pairs={{0,2},{2,0},{4,6},{6,4},{8,10},{10,8},{12,14},{14,12},{1,3},{3,1},... | collective-permute-start | bytes 589832 | tf_op jit(solution)/shard_map/ppermute | solution.py:265
  42.1 0.5 collective-permute-start.14
  42.6 0.7 shard_map.83.refs_0_.refs_2_
  43.3 0.3 collective-permute-start.15
  43.6 0.8 %collective-permute-done.7.refs_1_ = bf16[8,64,256]{2,1,0:T(8,128)(2,1)S(1)} collective-permute-done((bf16[8,64,256]{2,1,0:T(8,128)(2,1)S(1)}, bf16[8,64,256]{2,1,0:T(8,128)(2,1)S(1)}, u32[]{:S(2)}, u32[]{:S(2)}) %collective-permute-start.7) | collective-permute-done | bytes 262176 | tf_op jit(solution)/shard_map/ppermute | solution.py:299
  44.4 0.6 shard_map.84.refs_3_
  45.0 2.6 %collective-permute-done.5.refs_2_ = bf16[6,64,256]{2,1,0:T(8,128)(2,1)S(1)} collective-permute-done((bf16[6,64,256]{2,1,0:T(8,128)(2,1)S(1)}, bf16[6,64,256]{2,1,0:T(8,128)(2,1)S(1)}, u32[]{:S(2)}, u32[]{:S(2)}) %collective-permute-start.5) | collective-permute-done | bytes 196640 | tf_op jit(solution)/shard_map/ppermute | solution.py:265
  47.7 1.5 %shard_map.85.refs_0_.refs_2_ = bf16[8,64,256]{2,1,0:T(8,128)(2,1)S(1)} custom-call(s32[156]{0:T(256)S(1)} %copy-done.3, bf16[40,64,256]{2,1,0:T(8,128)(2,1)S(1)} %bitcast.17, bf16[40,64,256]{2,1,0:T(8,128)(2,1)} %collective-permute-done.1.refs_1_, bf16[6,64,256]{2,1,0:T(8,128)(2,1)S(1)} %collective-permute-done.5.refs_2_, ...), custom_call_target="tpu_custom_call" | custom-call | bytes 1000 | tf_op jit(solution)/shard_map/pallas_call | solution.py:172
  49.2 0.9 %collective-permute-done.11.refs_1_ = bf16[8,64,256]{2,1,0:T(8,128)(2,1)S(1)} collective-permute-done((bf16[8,64,256]{2,1,0:T(8,128)(2,1)S(1)}, bf16[8,64,256]{2,1,0:T(8,128)(2,1)S(1)}, u32[]{:S(2)}, u32[]{:S(2)}) %collective-permute-start.11) | collective-permute-done | bytes 262176 | tf_op jit(solution)/shard_map/ppermute | solution.py:299
  50.1 0.6 shard_map.89.refs_3_
  50.7 0.7 collective-permute-start.16
  51.3 4.5 %collective-permute-start.8 = (bf16[8,64,256]{2,1,0:T(8,128)(2,1)S(1)}, bf16[8,64,256]{2,1,0:T(8,128)(2,1)S(1)}, u32[]{:S(2)}, u32[]{:S(2)}) collective-permute-start(bf16[8,64,256]{2,1,0:T(8,128)(2,1)S(1)} %shard_map.85.refs_0_.refs_2_), channel_id=1, source_target_pairs={{0,4},{2,6},{4,0},{6,2},{8,12},{10,14},{12,8},{14,10},{1,5},{3,7},... | collective-permute-start | bytes 786440 | tf_op jit(solution)/shard_map/ppermute | solution.py:299
  55.8 0.7 collective-permute-start.12
  56.5 0.7 collective-permute-start.10
  57.2 1.4 %collective-permute-start.9 = (bf16[6,64,256]{2,1,0:T(8,128)(2,1)S(1)}, bf16[6,64,256]{2,1,0:T(8,128)(2,1)S(1)}, u32[]{:S(2)}, u32[]{:S(2)}) collective-permute-start(bf16[6,64,256]{2,1,0:T(8,128)(2,1)S(1)} %get-tuple-element.20), channel_id=1, source_target_pairs={{0,2},{2,0},{4,6},{6,4},{8,10},{10,8},{12,14},{14,12},{1,3},{3,1},... | collective-permute-start | bytes 589832 | tf_op jit(solution)/shard_map/ppermute | solution.py:265
  58.6 0.6 shard_map.92.refs_3_
  59.2 1.5 %shard_map.93.refs_0_.refs_2_ = bf16[8,64,256]{2,1,0:T(8,128)(2,1)S(1)} custom-call(s32[156]{0:T(256)S(1)} %copy-done.3, bf16[40,64,256]{2,1,0:T(8,128)(2,1)S(1)} %bitcast.18, bf16[40,64,256]{2,1,0:T(8,128)(2,1)} %collective-permute-done.1.refs_1_, bf16[6,64,256]{2,1,0:T(8,128)(2,1)S(1)} %collective-permute-done.14.refs_2_, ...), custom_call_target="tpu_custom_call" | custom-call | bytes 1000 | tf_op jit(solution)/shard_map/pallas_call | solution.py:172
  60.7 1.6 %collective-permute-done.10.refs_2_ = bf16[6,64,256]{2,1,0:T(8,128)(2,1)S(1)} collective-permute-done((bf16[6,64,256]{2,1,0:T(8,128)(2,1)S(1)}, bf16[6,64,256]{2,1,0:T(8,128)(2,1)S(1)}, u32[]{:S(2)}, u32[]{:S(2)}) %collective-permute-start.10) | collective-permute-done | bytes 196640 | tf_op jit(solution)/shard_map/ppermute | solution.py:265
  62.2 0.7 collective-permute-start.18
  62.9 0.7 shard_map.90.refs_0_.refs_2_
  63.6 0.0 collective-permute-done.16.refs_1_
  63.6 0.6 shard_map.94
  64.2 4.6 %collective-permute-start.17 = (bf16[8,64,256]{2,1,0:T(8,128)(2,1)S(1)}, bf16[8,64,256]{2,1,0:T(8,128)(2,1)S(1)}, u32[]{:S(2)}, u32[]{:S(2)}) collective-permute-start(bf16[8,64,256]{2,1,0:T(8,128)(2,1)S(1)} %shard_map.94), channel_id=1, source_target_pairs={{0,4},{2,6},{4,0},{6,2},{8,12},{10,14},{12,8},{14,10},{1,5},{3,7},... | collective-permute-start | bytes 786440 | tf_op jit(solution)/shard_map/ppermute | solution.py:299
  68.8 0.0 collective-permute-done.8.refs_1_
  68.8 0.6 shard_map.86.refs_3_
  69.4 0.7 collective-permute-start.19
  70.1 0.0 collective-permute-done.12.refs_1_
  70.1 0.6 shard_map.91
  70.7 1.8 %collective-permute-start.13 = (bf16[8,64,256]{2,1,0:T(8,128)(2,1)S(1)}, bf16[8,64,256]{2,1,0:T(8,128)(2,1)S(1)}, u32[]{:S(2)}, u32[]{:S(2)}) collective-permute-start(bf16[8,64,256]{2,1,0:T(8,128)(2,1)S(1)} %shard_map.91), channel_id=1, source_target_pairs={{0,4},{2,6},{4,0},{6,2},{8,12},{10,14},{12,8},{14,10},{1,5},{3,7},... | collective-permute-start | bytes 786440 | tf_op jit(solution)/shard_map/ppermute | solution.py:299
  72.4 0.6 collective-permute-start.2
  73.1 1.5 %shard_map.88.refs_1_ = f32[8,64,256]{2,1,0:T(8,128)S(1)} custom-call(s32[156]{0:T(256)S(1)} %copy-done.3, bf16[40,64,256]{2,1,0:T(8,128)(2,1)S(1)} %bitcast.19, bf16[40,64,256]{2,1,0:T(8,128)(2,1)} %collective-permute-done.1.refs_1_, bf16[6,64,256]{2,1,0:T(8,128)(2,1)S(1)} %collective-permute-done.9.refs_2_, bf16[8,64,256]{2,1,0:T(8,128)(2,1)S(1)} %shard_map.86.refs_3_), custom_call_target="tpu_custom_call" | custom-call | bytes 1000 | tf_op jit(solution)/shard_map/pallas_call | solution.py:172
  74.6 0.0 copy-start.4
  74.6 3.5 %collective-permute-done.2.refs_2_ = bf16[6,64,256]{2,1,0:T(8,128)(2,1)S(1)} collective-permute-done((bf16[6,64,256]{2,1,0:T(8,128)(2,1)S(1)}, bf16[6,64,256]{2,1,0:T(8,128)(2,1)S(1)}, u32[]{:S(2)}, u32[]{:S(2)}) %collective-permute-start.2) | collective-permute-done | bytes 196640 | tf_op jit(solution)/shard_map/ppermute | solution.py:265
  78.1 0.7 shard_map.87.refs_0_
  78.8 0.0 collective-permute-done.18.refs_4_
  78.8 0.0 collective-permute-done.19.refs_5_
  78.9 0.0 collective-permute-done.13.refs_2_
  78.9 1.6 %shard_map.95 = bf16[8,128,256]{2,1,0:T(8,128)(2,1)} custom-call(s32[8]{0:T(128)S(1)} %copy-done.4, f32[8,64,256]{2,1,0:T(8,128)S(1)} %shard_map.87.refs_0_, f32[8,64,256]{2,1,0:T(8,128)S(1)} %shard_map.88.refs_1_, bf16[8,64,256]{2,1,0:T(8,128)(2,1)S(1)} %collective-permute-done.13.refs_2_, bf16[8,64,256]{2,1,0:T(8,128)(2,1)S(1)} %collective-permute-done.17.refs_3_, ...), custom_call_target="tpu_custom_call" | custom-call | bytes 1000 | tf_op jit(solution)/shard_map/pallas_call | solution.py:244
  (12 shorter events, 0.0 us)
Async XLA Ops:
  16.8 1.1 %copy-start = (bf16[5,8,64,256]{3,2,1,0:T(8,128)(2,1)}, bf16[5,8,64,256]{3,2,1,0:T(8,128)(2,1)S(1)}, u32[]{:S(2)}) copy-start(bf16[5,8,64,256]{3,2,1,0:T(8,128)(2,1)S(1)} %get-tuple-element.15) | copy-start | bytes 3932164
  17.9 4.8 %collective-permute-start = (bf16[40,64,256]{2,1,0:T(8,128)(2,1)}, bf16[40,64,256]{2,1,0:T(8,128)(2,1)S(1)}, u32[]{:S(2)}, u32[]{:S(2)}) collective-permute-start(bf16[40,64,256]{2,1,0:T(8,128)(2,1)} %bitcast.2), channel_id=1, source_target_pairs={{0,1},{1,0},{2,3},{3,2},{4,5},{5,4},{6,7},{7,6},{8,9},{9,8},{10,11... | collective-permute-start | bytes 3932168 | tf_op jit(solution)/shard_map/ppermute | solution.py:268
  18.4 8.6 %collective-permute-start.1 = (bf16[40,64,256]{2,1,0:T(8,128)(2,1)}, bf16[40,64,256]{2,1,0:T(8,128)(2,1)}, u32[]{:S(2)}, u32[]{:S(2)}) collective-permute-start(bf16[40,64,256]{2,1,0:T(8,128)(2,1)} %bitcast.4), channel_id=1, source_target_pairs={{0,1},{1,0},{2,3},{3,2},{4,5},{5,4},{6,7},{7,6},{8,9},{9,8},{10,11... | collective-permute-start | bytes 3932168 | tf_op jit(solution)/shard_map/ppermute | solution.py:268
  22.7 0.7 copy-start.2
  23.4 3.6 %copy-start.1 = (bf16[5,8,64,256]{3,2,1,0:T(8,128)(2,1)S(1)}, bf16[5,8,64,256]{3,2,1,0:T(8,128)(2,1)}, u32[]{:S(2)}) copy-start(bf16[5,8,64,256]{3,2,1,0:T(8,128)(2,1)} %copy-done) | copy-start | bytes 3932164
  23.4 3.6 %copy-start.3 = (s32[156]{0:T(256)S(1)}, s32[156]{0:T(256)}, u32[]{:S(2)}) copy-start(s32[156]{0:T(256)} %shard_map.73.table) | copy-start | bytes 1876
  24.0 10.5 %collective-permute-start.4 = (bf16[6,64,256]{2,1,0:T(8,128)(2,1)S(1)}, bf16[6,64,256]{2,1,0:T(8,128)(2,1)S(1)}, u32[]{:S(2)}, u32[]{:S(2)}) collective-permute-start(bf16[6,64,256]{2,1,0:T(8,128)(2,1)S(1)} %shard_map.75.refs_2_), channel_id=1, source_target_pairs={{0,2},{2,0},{4,6},{6,4},{8,10},{10,8},{12,14},{14,12},{1,3},{3,1},... | collective-permute-start | bytes 589832 | tf_op jit(solution)/shard_map/ppermute | solution.py:265
  28.3 8.5 %collective-permute-start.3 = (bf16[6,64,256]{2,1,0:T(8,128)(2,1)S(1)}, bf16[6,64,256]{2,1,0:T(8,128)(2,1)S(1)}, u32[]{:S(2)}, u32[]{:S(2)}) collective-permute-start(bf16[6,64,256]{2,1,0:T(8,128)(2,1)S(1)} %shard_map.76.refs_2_), channel_id=1, source_target_pairs={{0,2},{2,0},{4,6},{6,4},{8,10},{10,8},{12,14},{14,12},{1,3},{3,1},... | collective-permute-start | bytes 589832 | tf_op jit(solution)/shard_map/ppermute | solution.py:265
  29.6 12.9 %collective-permute-start.6 = (bf16[6,64,256]{2,1,0:T(8,128)(2,1)S(1)}, bf16[6,64,256]{2,1,0:T(8,128)(2,1)S(1)}, u32[]{:S(2)}, u32[]{:S(2)}) collective-permute-start(bf16[6,64,256]{2,1,0:T(8,128)(2,1)S(1)} %shard_map.77.refs_2_), channel_id=1, source_target_pairs={{0,2},{2,0},{4,6},{6,4},{8,10},{10,8},{12,14},{14,12},{1,3},{3,1},... | collective-permute-start | bytes 589832 | tf_op jit(solution)/shard_map/ppermute | solution.py:265
  35.1 9.3 %collective-permute-start.7 = (bf16[8,64,256]{2,1,0:T(8,128)(2,1)S(1)}, bf16[8,64,256]{2,1,0:T(8,128)(2,1)S(1)}, u32[]{:S(2)}, u32[]{:S(2)}) collective-permute-start(bf16[8,64,256]{2,1,0:T(8,128)(2,1)S(1)} %shard_map.81.refs_3_.refs_0_.refs_2_), channel_id=1, source_target_pairs={{0,4},{2,6},{4,0},{6,2},{8,12},{10,14},{12,8},{14,10},{1,5},{3,7},... | collective-permute-start | bytes 786440 | tf_op jit(solution)/shard_map/ppermute | solution.py:299
  38.3 11.7 %collective-permute-start.11 = (bf16[8,64,256]{2,1,0:T(8,128)(2,1)S(1)}, bf16[8,64,256]{2,1,0:T(8,128)(2,1)S(1)}, u32[]{:S(2)}, u32[]{:S(2)}) collective-permute-start(bf16[8,64,256]{2,1,0:T(8,128)(2,1)S(1)} %shard_map.82.refs_3_.refs_0_.refs_2_), channel_id=1, source_target_pairs={{0,4},{2,6},{4,0},{6,2},{8,12},{10,14},{12,8},{14,10},{1,5},{3,7},... | collective-permute-start | bytes 786440 | tf_op jit(solution)/shard_map/ppermute | solution.py:299
  40.5 7.1 %collective-permute-start.5 = (bf16[6,64,256]{2,1,0:T(8,128)(2,1)S(1)}, bf16[6,64,256]{2,1,0:T(8,128)(2,1)S(1)}, u32[]{:S(2)}, u32[]{:S(2)}) collective-permute-start(bf16[6,64,256]{2,1,0:T(8,128)(2,1)S(1)} %shard_map.78.refs_2_), channel_id=1, source_target_pairs={{0,2},{2,0},{4,6},{6,4},{8,10},{10,8},{12,14},{14,12},{1,3},{3,1},... | collective-permute-start | bytes 589832 | tf_op jit(solution)/shard_map/ppermute | solution.py:265
  42.1 14.4 %collective-permute-start.14 = (bf16[6,64,256]{2,1,0:T(8,128)(2,1)S(1)}, bf16[6,64,256]{2,1,0:T(8,128)(2,1)S(1)}, u32[]{:S(2)}, u32[]{:S(2)}) collective-permute-start(bf16[6,64,256]{2,1,0:T(8,128)(2,1)S(1)} %get-tuple-element.19.refs_3_), channel_id=1, source_target_pairs={{0,2},{2,0},{4,6},{6,4},{8,10},{10,8},{12,14},{14,12},{1,3},{3,1},... | collective-permute-start | bytes 589832 | tf_op jit(solution)/shard_map/ppermute | solution.py:265
  43.3 13.9 %collective-permute-start.15 = (bf16[8,64,256]{2,1,0:T(8,128)(2,1)S(1)}, bf16[8,64,256]{2,1,0:T(8,128)(2,1)S(1)}, u32[]{:S(2)}, u32[]{:S(2)}) collective-permute-start(bf16[8,64,256]{2,1,0:T(8,128)(2,1)S(1)} %shard_map.83.refs_0_.refs_2_), channel_id=1, source_target_pairs={{0,4},{2,6},{4,0},{6,2},{8,12},{10,14},{12,8},{14,10},{1,5},{3,7},... | collective-permute-start | bytes 786440 | tf_op jit(solution)/shard_map/ppermute | solution.py:299
  50.7 13.0 %collective-permute-start.16 = (bf16[8,64,256]{2,1,0:T(8,128)(2,1)S(1)}, bf16[8,64,256]{2,1,0:T(8,128)(2,1)S(1)}, u32[]{:S(2)}, u32[]{:S(2)}) collective-permute-start(bf16[8,64,256]{2,1,0:T(8,128)(2,1)S(1)} %shard_map.89.refs_3_), channel_id=1, source_target_pairs={{4,8},{6,10},{8,4},{10,6},{5,9},{7,11},{9,5},{11,7},{20,24},{22,26... | collective-permute-start | bytes 786440 | tf_op jit(solution)/shard_map/ppermute | solution.py:300
  51.3 17.5 %collective-permute-start.8 = (bf16[8,64,256]{2,1,0:T(8,128)(2,1)S(1)}, bf16[8,64,256]{2,1,0:T(8,128)(2,1)S(1)}, u32[]{:S(2)}, u32[]{:S(2)}) collective-permute-start(bf16[8,64,256]{2,1,0:T(8,128)(2,1)S(1)} %shard_map.85.refs_0_.refs_2_), channel_id=1, source_target_pairs={{0,4},{2,6},{4,0},{6,2},{8,12},{10,14},{12,8},{14,10},{1,5},{3,7},... | collective-permute-start | bytes 786440 | tf_op jit(solution)/shard_map/ppermute | solution.py:299
  55.8 14.3 %collective-permute-start.12 = (bf16[8,64,256]{2,1,0:T(8,128)(2,1)S(1)}, bf16[8,64,256]{2,1,0:T(8,128)(2,1)S(1)}, u32[]{:S(2)}, u32[]{:S(2)}) collective-permute-start(bf16[8,64,256]{2,1,0:T(8,128)(2,1)S(1)} %shard_map.84.refs_3_), channel_id=1, source_target_pairs={{4,8},{6,10},{8,4},{10,6},{5,9},{7,11},{9,5},{11,7},{20,24},{22,26... | collective-permute-start | bytes 786440 | tf_op jit(solution)/shard_map/ppermute | solution.py:300
  56.5 5.7 %collective-permute-start.10 = (bf16[6,64,256]{2,1,0:T(8,128)(2,1)S(1)}, bf16[6,64,256]{2,1,0:T(8,128)(2,1)S(1)}, u32[]{:S(2)}, u32[]{:S(2)}) collective-permute-start(bf16[6,64,256]{2,1,0:T(8,128)(2,1)S(1)} %get-tuple-element.18.refs_2_), channel_id=1, source_target_pairs={{0,2},{2,0},{4,6},{6,4},{8,10},{10,8},{12,14},{14,12},{1,3},{3,1},... | collective-permute-start | bytes 589832 | tf_op jit(solution)/shard_map/ppermute | solution.py:265
  57.2 15.2 %collective-permute-start.9 = (bf16[6,64,256]{2,1,0:T(8,128)(2,1)S(1)}, bf16[6,64,256]{2,1,0:T(8,128)(2,1)S(1)}, u32[]{:S(2)}, u32[]{:S(2)}) collective-permute-start(bf16[6,64,256]{2,1,0:T(8,128)(2,1)S(1)} %get-tuple-element.20), channel_id=1, source_target_pairs={{0,2},{2,0},{4,6},{6,4},{8,10},{10,8},{12,14},{14,12},{1,3},{3,1},... | collective-permute-start | bytes 589832 | tf_op jit(solution)/shard_map/ppermute | solution.py:265
  62.2 16.6 %collective-permute-start.18 = (bf16[8,64,256]{2,1,0:T(8,128)(2,1)S(1)}, bf16[8,64,256]{2,1,0:T(8,128)(2,1)S(1)}, u32[]{:S(2)}, u32[]{:S(2)}) collective-permute-start(bf16[8,64,256]{2,1,0:T(8,128)(2,1)S(1)} %shard_map.92.refs_3_), channel_id=1, source_target_pairs={{4,8},{6,10},{8,4},{10,6},{5,9},{7,11},{9,5},{11,7},{20,24},{22,26... | collective-permute-start | bytes 786440 | tf_op jit(solution)/shard_map/ppermute | solution.py:300
  64.2 14.6 %collective-permute-start.17 = (bf16[8,64,256]{2,1,0:T(8,128)(2,1)S(1)}, bf16[8,64,256]{2,1,0:T(8,128)(2,1)S(1)}, u32[]{:S(2)}, u32[]{:S(2)}) collective-permute-start(bf16[8,64,256]{2,1,0:T(8,128)(2,1)S(1)} %shard_map.94), channel_id=1, source_target_pairs={{0,4},{2,6},{4,0},{6,2},{8,12},{10,14},{12,8},{14,10},{1,5},{3,7},... | collective-permute-start | bytes 786440 | tf_op jit(solution)/shard_map/ppermute | solution.py:299
  69.4 9.5 %collective-permute-start.19 = (bf16[8,64,256]{2,1,0:T(8,128)(2,1)S(1)}, bf16[8,64,256]{2,1,0:T(8,128)(2,1)S(1)}, u32[]{:S(2)}, u32[]{:S(2)}) collective-permute-start(bf16[8,64,256]{2,1,0:T(8,128)(2,1)S(1)} %shard_map.86.refs_3_), channel_id=1, source_target_pairs={{4,8},{6,10},{8,4},{10,6},{5,9},{7,11},{9,5},{11,7},{20,24},{22,26... | collective-permute-start | bytes 786440 | tf_op jit(solution)/shard_map/ppermute | solution.py:300
  70.7 8.2 %collective-permute-start.13 = (bf16[8,64,256]{2,1,0:T(8,128)(2,1)S(1)}, bf16[8,64,256]{2,1,0:T(8,128)(2,1)S(1)}, u32[]{:S(2)}, u32[]{:S(2)}) collective-permute-start(bf16[8,64,256]{2,1,0:T(8,128)(2,1)S(1)} %shard_map.91), channel_id=1, source_target_pairs={{0,4},{2,6},{4,0},{6,2},{8,12},{10,14},{12,8},{14,10},{1,5},{3,7},... | collective-permute-start | bytes 786440 | tf_op jit(solution)/shard_map/ppermute | solution.py:299
  72.4 5.7 %collective-permute-start.2 = (bf16[6,64,256]{2,1,0:T(8,128)(2,1)S(1)}, bf16[6,64,256]{2,1,0:T(8,128)(2,1)S(1)}, u32[]{:S(2)}, u32[]{:S(2)}) collective-permute-start(bf16[6,64,256]{2,1,0:T(8,128)(2,1)S(1)} %get-tuple-element.17), channel_id=1, source_target_pairs={{0,2},{2,0},{4,6},{6,4},{8,10},{10,8},{12,14},{14,12},{1,3},{3,1},... | collective-permute-start | bytes 589832 | tf_op jit(solution)/shard_map/ppermute | solution.py:265
  74.6 4.3 %copy-start.4 = (s32[8]{0:T(128)S(1)}, s32[8]{0:T(128)}, u32[]{:S(2)}) copy-start(s32[8]{0:T(128)} %rows.1) | copy-start | bytes 100

commit v5 on v4

--- a/solution.py
+++ b/solution.py
@@ -159,96 +159,187 @@
         out_shape=jax.ShapeDtypeStruct((3 * (n // Y) * (1 + 2 * cap),), jnp.int32),
         in_specs=[SMEM],
         out_specs=SMEM,
+        compiler_params=pltpu.CompilerParams(vmem_limit_bytes=2**20),
         cost_estimate=pl.CostEstimate(flops=4000, bytes_accessed=4000, transcendentals=0),
     )(dest)
 
 
-def small_call(kernel, outs, table, ins, after=(), scratch=()):
-    spare = len(after)
-
-    def body(table, *refs):
-        kernel(table, *refs[:len(ins)], *refs[len(ins) + spare:])
+def small_call(kernel, outs, ins, table=None, after=(), scratch=(), cost=1000):
+    front = [] if table is None else [table]
+    used = len(front) + len(ins)
+
+    def body(*refs):
+        kernel(*refs[:used], *refs[used + len(after):])
 
     return pl.pallas_call(
         body,
         out_shape=outs,
-        in_specs=[SMEM] + [VMEM] * len(ins) + [pl.BlockSpec(memory_space=pl.ANY)] * spare,
+        in_specs=[SMEM] * len(front) + [VMEM] * len(ins) + [pl.BlockSpec(memory_space=pl.ANY)] * len(after),
         out_specs=[VMEM] * len(outs),
         scratch_shapes=scratch,
-        compiler_params=pltpu.CompilerParams(vmem_limit_bytes=16 * 2**20),
-        cost_estimate=pl.CostEstimate(flops=0, bytes_accessed=1000, transcendentals=0),
-    )(table, *ins, *after)
-
-
-def pack(cap, qs, table, keep, recv, after):
+        compiler_params=pltpu.CompilerParams(vmem_limit_bytes=8 * 2**20),
+        cost_estimate=pl.CostEstimate(flops=0, bytes_accessed=cost, transcendentals=0),
+    )(*front, *ins, *after)
+
+
+def ready(table):
+    def kernel(table, out):
+        out[...] = jnp.full(out.shape, table[0], jnp.int32)
+
+    return small_call(kernel, [jax.ShapeDtypeStruct((8, 128), jnp.int32)], (), table)
+
+
+def join(cap, table, keep, recv, after):
     _, size, blk = keep.shape
 
-    def kernel(table, keep, recv, *outs):
-        for q, out in zip(qs, outs):
+    def kernel(table, keep, recv, joined, out):
+        joined[...] = keep[...] + recv[...]
+        for slot in range(cap):
+            out[slot] = joined[table[table_at(cap, 0, SEND) + 1 + slot]]
+
+    return small_call(
+        kernel,
+        [keep, jax.ShapeDtypeStruct((cap, size, blk), jnp.bfloat16)],
+        (keep, recv),
+        table,
+        after,
+    )
+
+
+def pack(cap, spots, table, joined, after):
+    _, size, blk = joined[0].shape
+    used = sorted({i for _, i in spots})
+
+    def kernel(table, *refs):
+        out = refs[-1]
+        for at, (q, i) in enumerate(spots):
             for slot in range(cap):
-                j = table[table_at(cap, q, SEND) + 1 + slot]
-                out[slot] = keep[j] + recv[j]
-
-    return small_call(kernel, [jax.ShapeDtypeStruct((cap, size, blk), jnp.bfloat16)] * len(qs), table, (keep, recv), after)
-
-
-def gather(cap, q, n_s, table, keep, recv, crossed, after, dtype=jnp.bfloat16):
-    _, size, blk = keep.shape
-
-    def kernel(table, keep, recv, crossed, out, total):
-        total[...] = jnp.zeros_like(total)
-        at = table_at(cap, q, OWN) + 1
-        for slot in range(cap):
-            j = table[at + slot]
-            total[table[at + cap + slot]] += (keep[j] + recv[j]).astype(jnp.float32)
-        at = table_at(cap, q, CROSS) + 1
-        for slot in range(cap):
-            total[table[at + cap + slot]] += crossed[slot].astype(jnp.float32)
-        out[...] = total[:n_s].astype(dtype)
+                out[at * cap + slot] = refs[used.index(i)][table[table_at(cap, q, SEND) + 1 + slot]]
 
     (out,) = small_call(
         kernel,
-        [jax.ShapeDtypeStruct((n_s, size, blk), dtype)],
+        [jax.ShapeDtypeStruct((len(spots) * cap, size, blk), jnp.bfloat16)],
+        [joined[i] for i in used],
         table,
-        (keep, recv, crossed),
+        after,
+    )
+    return out
+
+
+def gather(cap, q, pieces, n_s, table, joined, crossed, after, dtype=jnp.bfloat16, cost=1000):
+    _, size, blk = joined[0].shape
+    count = len(pieces)
+    spots = [crossed[q, i] for i in pieces]
+
+    def kernel(table, *refs):
+        out, total = refs[-2:]
+        for k in range(count):
+            a, c = refs[k], refs[count + k]
+            total[...] = jnp.zeros_like(total)
+            at = table_at(cap, q, OWN) + 1
+            for slot in range(cap):
+                j = table[at + slot]
+                total[table[at + cap + slot]] += a[j].astype(jnp.float32)
+            at = table_at(cap, q, CROSS) + 1
+            for slot in range(cap):
+                total[table[at + cap + slot]] += c[spots[k][1] + slot].astype(jnp.float32)
+            out[k * n_s:(k + 1) * n_s] = total[:n_s].astype(dtype)
+
+    (out,) = small_call(
+        kernel,
+        [jax.ShapeDtypeStruct((count * n_s, size, blk), dtype)],
+        [joined[i] for i in pieces] + [x for x, _ in spots],
+        table,
         after,
         [pltpu.VMEM((n_s + 1, size, blk), jnp.float32)],
+        cost,
     )
     return out
 
 
-def plus(table, a, b, after):
-    def kernel(table, a, b, out):
-        out[...] = a[...] + b[...]
-
-    (out,) = small_call(kernel, [jax.ShapeDtypeStruct(a.shape, a.dtype)], table, (a, b), after)
-    return out
-
-
-def finish(rows, bases, arrived):
-    n_s, size, blk = bases[0].shape
-    pieces = len(bases)
-
-    def kernel(rows, *refs):
-        out = refs[-1]
-        line = lax.broadcasted_iota(jnp.int32, (size, blk), 0) + lax.axis_index("mpo") * (size * pieces)
-        for piece in range(pieces):
-            for p in range(n_s):
-                total = refs[piece][p]
-                for part in refs[pieces + piece:-1:pieces]:
-                    total += part[p].astype(jnp.float32)
-                total = jnp.where(line + piece * size < rows[p], total, 0.0)
-                out[p, piece * size:(piece + 1) * size] = total.astype(jnp.bfloat16)
-
-    flat = list(bases) + [x for parts in arrived for x in parts]
+def advance(cap, n_s, line, step, i, table, joined, crossed, acc, near_in, far_in, after):
+    size, blk = joined.shape[1:]
+    block = jax.ShapeDtypeStruct((n_s, size, blk), jnp.bfloat16)
+    sends = [(step - 1, far_in)] + ([(line - 1 - step, near_in)] if step > 1 else [])
+    fresh = sorted({q for q, _ in sends if q not in acc})
+    ins, at = [joined], {}
+    for q in fresh:
+        at[q] = len(ins)
+        ins.append(crossed[q, i][0])
+    for q, arrived in sends:
+        if q not in fresh:
+            at[q] = len(ins)
+            ins.append(acc[q])
+    came = []
+    for _, arrived in sends:
+        came.append(len(ins))
+        if arrived is not None:
+            ins.append(arrived)
+    saved = [q for q in fresh if step < max(q + 1, line - 1 - q) and step > 1]
+
+    def kernel(*refs):
+        if fresh:
+            table, refs = refs[0], refs[1:]
+        totals = refs[len(refs) - len(fresh):]
+        outs = refs[len(ins):]
+        for total, q in zip(totals, fresh):
+            total[...] = jnp.zeros_like(total)
+            spot = table_at(cap, q, OWN) + 1
+            for slot in range(cap):
+                total[table[spot + cap + slot]] += refs[0][table[spot + slot]].astype(jnp.float32)
+            spot = table_at(cap, q, CROSS) + 1
+            for slot in range(cap):
+                total[table[spot + cap + slot]] += refs[at[q]][crossed[q, i][1] + slot].astype(jnp.float32)
+        for k, (q, arrived) in enumerate(sends):
+            message = totals[fresh.index(q)][:n_s] if q in fresh else refs[at[q]][...].astype(jnp.float32)
+            if arrived is not None:
+                message += refs[came[k]][...].astype(jnp.float32)
+            outs[k][...] = message.astype(jnp.bfloat16)
+        for k, q in enumerate(saved):
+            outs[len(sends) + k][...] = totals[fresh.index(q)][:n_s].astype(jnp.bfloat16)
+
+    outs = small_call(
+        kernel,
+        [block] * (len(sends) + len(saved)),
+        ins,
+        table if fresh else None,
+        after,
+        [pltpu.VMEM((n_s + 1, size, blk), jnp.float32)] * len(fresh),
+    )
+    for q, x in zip(saved, outs[len(sends):]):
+        acc[q] = x
+    if step == 1:
+        acc[0] = outs[0]
+    return outs[:len(sends)]
+
+
+def finish(n_s, piece, rows, base, arrived, out=None):
+    size, blk = base.shape[1:]
+    half = blk // 2
+
+    def kernel(rows, base, *refs):
+        parts, (out, held, sem) = refs[:len(arrived)], refs[-3:]
+        line = lax.broadcasted_iota(jnp.int32, (size, blk), 0) + (lax.axis_index("mpo") * half + piece * size)
+        for p in range(n_s):
+            total = base[p]
+            for part in parts:
+                total += part[p].astype(jnp.float32)
+            held[p] = jnp.where(line < rows[p:p + 1], total, 0.0).astype(jnp.bfloat16)
+        leave = pltpu.make_async_copy(held, out.at[:, piece * size:(piece + 1) * size], sem)
+        leave.start()
+        leave.wait()
+
+    ins = [rows, base, *arrived]
     return pl.pallas_call(
         kernel,
-        out_shape=jax.ShapeDtypeStruct((n_s, size * pieces, blk), jnp.bfloat16),
-        in_specs=[SMEM] + [VMEM] * len(flat),
-        out_specs=VMEM,
-        compiler_params=pltpu.CompilerParams(vmem_limit_bytes=16 * 2**20),
+        out_shape=jax.ShapeDtypeStruct((n_s, half, blk), jnp.bfloat16),
+        in_specs=[VMEM] * len(ins) + ([HBM] if out is not None else []),
+        out_specs=HBM,
+        scratch_shapes=[pltpu.VMEM((n_s, size, blk), jnp.bfloat16), pltpu.SemaphoreType.DMA],
+        input_output_aliases={len(ins): 0} if out is not None else {},
+        compiler_params=pltpu.CompilerParams(vmem_limit_bytes=8 * 2**20),
         cost_estimate=pl.CostEstimate(flops=0, bytes_accessed=1000, transcendentals=0),
-    )(rows, *flat)
+    )(*ins, *([out] if out is not None else []))
 
 
 def body(psi, left_env, right_env, term_class, active, dest, sector_rows):
@@ -256,50 +347,50 @@
     line = n // Y
     classes, n_s = dest.shape
     cap = (classes * n_s + n - 1) // n + 1
-    pieces = range(2)
+    pieces = [0, 1]
     across = [(d, d ^ 1) for d in range(n)]
     near = [(z * Y + y, (z ^ 1) * Y + y) for z in range(line) for y in range(Y)]
     far = [(z * Y + y, (((z + 1) ^ 1) - 1) * Y + y) for z in range(1, line - 1) for y in range(Y)]
 
-    def cross(x):
-        return lax.ppermute(x, "sector", across)
-
     send, keep = shift_sums(psi, left_env, right_env, term_class, active, sector_rows, classes, len(pieces))
     recv = [lax.ppermute(x, "mpo", [(0, 1), (1, 0)]) for x in send]
     table = make_table(n, cap, dest)
-    last = ()
-    crossed = [[None] * len(pieces) for _ in range(line)]
-    for qs in ([0], [1], list(range(2, line))):
+
+    loads = [[(q, i)] for q in range(line - 1) for i in pieces]
+    loads.append([(line - 1, i) for i in pieces])
+    crossed, joined, came = {}, [], []
+    last = ready(table)
+    for k, spots in enumerate(loads):
+        if k < len(pieces):
+            whole, packed = join(cap, table, keep[k], recv[k], last)
+            joined.append(whole)
+        else:
+            packed = pack(cap, spots, table, joined, last)
+        last = [packed]
+        if k == 3:
+            firsts = packed
+        came.append(lax.ppermute(packed, "sector", across))
+        for at, spot in enumerate(spots):
+            crossed[spot] = (came[k], at * cap)
+        if k >= 3:
+            last = [packed, came[k - 2]]
+
+    acc = [{} for _ in pieces]
+    near_in, far_in = [None for _ in pieces], [None for _ in pieces]
+    last = [firsts]
+    for step in range(1, line):
         for i in pieces:
-            packed = pack(cap, qs, table, keep[i], recv[i], last)
-            last = (packed[0],)
-            for q, x in zip(qs, packed):
-                crossed[q][i] = cross(x)
-
-    acc = [[None] * len(pieces) for _ in range(line)]
-
-    def sums(q, i):
-        if acc[q][i] is None:
-            dtype = jnp.float32 if q == line - 1 else jnp.bfloat16
-            acc[q][i] = gather(cap, q, n_s, table, keep[i], recv[i], crossed[q][i], last, dtype)
-        return acc[q][i], (acc[q][i],)
-
-    near_in, far_in = [None] * len(pieces), [None] * len(pieces)
-    for step in range(1, line):
-        near_out, far_out = [None] * len(pieces), [None] * len(pieces)
-        for i in pieces:
-            near_out[i], last = sums(step - 1, i)
-            if far_in[i] is not None:
-                near_out[i] = plus(table, near_out[i], far_in[i], last)
-                last = (near_out[i],)
-            if step > 1:
-                base, last = sums(line - 1 - step, i)
-                far_out[i] = plus(table, base, near_in[i], last)
-                last = (far_out[i],)
-        near_in = [lax.ppermute(x, "sector", near) for x in near_out]
-        far_in = [None if x is None else lax.ppermute(x, "sector", far) for x in far_out]
-    bases = [sums(line - 1, i)[0] for i in pieces]
-    return finish(sector_rows, bases, [x for x in (near_in, far_in) if x[0] is not None])
+            out = advance(cap, n_s, line, step, i, table, joined[i], crossed, acc[i], near_in[i], far_in[i], last)
+            last = [out[0]]
+            near_in[i] = lax.ppermute(out[0], "sector", near)
+            far_in[i] = lax.ppermute(out[1], "sector", far) if step > 1 else None
+    limits = jnp.broadcast_to(sector_rows[:, None], (n_s, psi.shape[2]))
+    out = None
+    for i in pieces:
+        base = gather(cap, line - 1, [i], n_s, table, joined, crossed, (), jnp.float32)
+        arrived = [x[i] for x in (near_in, far_in) if x[i] is not None]
+        out = finish(n_s, i, limits, base, arrived, out)
+    return out
 
 
 def solution(mesh):

time: 81 us -> 67.4 us (0.83)
  Pallas kernels: 36.5 us -> 27.7 us
  starting transfers between devices: 28.1 us -> 26.2 us
  local copies, waits for them, and re-layouts: 1.77 us -> 0.09 us
  waiting for transfers between devices: 10.9 us -> 9.63 us
    pallas_call x21 -> x18, Pallas kernels: 19.7 us -> 12.5 us  [the longest x16 10.8 us: small_call(): pl.pallas_call(body, out_shape=outs, in_specs=[SMEM] * len(front) + [VMEM...]
    ppermute x18 -> x17, starting transfers between devices: 27.6 us -> 25.7 us  [the longest x6 13.9 us: body(): near_in[i] = lax.ppermute(out[0], 'sector', near)]
    unnamed x10 -> x8, local copies, waits for them, and re-layouts: 1.77 us -> 0.02 us
    pallas_call x1, Pallas kernels: 13.9 us -> 12.4 us  [shift_sums(): pl.pallas_call(shifts_kernel, out_shape=[jax.ShapeDtypeStruct((classes, n...]
    ppermute x2, waiting for transfers between devices: 1.35 us -> 0.01 us  [body(): recv = [lax.ppermute(x, 'mpo', [(0, 1), (1, 0)]) for x in send]]
    ppermute x18 -> x17, waiting for transfers between devices: 9.56 us -> 9.63 us  [the longest x7 8.24 us: body(): came.append(lax.ppermute(packed, 'sector', across))]
  transfers between devices with their start and end apart: 20 -> 19, of which waited for: 7 -> 4; matrix products, arithmetic and copies ran while one was open for 0% -> 0% of each run, Pallas kernels for 26% -> 22%
where the time goes in v5:
time: 67.4 us; the launch traced here: 66.2 us
  Pallas kernels  27.7 us (41%)
  starting transfers between devices  26.2 us (39%)
  waiting for transfers between devices  9.63 us (14%)
  other arithmetic  2.25 us (3%)
    ppermute x6, starting transfers between devices, body(): near_in[i] = lax.ppermute(out[0], 'sector', near)  13.9 us
    pallas_call x1, Pallas kernels, shift_sums(): pl.pallas_call(shifts_kernel, out_shape=[jax.ShapeDtypeStruct((classes, n...  12.4 us
    pallas_call x16, Pallas kernels, small_call(): pl.pallas_call(body, out_shape=outs, in_specs=[SMEM] * len(front) + [VMEM...  10.8 us
    ppermute x7, starting transfers between devices, body(): came.append(lax.ppermute(packed, 'sector', across))  9.04 us
    ppermute x7, waiting for transfers between devices, body(): came.append(lax.ppermute(packed, 'sector', across))  8.24 us
    pallas_call x1, Pallas kernels, make_table(): pl.pallas_call(functools.partial(table_kernel, n, cap), out_shape=jax.Sha...  2.84 us
    ppermute x4, starting transfers between devices, body(): far_in[i] = lax.ppermute(out[1], 'sector', far) if step > 1 else None  2.69 us
    pallas_call x2, Pallas kernels, finish(): pl.pallas_call(kernel, out_shape=jax.ShapeDtypeStruct((n_s, half, blk), j...  1.65 us
  transfers between devices with their start and end apart: 19, of which 4 were waited for; matrix products, arithmetic and copies ran while one was open for 0% of the time, Pallas kernels for 22%

profile of v5, /device:TPU:0, one launch (start us, length us, event | category | flops | bytes accessed | tf_op | source)
XLA Modules:
  0.0 66.2 jit_solution(7569551745531680477)
XLA Ops:
  0.0 0.8 %iota_compare_fusion = pred[8,256]{1,0:T(8,128)(4,1)S(1)} fusion(s32[8]{0:T(128)} %param.13), kind=kLoop, calls=%fused_computation.1 | loop fusion | flops 2048 | bytes 2080 | tf_op jit(solution)/shard_map/lt | solution.py:84
  0.8 1.5 %broadcast_select_fusion.masked = bf16[8,256,256]{2,1,0:T(8,128)(2,1)S(1)} fusion(bf16[8,256,256]{2,1,0:T(8,128)(2,1)} %param.7, pred[8,256]{1,0:T(8,128)(4,1)S(1)} %iota_compare_fusion), kind=kLoop, calls=%fused_computation | loop fusion | flops 524288 | bytes 2099200 | tf_op jit(solution)/shard_map/jit(_where)/select_n | solution.py:84
  2.3 0.0 copy-done.3
  2.3 0.0 copy-start
  2.3 12.4 %shard_map.74 = (bf16[5,8,64,256]{3,2,1,0:T(8,128)(2,1)S(1)}, bf16[5,8,64,256]{3,2,1,0:T(8,128)(2,1)S(1)}, bf16[5,8,64,256]{3,2,1,0:T(8,128)(2,1)S(1)}, bf16[5,8,64,256]{3,2,1,0:T(8,128)(2,1)S(1)}) custom-call(s32[8,13]{1,0:T(8,128)S(1)} %select_bitcast_fusion.slots, bf16[8,256,256]{2,1,0:T(8,128)(2,1)S(1)} %broadcast_select_fusion.masked, ...), custom_call_target="tpu_custom_call" | custom-call | flops 6979321856 | bytes 27262976 | tf_op jit(solution)/shard_map/pallas_call | solution.py:86
  14.7 0.5 collective-permute-start.1
  15.2 0.1 collective-permute-start
  15.3 2.8 %shard_map.73.refs_0_ = s32[156]{0:T(256)S(1)} custom-call(s32[5,8]{1,0:T(8,128)S(1)} %copy-done), custom_call_target="tpu_custom_call" | custom-call | flops 4000 | bytes 4000 | tf_op jit(solution)/shard_map/pallas_call | solution.py:157
  18.1 0.6 shard_map.75.refs_3_
  18.7 0.0 collective-permute-done.1.refs_2_
  18.7 0.7 %shard_map.76 = (bf16[40,64,256]{2,1,0:T(8,128)(2,1)S(1)}, bf16[6,64,256]{2,1,0:T(8,128)(2,1)S(1)}) custom-call(s32[156]{0:T(256)S(1)} %shard_map.73.refs_0_, bf16[40,64,256]{2,1,0:T(8,128)(2,1)S(1)} %bitcast.7, bf16[40,64,256]{2,1,0:T(8,128)(2,1)S(1)} %collective-permute-done.1.refs_2_, s32[8,128]{1,0:T(8,128)S(1)} %shard_map.75.refs_3_), custom_call_target="tpu_custom_call" | custom-call | bytes 1000 | tf_op jit(solution)/shard_map/pallas_call | solution.py:174
  19.4 3.0 %collective-permute-start.7 = (bf16[6,64,256]{2,1,0:T(8,128)(2,1)S(1)}, bf16[6,64,256]{2,1,0:T(8,128)(2,1)S(1)}, u32[]{:S(2)}, u32[]{:S(2)}) collective-permute-start(bf16[6,64,256]{2,1,0:T(8,128)(2,1)S(1)} %get-tuple-element.25.refs_3_), channel_id=1, source_target_pairs={{0,2},{2,0},{4,6},{6,4},{8,10},{10,8},{12,14},{14,12},{1,3},{3,1},... | collective-permute-start | bytes 589832 | tf_op jit(solution)/shard_map/ppermute | solution.py:372
  22.5 0.0 collective-permute-done.refs_2_
  22.5 0.7 %shard_map.77 = (bf16[40,64,256]{2,1,0:T(8,128)(2,1)S(1)}, bf16[6,64,256]{2,1,0:T(8,128)(2,1)S(1)}) custom-call(s32[156]{0:T(256)S(1)} %shard_map.73.refs_0_, bf16[40,64,256]{2,1,0:T(8,128)(2,1)S(1)} %bitcast.6, bf16[40,64,256]{2,1,0:T(8,128)(2,1)S(1)} %collective-permute-done.refs_2_, bf16[6,64,256]{2,1,0:T(8,128)(2,1)S(1)} %get-tuple-element.25.refs_3_), custom_call_target="tpu_custom_call" | custom-call | bytes 1000 | tf_op jit(solution)/shard_map/pallas_call | solution.py:174
  23.2 0.2 collective-permute-start.2
  23.4 0.6 shard_map.78.refs_2_
  24.0 0.6 shard_map.79.refs_2_.refs_3_
  24.6 3.6 %collective-permute-done.7.refs_2_ = bf16[6,64,256]{2,1,0:T(8,128)(2,1)S(1)} collective-permute-done((bf16[6,64,256]{2,1,0:T(8,128)(2,1)S(1)}, bf16[6,64,256]{2,1,0:T(8,128)(2,1)S(1)}, u32[]{:S(2)}, u32[]{:S(2)}) %collective-permute-start.7) | collective-permute-done | bytes 196640 | tf_op jit(solution)/shard_map/ppermute | solution.py:372
  28.2 0.7 %shard_map.84.refs_3_ = bf16[8,64,256]{2,1,0:T(8,128)(2,1)S(1)} custom-call(s32[156]{0:T(256)S(1)} %shard_map.73.refs_0_, bf16[40,64,256]{2,1,0:T(8,128)(2,1)S(1)} %get-tuple-element.27.refs_1_, bf16[6,64,256]{2,1,0:T(8,128)(2,1)S(1)} %collective-permute-done.7.refs_2_, bf16[6,64,256]{2,1,0:T(8,128)(2,1)S(1)} %shard_map.79.refs_2_.refs_3_), custom_call_target="tpu_custom_call" | custom-call | bytes 1000 | tf_op jit(solution)/shard_map/pallas_call | solution.py:174
  28.9 2.2 %collective-permute-start.9 = (bf16[8,64,256]{2,1,0:T(8,128)(2,1)S(1)}, bf16[8,64,256]{2,1,0:T(8,128)(2,1)S(1)}, u32[]{:S(2)}, u32[]{:S(2)}) collective-permute-start(bf16[8,64,256]{2,1,0:T(8,128)(2,1)S(1)} %shard_map.84.refs_3_), channel_id=1, source_target_pairs={{0,4},{2,6},{4,0},{6,2},{8,12},{10,14},{12,8},{14,10},{1,5},{3,7},... | collective-permute-start | bytes 786440 | tf_op jit(solution)/shard_map/ppermute | solution.py:385
  31.1 1.5 %collective-permute-start.3 = (bf16[6,64,256]{2,1,0:T(8,128)(2,1)S(1)}, bf16[6,64,256]{2,1,0:T(8,128)(2,1)S(1)}, u32[]{:S(2)}, u32[]{:S(2)}) collective-permute-start(bf16[6,64,256]{2,1,0:T(8,128)(2,1)S(1)} %shard_map.78.refs_2_), channel_id=1, source_target_pairs={{0,2},{2,0},{4,6},{6,4},{8,10},{10,8},{12,14},{14,12},{1,3},{3,1},... | collective-permute-start | bytes 589832 | tf_op jit(solution)/shard_map/ppermute | solution.py:372
  32.6 0.0 collective-permute-done.2.refs_3_.refs_2_
  32.6 0.7 %shard_map.85.refs_4_.refs_3_ = bf16[8,64,256]{2,1,0:T(8,128)(2,1)S(1)} custom-call(s32[156]{0:T(256)S(1)} %shard_map.73.refs_0_, bf16[40,64,256]{2,1,0:T(8,128)(2,1)S(1)} %get-tuple-element.26.refs_1_.refs_2_, bf16[6,64,256]{2,1,0:T(8,128)(2,1)S(1)} %collective-permute-done.2.refs_3_.refs_2_, bf16[8,64,256]{2,1,0:T(8,128)(2,1)S(1)} %shard_map.84.refs_3_), custom_call_target="tpu_custom_call" | custom-call | bytes 1000 | tf_op jit(solution)/shard_map/pallas_call | solution.py:174
  33.3 2.0 %collective-permute-start.8 = (bf16[8,64,256]{2,1,0:T(8,128)(2,1)S(1)}, bf16[8,64,256]{2,1,0:T(8,128)(2,1)S(1)}, u32[]{:S(2)}, u32[]{:S(2)}) collective-permute-start(bf16[8,64,256]{2,1,0:T(8,128)(2,1)S(1)} %shard_map.85.refs_4_.refs_3_), channel_id=1, source_target_pairs={{0,4},{2,6},{4,0},{6,2},{8,12},{10,14},{12,8},{14,10},{1,5},{3,7},... | collective-permute-start | bytes 786440 | tf_op jit(solution)/shard_map/ppermute | solution.py:385
  35.3 1.5 %collective-permute-start.4 = (bf16[6,64,256]{2,1,0:T(8,128)(2,1)S(1)}, bf16[6,64,256]{2,1,0:T(8,128)(2,1)S(1)}, u32[]{:S(2)}, u32[]{:S(2)}) collective-permute-start(bf16[6,64,256]{2,1,0:T(8,128)(2,1)S(1)} %shard_map.79.refs_2_.refs_3_), channel_id=1, source_target_pairs={{0,2},{2,0},{4,6},{6,4},{8,10},{10,8},{12,14},{14,12},{1,3},{3,1},... | collective-permute-start | bytes 589832 | tf_op jit(solution)/shard_map/ppermute | solution.py:372
  36.8 0.6 shard_map.80.refs_2_
  37.4 0.6 collective-permute-start.12
  37.9 0.0 collective-permute-done.3.refs_3_.refs_2_
  37.9 0.0 collective-permute-done.9.refs_3_
  37.9 0.8 %shard_map.86 = (bf16[8,64,256]{2,1,0:T(8,128)(2,1)S(1)}, bf16[8,64,256]{2,1,0:T(8,128)(2,1)S(1)}) custom-call(s32[156]{0:T(256)S(1)} %shard_map.73.refs_0_, bf16[40,64,256]{2,1,0:T(8,128)(2,1)S(1)} %get-tuple-element.27.refs_1_, bf16[6,64,256]{2,1,0:T(8,128)(2,1)S(1)} %collective-permute-done.3.refs_3_.refs_2_, ...), custom_call_target="tpu_custom_call" | custom-call | bytes 1000 | tf_op jit(solution)/shard_map/pallas_call | solution.py:174
  38.7 0.7 %collective-permute-start.13 = (bf16[8,64,256]{2,1,0:T(8,128)(2,1)S(1)}, bf16[8,64,256]{2,1,0:T(8,128)(2,1)S(1)}, u32[]{:S(2)}, u32[]{:S(2)}) collective-permute-start(bf16[8,64,256]{2,1,0:T(8,128)(2,1)S(1)} %get-tuple-element.32), channel_id=1, source_target_pairs={{4,8},{6,10},{8,4},{10,6},{5,9},{7,11},{9,5},{11,7},{20,24},{22,26... | collective-permute-start | bytes 786440 | tf_op jit(solution)/shard_map/ppermute | solution.py:386
  39.4 4.5 %collective-permute-start.14 = (bf16[8,64,256]{2,1,0:T(8,128)(2,1)S(1)}, bf16[8,64,256]{2,1,0:T(8,128)(2,1)S(1)}, u32[]{:S(2)}, u32[]{:S(2)}) collective-permute-start(bf16[8,64,256]{2,1,0:T(8,128)(2,1)S(1)} %get-tuple-element.29.refs_4_), channel_id=1, source_target_pairs={{0,4},{2,6},{4,0},{6,2},{8,12},{10,14},{12,8},{14,10},{1,5},{3,7},... | collective-permute-start | bytes 786440 | tf_op jit(solution)/shard_map/ppermute | solution.py:385
  43.8 0.0 collective-permute-done.4.refs_4_.refs_2_
  43.8 0.0 collective-permute-done.8.refs_3_
  43.9 0.8 %shard_map.87 = (bf16[8,64,256]{2,1,0:T(8,128)(2,1)S(1)}, bf16[8,64,256]{2,1,0:T(8,128)(2,1)S(1)}) custom-call(s32[156]{0:T(256)S(1)} %shard_map.73.refs_0_, bf16[40,64,256]{2,1,0:T(8,128)(2,1)S(1)} %get-tuple-element.26.refs_1_.refs_2_, bf16[6,64,256]{2,1,0:T(8,128)(2,1)S(1)} %collective-permute-done.4.refs_4_.refs_2_, ...), custom_call_target="tpu_custom_call" | custom-call | bytes 1000 | tf_op jit(solution)/shard_map/pallas_call | solution.py:174
  44.6 0.7 %collective-permute-start.10 = (bf16[8,64,256]{2,1,0:T(8,128)(2,1)S(1)}, bf16[8,64,256]{2,1,0:T(8,128)(2,1)S(1)}, u32[]{:S(2)}, u32[]{:S(2)}) collective-permute-start(bf16[8,64,256]{2,1,0:T(8,128)(2,1)S(1)} %get-tuple-element.30), channel_id=1, source_target_pairs={{4,8},{6,10},{8,4},{10,6},{5,9},{7,11},{9,5},{11,7},{20,24},{22,26... | collective-permute-start | bytes 786440 | tf_op jit(solution)/shard_map/ppermute | solution.py:386
  45.3 3.7 %collective-permute-start.11 = (bf16[8,64,256]{2,1,0:T(8,128)(2,1)S(1)}, bf16[8,64,256]{2,1,0:T(8,128)(2,1)S(1)}, u32[]{:S(2)}, u32[]{:S(2)}) collective-permute-start(bf16[8,64,256]{2,1,0:T(8,128)(2,1)S(1)} %get-tuple-element.31.refs_6_), channel_id=1, source_target_pairs={{0,4},{2,6},{4,0},{6,2},{8,12},{10,14},{12,8},{14,10},{1,5},{3,7},... | collective-permute-start | bytes 786440 | tf_op jit(solution)/shard_map/ppermute | solution.py:385
  49.0 0.6 shard_map.81.refs_3_
  49.5 0.0 collective-permute-done.12.refs_2_
  49.5 1.6 %collective-permute-start.6 = (bf16[6,64,256]{2,1,0:T(8,128)(2,1)S(1)}, bf16[6,64,256]{2,1,0:T(8,128)(2,1)S(1)}, u32[]{:S(2)}, u32[]{:S(2)}) collective-permute-start(bf16[6,64,256]{2,1,0:T(8,128)(2,1)S(1)} %shard_map.81.refs_3_), channel_id=1, source_target_pairs={{0,2},{2,0},{4,6},{6,4},{8,10},{10,8},{12,14},{14,12},{1,3},{3,1},... | collective-permute-start | bytes 589832 | tf_op jit(solution)/shard_map/ppermute | solution.py:372
  51.1 0.6 shard_map.82
  51.7 0.0 collective-permute-done.13.refs_4_
  51.7 0.6 collective-permute-start.5
  52.3 0.0 collective-permute-done.14.refs_5_
  52.3 0.8 %shard_map.88 = (bf16[8,64,256]{2,1,0:T(8,128)(2,1)S(1)}, bf16[8,64,256]{2,1,0:T(8,128)(2,1)S(1)}) custom-call(s32[156]{0:T(256)S(1)} %shard_map.73.refs_0_, bf16[40,64,256]{2,1,0:T(8,128)(2,1)S(1)} %get-tuple-element.27.refs_1_, bf16[6,64,256]{2,1,0:T(8,128)(2,1)S(1)} %collective-permute-done.12.refs_2_, bf16[8,64,256]{2,1,0:T(8,128)(2,1)S(1)} %shard_map.84.refs_3_, ...), custom_call_target="tpu_custom_call" | custom-call | bytes 1000 | tf_op jit(solution)/shard_map/pallas_call | solution.py:174
  53.1 0.1 collective-permute-start.17
  53.2 4.2 %collective-permute-done.6.refs_2_ = bf16[6,64,256]{2,1,0:T(8,128)(2,1)S(1)} collective-permute-done((bf16[6,64,256]{2,1,0:T(8,128)(2,1)S(1)}, bf16[6,64,256]{2,1,0:T(8,128)(2,1)S(1)}, u32[]{:S(2)}, u32[]{:S(2)}) %collective-permute-start.6) | collective-permute-done | bytes 196640 | tf_op jit(solution)/shard_map/ppermute | solution.py:372
  57.4 0.7 %collective-permute-start.18 = (bf16[8,64,256]{2,1,0:T(8,128)(2,1)S(1)}, bf16[8,64,256]{2,1,0:T(8,128)(2,1)S(1)}, u32[]{:S(2)}, u32[]{:S(2)}) collective-permute-start(bf16[8,64,256]{2,1,0:T(8,128)(2,1)S(1)} %get-tuple-element.36), channel_id=1, source_target_pairs={{4,8},{6,10},{8,4},{10,6},{5,9},{7,11},{9,5},{11,7},{20,24},{22,26... | collective-permute-start | bytes 786440 | tf_op jit(solution)/shard_map/ppermute | solution.py:386
  58.1 0.0 collective-permute-done.10.refs_4_
  58.1 0.0 collective-permute-done.11.refs_5_
  58.1 0.8 %shard_map.89 = (bf16[8,64,256]{2,1,0:T(8,128)(2,1)S(1)}, bf16[8,64,256]{2,1,0:T(8,128)(2,1)S(1)}) custom-call(s32[156]{0:T(256)S(1)} %shard_map.73.refs_0_, bf16[40,64,256]{2,1,0:T(8,128)(2,1)S(1)} %get-tuple-element.26.refs_1_.refs_2_, bf16[6,64,256]{2,1,0:T(8,128)(2,1)S(1)} %collective-permute-done.6.refs_2_, ...), custom_call_target="tpu_custom_call" | custom-call | bytes 1000 | tf_op jit(solution)/shard_map/pallas_call | solution.py:174
  59.0 1.6 %collective-permute-start.15 = (bf16[8,64,256]{2,1,0:T(8,128)(2,1)S(1)}, bf16[8,64,256]{2,1,0:T(8,128)(2,1)S(1)}, u32[]{:S(2)}, u32[]{:S(2)}) collective-permute-start(bf16[8,64,256]{2,1,0:T(8,128)(2,1)S(1)} %get-tuple-element.34), channel_id=1, source_target_pairs={{0,4},{2,6},{4,0},{6,2},{8,12},{10,14},{12,8},{14,10},{1,5},{3,7},... | collective-permute-start | bytes 786440 | tf_op jit(solution)/shard_map/ppermute | solution.py:385
  60.6 0.7 %collective-permute-start.16 = (bf16[8,64,256]{2,1,0:T(8,128)(2,1)S(1)}, bf16[8,64,256]{2,1,0:T(8,128)(2,1)S(1)}, u32[]{:S(2)}, u32[]{:S(2)}) collective-permute-start(bf16[8,64,256]{2,1,0:T(8,128)(2,1)S(1)} %get-tuple-element.35), channel_id=1, source_target_pairs={{4,8},{6,10},{8,4},{10,6},{5,9},{7,11},{9,5},{11,7},{20,24},{22,26... | collective-permute-start | bytes 786440 | tf_op jit(solution)/shard_map/ppermute | solution.py:386
  61.3 0.4 collective-permute-done.5.refs_2_
  61.7 0.7 %shard_map.90.base = f32[8,64,256]{2,1,0:T(8,128)S(1)} custom-call(s32[156]{0:T(256)S(1)} %shard_map.73.refs_0_, bf16[40,64,256]{2,1,0:T(8,128)(2,1)S(1)} %get-tuple-element.27.refs_1_, bf16[12,64,256]{2,1,0:T(8,128)(2,1)S(1)} %collective-permute-done.5.refs_2_), custom_call_target="tpu_custom_call" | custom-call | bytes 1000 | tf_op jit(solution)/shard_map/pallas_call | solution.py:174
  62.4 0.0 copy-start.2
  62.4 0.7 %shard_map.83.base = f32[8,64,256]{2,1,0:T(8,128)S(1)} custom-call(s32[156]{0:T(256)S(1)} %shard_map.73.refs_0_, bf16[40,64,256]{2,1,0:T(8,128)(2,1)S(1)} %get-tuple-element.26.refs_1_.refs_2_, bf16[12,64,256]{2,1,0:T(8,128)(2,1)S(1)} %collective-permute-done.5.refs_2_), custom_call_target="tpu_custom_call" | custom-call | bytes 1000 | tf_op jit(solution)/shard_map/pallas_call | solution.py:174
  63.1 0.0 collective-permute-done.17.refs_0_
  63.1 0.0 collective-permute-done.18.refs_1_
  63.2 0.1 broadcast_in_dim.32.rows
  63.2 0.8 %shard_map.91.refs_2_ = bf16[8,128,256]{2,1,0:T(8,128)(2,1)} custom-call(s32[8,256]{1,0:T(8,128)S(1)} %broadcast_in_dim.32.rows, f32[8,64,256]{2,1,0:T(8,128)S(1)} %shard_map.90.base, bf16[8,64,256]{2,1,0:T(8,128)(2,1)S(1)} %collective-permute-done.17.refs_0_, bf16[8,64,256]{2,1,0:T(8,128)(2,1)S(1)} %collective-permute-done.18.refs_1_), custom_call_target="tpu_custom_call" | custom-call | bytes 1000 | tf_op jit(solution)/shard_map/pallas_call | solution.py:333
  64.1 1.4 %collective-permute-done.15.refs_0_ = bf16[8,64,256]{2,1,0:T(8,128)(2,1)S(1)} collective-permute-done((bf16[8,64,256]{2,1,0:T(8,128)(2,1)S(1)}, bf16[8,64,256]{2,1,0:T(8,128)(2,1)S(1)}, u32[]{:S(2)}, u32[]{:S(2)}) %collective-permute-start.15) | collective-permute-done | bytes 262176 | tf_op jit(solution)/shard_map/ppermute | solution.py:385
  65.4 0.0 collective-permute-done.16.refs_1_
  65.4 0.8 %shard_map.92 = bf16[8,128,256]{2,1,0:T(8,128)(2,1)} custom-call(s32[8,256]{1,0:T(8,128)S(1)} %broadcast_in_dim.32.rows, f32[8,64,256]{2,1,0:T(8,128)S(1)} %shard_map.83.base, bf16[8,64,256]{2,1,0:T(8,128)(2,1)S(1)} %collective-permute-done.15.refs_0_, bf16[8,64,256]{2,1,0:T(8,128)(2,1)S(1)} %collective-permute-done.16.refs_1_, ...), custom_call_target="tpu_custom_call", output_to_operand_aliasing={{}: (4, {})} | custom-call | bytes 1000 | tf_op jit(solution)/shard_map/pallas_call | solution.py:333
  (6 shorter events, 0.0 us)
Async XLA Ops:
  0.0 2.3 %copy-start.3 = (s32[13]{0:T(128)S(1)}, s32[13]{0:T(128)}, u32[]{:S(2)}) copy-start(s32[13]{0:T(128)} %param.10) | copy-start | bytes 160
  0.0 2.3 %copy-start.1 = (s32[13,8]{0,1:T(8,128)S(1)}, s32[13,8]{0,1:T(8,128)}, u32[]{:S(2)}) copy-start(s32[13,8]{0,1:T(8,128)} %param.11) | copy-start | bytes 1252
  2.3 13.0 %copy-start = (s32[5,8]{1,0:T(8,128)S(1)}, s32[5,8]{1,0:T(8,128)}, u32[]{:S(2)}) copy-start(s32[5,8]{1,0:T(8,128)} %dest.1) | copy-start | bytes 484
  14.7 4.0 %collective-permute-start.1 = (bf16[40,64,256]{2,1,0:T(8,128)(2,1)S(1)}, bf16[40,64,256]{2,1,0:T(8,128)(2,1)S(1)}, u32[]{:S(2)}, u32[]{:S(2)}) collective-permute-start(bf16[40,64,256]{2,1,0:T(8,128)(2,1)S(1)} %bitcast.9), channel_id=1, source_target_pairs={{0,1},{1,0},{2,3},{3,2},{4,5},{5,4},{6,7},{7,6},{8,9},{9,8},{10,11... | collective-permute-start | bytes 3932168 | tf_op jit(solution)/shard_map/ppermute | solution.py:356
  15.2 7.3 %collective-permute-start = (bf16[40,64,256]{2,1,0:T(8,128)(2,1)S(1)}, bf16[40,64,256]{2,1,0:T(8,128)(2,1)S(1)}, u32[]{:S(2)}, u32[]{:S(2)}) collective-permute-start(bf16[40,64,256]{2,1,0:T(8,128)(2,1)S(1)} %bitcast.8), channel_id=1, source_target_pairs={{0,1},{1,0},{2,3},{3,2},{4,5},{5,4},{6,7},{7,6},{8,9},{9,8},{10,11... | collective-permute-start | bytes 3932168 | tf_op jit(solution)/shard_map/ppermute | solution.py:356
  19.4 8.7 %collective-permute-start.7 = (bf16[6,64,256]{2,1,0:T(8,128)(2,1)S(1)}, bf16[6,64,256]{2,1,0:T(8,128)(2,1)S(1)}, u32[]{:S(2)}, u32[]{:S(2)}) collective-permute-start(bf16[6,64,256]{2,1,0:T(8,128)(2,1)S(1)} %get-tuple-element.25.refs_3_), channel_id=1, source_target_pairs={{0,2},{2,0},{4,6},{6,4},{8,10},{10,8},{12,14},{14,12},{1,3},{3,1},... | collective-permute-start | bytes 589832 | tf_op jit(solution)/shard_map/ppermute | solution.py:372
  23.2 9.4 %collective-permute-start.2 = (bf16[6,64,256]{2,1,0:T(8,128)(2,1)S(1)}, bf16[6,64,256]{2,1,0:T(8,128)(2,1)S(1)}, u32[]{:S(2)}, u32[]{:S(2)}) collective-permute-start(bf16[6,64,256]{2,1,0:T(8,128)(2,1)S(1)} %get-tuple-element.28.refs_2_), channel_id=1, source_target_pairs={{0,2},{2,0},{4,6},{6,4},{8,10},{10,8},{12,14},{14,12},{1,3},{3,1},... | collective-permute-start | bytes 589832 | tf_op jit(solution)/shard_map/ppermute | solution.py:372
  28.9 9.0 %collective-permute-start.9 = (bf16[8,64,256]{2,1,0:T(8,128)(2,1)S(1)}, bf16[8,64,256]{2,1,0:T(8,128)(2,1)S(1)}, u32[]{:S(2)}, u32[]{:S(2)}) collective-permute-start(bf16[8,64,256]{2,1,0:T(8,128)(2,1)S(1)} %shard_map.84.refs_3_), channel_id=1, source_target_pairs={{0,4},{2,6},{4,0},{6,2},{8,12},{10,14},{12,8},{14,10},{1,5},{3,7},... | collective-permute-start | bytes 786440 | tf_op jit(solution)/shard_map/ppermute | solution.py:385
  31.1 6.9 %collective-permute-start.3 = (bf16[6,64,256]{2,1,0:T(8,128)(2,1)S(1)}, bf16[6,64,256]{2,1,0:T(8,128)(2,1)S(1)}, u32[]{:S(2)}, u32[]{:S(2)}) collective-permute-start(bf16[6,64,256]{2,1,0:T(8,128)(2,1)S(1)} %shard_map.78.refs_2_), channel_id=1, source_target_pairs={{0,2},{2,0},{4,6},{6,4},{8,10},{10,8},{12,14},{14,12},{1,3},{3,1},... | collective-permute-start | bytes 589832 | tf_op jit(solution)/shard_map/ppermute | solution.py:372
  33.3 10.6 %collective-permute-start.8 = (bf16[8,64,256]{2,1,0:T(8,128)(2,1)S(1)}, bf16[8,64,256]{2,1,0:T(8,128)(2,1)S(1)}, u32[]{:S(2)}, u32[]{:S(2)}) collective-permute-start(bf16[8,64,256]{2,1,0:T(8,128)(2,1)S(1)} %shard_map.85.refs_4_.refs_3_), channel_id=1, source_target_pairs={{0,4},{2,6},{4,0},{6,2},{8,12},{10,14},{12,8},{14,10},{1,5},{3,7},... | collective-permute-start | bytes 786440 | tf_op jit(solution)/shard_map/ppermute | solution.py:385
  35.3 8.6 %collective-permute-start.4 = (bf16[6,64,256]{2,1,0:T(8,128)(2,1)S(1)}, bf16[6,64,256]{2,1,0:T(8,128)(2,1)S(1)}, u32[]{:S(2)}, u32[]{:S(2)}) collective-permute-start(bf16[6,64,256]{2,1,0:T(8,128)(2,1)S(1)} %shard_map.79.refs_2_.refs_3_), channel_id=1, source_target_pairs={{0,2},{2,0},{4,6},{6,4},{8,10},{10,8},{12,14},{14,12},{1,3},{3,1},... | collective-permute-start | bytes 589832 | tf_op jit(solution)/shard_map/ppermute | solution.py:372
  37.4 12.2 %collective-permute-start.12 = (bf16[6,64,256]{2,1,0:T(8,128)(2,1)S(1)}, bf16[6,64,256]{2,1,0:T(8,128)(2,1)S(1)}, u32[]{:S(2)}, u32[]{:S(2)}) collective-permute-start(bf16[6,64,256]{2,1,0:T(8,128)(2,1)S(1)} %shard_map.80.refs_2_), channel_id=1, source_target_pairs={{0,2},{2,0},{4,6},{6,4},{8,10},{10,8},{12,14},{14,12},{1,3},{3,1},... | collective-permute-start | bytes 589832 | tf_op jit(solution)/shard_map/ppermute | solution.py:372
  38.7 13.0 %collective-permute-start.13 = (bf16[8,64,256]{2,1,0:T(8,128)(2,1)S(1)}, bf16[8,64,256]{2,1,0:T(8,128)(2,1)S(1)}, u32[]{:S(2)}, u32[]{:S(2)}) collective-permute-start(bf16[8,64,256]{2,1,0:T(8,128)(2,1)S(1)} %get-tuple-element.32), channel_id=1, source_target_pairs={{4,8},{6,10},{8,4},{10,6},{5,9},{7,11},{9,5},{11,7},{20,24},{22,26... | collective-permute-start | bytes 786440 | tf_op jit(solution)/shard_map/ppermute | solution.py:386
  39.4 12.9 %collective-permute-start.14 = (bf16[8,64,256]{2,1,0:T(8,128)(2,1)S(1)}, bf16[8,64,256]{2,1,0:T(8,128)(2,1)S(1)}, u32[]{:S(2)}, u32[]{:S(2)}) collective-permute-start(bf16[8,64,256]{2,1,0:T(8,128)(2,1)S(1)} %get-tuple-element.29.refs_4_), channel_id=1, source_target_pairs={{0,4},{2,6},{4,0},{6,2},{8,12},{10,14},{12,8},{14,10},{1,5},{3,7},... | collective-permute-start | bytes 786440 | tf_op jit(solution)/shard_map/ppermute | solution.py:385
  44.6 13.5 %collective-permute-start.10 = (bf16[8,64,256]{2,1,0:T(8,128)(2,1)S(1)}, bf16[8,64,256]{2,1,0:T(8,128)(2,1)S(1)}, u32[]{:S(2)}, u32[]{:S(2)}) collective-permute-start(bf16[8,64,256]{2,1,0:T(8,128)(2,1)S(1)} %get-tuple-element.30), channel_id=1, source_target_pairs={{4,8},{6,10},{8,4},{10,6},{5,9},{7,11},{9,5},{11,7},{20,24},{22,26... | collective-permute-start | bytes 786440 | tf_op jit(solution)/shard_map/ppermute | solution.py:386
  45.3 12.8 %collective-permute-start.11 = (bf16[8,64,256]{2,1,0:T(8,128)(2,1)S(1)}, bf16[8,64,256]{2,1,0:T(8,128)(2,1)S(1)}, u32[]{:S(2)}, u32[]{:S(2)}) collective-permute-start(bf16[8,64,256]{2,1,0:T(8,128)(2,1)S(1)} %get-tuple-element.31.refs_6_), channel_id=1, source_target_pairs={{0,4},{2,6},{4,0},{6,2},{8,12},{10,14},{12,8},{14,10},{1,5},{3,7},... | collective-permute-start | bytes 786440 | tf_op jit(solution)/shard_map/ppermute | solution.py:385
  49.5 7.9 %collective-permute-start.6 = (bf16[6,64,256]{2,1,0:T(8,128)(2,1)S(1)}, bf16[6,64,256]{2,1,0:T(8,128)(2,1)S(1)}, u32[]{:S(2)}, u32[]{:S(2)}) collective-permute-start(bf16[6,64,256]{2,1,0:T(8,128)(2,1)S(1)} %shard_map.81.refs_3_), channel_id=1, source_target_pairs={{0,2},{2,0},{4,6},{6,4},{8,10},{10,8},{12,14},{14,12},{1,3},{3,1},... | collective-permute-start | bytes 589832 | tf_op jit(solution)/shard_map/ppermute | solution.py:372
  51.7 10.0 %collective-permute-start.5 = (bf16[12,64,256]{2,1,0:T(8,128)(2,1)S(1)}, bf16[12,64,256]{2,1,0:T(8,128)(2,1)S(1)}, u32[]{:S(2)}, u32[]{:S(2)}) collective-permute-start(bf16[12,64,256]{2,1,0:T(8,128)(2,1)S(1)} %shard_map.82), channel_id=1, source_target_pairs={{0,2},{2,0},{4,6},{6,4},{8,10},{10,8},{12,14},{14,12},{1,3},{3,1},... | collective-permute-start | bytes 1179656 | tf_op jit(solution)/shard_map/ppermute | solution.py:372
  53.1 10.0 %collective-permute-start.17 = (bf16[8,64,256]{2,1,0:T(8,128)(2,1)S(1)}, bf16[8,64,256]{2,1,0:T(8,128)(2,1)S(1)}, u32[]{:S(2)}, u32[]{:S(2)}) collective-permute-start(bf16[8,64,256]{2,1,0:T(8,128)(2,1)S(1)} %get-tuple-element.33.refs_6_), channel_id=1, source_target_pairs={{0,4},{2,6},{4,0},{6,2},{8,12},{10,14},{12,8},{14,10},{1,5},{3,7},... | collective-permute-start | bytes 786440 | tf_op jit(solution)/shard_map/ppermute | solution.py:385
  57.4 5.7 %collective-permute-start.18 = (bf16[8,64,256]{2,1,0:T(8,128)(2,1)S(1)}, bf16[8,64,256]{2,1,0:T(8,128)(2,1)S(1)}, u32[]{:S(2)}, u32[]{:S(2)}) collective-permute-start(bf16[8,64,256]{2,1,0:T(8,128)(2,1)S(1)} %get-tuple-element.36), channel_id=1, source_target_pairs={{4,8},{6,10},{8,4},{10,6},{5,9},{7,11},{9,5},{11,7},{20,24},{22,26... | collective-permute-start | bytes 786440 | tf_op jit(solution)/shard_map/ppermute | solution.py:386
  59.0 6.4 %collective-permute-start.15 = (bf16[8,64,256]{2,1,0:T(8,128)(2,1)S(1)}, bf16[8,64,256]{2,1,0:T(8,128)(2,1)S(1)}, u32[]{:S(2)}, u32[]{:S(2)}) collective-permute-start(bf16[8,64,256]{2,1,0:T(8,128)(2,1)S(1)} %get-tuple-element.34), channel_id=1, source_target_pairs={{0,4},{2,6},{4,0},{6,2},{8,12},{10,14},{12,8},{14,10},{1,5},{3,7},... | collective-permute-start | bytes 786440 | tf_op jit(solution)/shard_map/ppermute | solution.py:385
  60.6 4.8 %collective-permute-start.16 = (bf16[8,64,256]{2,1,0:T(8,128)(2,1)S(1)}, bf16[8,64,256]{2,1,0:T(8,128)(2,1)S(1)}, u32[]{:S(2)}, u32[]{:S(2)}) collective-permute-start(bf16[8,64,256]{2,1,0:T(8,128)(2,1)S(1)} %get-tuple-element.35), channel_id=1, source_target_pairs={{4,8},{6,10},{8,4},{10,6},{5,9},{7,11},{9,5},{11,7},{20,24},{22,26... | collective-permute-start | bytes 786440 | tf_op jit(solution)/shard_map/ppermute | solution.py:386
  62.4 0.8 %copy-start.2 = (s32[8]{0:T(128)S(1)}, s32[8]{0:T(128)}, u32[]{:S(2)}) copy-start(s32[8]{0:T(128)} %param.13) | copy-start | bytes 100

commit v6 on v5

--- a/solution.py
+++ b/solution.py
@@ -111,11 +111,11 @@
 def table_kernel(n, cap, dest, table):
     classes, n_s = dest.shape
     line = n // Y
+    spare = 3 * line
     d = lax.axis_index("sector")
     z, y = split(d, Y)
     even = (z & 1) == 0
-
-    for i in range(3 * line):
+    for i in range(spare + 1):
         table[i * (1 + 2 * cap)] = 0
         for slot in range(cap):
             table[i * (1 + 2 * cap) + 1 + slot] = 0
@@ -125,38 +125,27 @@
         m = wrap(lax.shift_right_arithmetic(twice, 1), line)
         return jnp.where(m == 0, line - 1, jnp.where(even, line - 1 - m, m - 1))
 
-    def note(q, kind, j, p):
-        at = table_at(cap, q, kind)
+    def note(which, j, p):
+        at = which * (1 + 2 * cap)
         count = table[at]
         table[at + 1 + count] = j
         table[at + 1 + cap + count] = p
         table[at] = count + 1
 
-    for c in range(classes):
-
-        def step(i, _, c=c):
-            t, p = split(dest[c, i], n_s)
-            k = wrap(t - d, n)
-            j = c * n_s + i
-
-            @pl.when((k & 1) == 0)
-            def _():
-                note(position(k), OWN, j, p)
-
-            @pl.when((k & 1) == 1)
-            def _():
-                note(position(k - 1 + 2 * y), SEND, j, p)
-                note(position(k + 1 - 2 * y), CROSS, j, p)
-
-            return 0
-
-        lax.fori_loop(0, n_s, step, 0)
+    for j in range(classes * n_s):
+        t, p = split(dest[j // n_s, j % n_s], n_s)
+        k = wrap(t - d, n)
+        odd = k & 1
+        stays = odd == 0
+        note(jnp.where(stays, position(k) * 3 + OWN, position(k - 1 + 2 * y) * 3 + SEND), j, p)
+        table[spare * (1 + 2 * cap)] = 0
+        note(jnp.where(stays, spare, position(k + 1 - 2 * y) * 3 + CROSS), j, p)
 
 
 def make_table(n, cap, dest):
     return pl.pallas_call(
         functools.partial(table_kernel, n, cap),
-        out_shape=jax.ShapeDtypeStruct((3 * (n // Y) * (1 + 2 * cap),), jnp.int32),
+        out_shape=jax.ShapeDtypeStruct(((3 * (n // Y) + 1) * (1 + 2 * cap),), jnp.int32),
         in_specs=[SMEM],
         out_specs=SMEM,
         compiler_params=pltpu.CompilerParams(vmem_limit_bytes=2**20),
@@ -206,24 +195,28 @@
     )
 
 
-def pack(cap, spots, table, joined, after):
+def pack(cap, loads, table, joined, after):
     _, size, blk = joined[0].shape
-    used = sorted({i for _, i in spots})
+    used = sorted({i for spots in loads for _, i in spots})
 
     def kernel(table, *refs):
-        out = refs[-1]
-        for at, (q, i) in enumerate(spots):
-            for slot in range(cap):
-                out[at * cap + slot] = refs[used.index(i)][table[table_at(cap, q, SEND) + 1 + slot]]
-
-    (out,) = small_call(
+        for spots, out in zip(loads, refs[len(used):]):
+            for at, (q, i) in enumerate(spots):
+                for slot in range(cap):
+                    out[at * cap + slot] = refs[used.index(i)][table[table_at(cap, q, SEND) + 1 + slot]]
+
+    return small_call(
         kernel,
-        [jax.ShapeDtypeStruct((len(spots) * cap, size, blk), jnp.bfloat16)],
+        [jax.ShapeDtypeStruct((len(spots) * cap, size, blk), jnp.bfloat16) for spots in loads],
         [joined[i] for i in used],
         table,
         after,
     )
-    return out
+
+
+def has_far(line):
+    z, _ = split(lax.axis_index("sector"), Y)
+    return (z > 0) & (z < line - 1)
 
 
 def gather(cap, q, pieces, n_s, table, joined, crossed, after, dtype=jnp.bfloat16, cost=1000):
@@ -293,7 +286,8 @@
         for k, (q, arrived) in enumerate(sends):
             message = totals[fresh.index(q)][:n_s] if q in fresh else refs[at[q]][...].astype(jnp.float32)
             if arrived is not None:
-                message += refs[came[k]][...].astype(jnp.float32)
+                extra = refs[came[k]][...].astype(jnp.float32)
+                message += jnp.where(has_far(line), extra, 0.0) if k == 0 else extra
             outs[k][...] = message.astype(jnp.bfloat16)
         for k, q in enumerate(saved):
             outs[len(sends) + k][...] = totals[fresh.index(q)][:n_s].astype(jnp.bfloat16)
@@ -313,18 +307,19 @@
     return outs[:len(sends)]
 
 
-def finish(n_s, piece, rows, base, arrived, out=None):
+def finish(n_s, line, piece, rows, base, arrived, out=None):
     size, blk = base.shape[1:]
     half = blk // 2
 
     def kernel(rows, base, *refs):
         parts, (out, held, sem) = refs[:len(arrived)], refs[-3:]
-        line = lax.broadcasted_iota(jnp.int32, (size, blk), 0) + (lax.axis_index("mpo") * half + piece * size)
+        row = lax.broadcasted_iota(jnp.int32, (size, blk), 0) + (lax.axis_index("mpo") * half + piece * size)
+        inner = has_far(line)
         for p in range(n_s):
-            total = base[p]
-            for part in parts:
-                total += part[p].astype(jnp.float32)
-            held[p] = jnp.where(line < rows[p:p + 1], total, 0.0).astype(jnp.bfloat16)
+            total = base[p] + parts[0][p].astype(jnp.float32)
+            for part in parts[1:]:
+                total += jnp.where(inner, part[p].astype(jnp.float32), 0.0)
+            held[p] = jnp.where(row < rows[p:p + 1], total, 0.0).astype(jnp.bfloat16)
         leave = pltpu.make_async_copy(held, out.at[:, piece * size:(piece + 1) * size], sem)
         leave.start()
         leave.wait()
@@ -350,7 +345,12 @@
     pieces = [0, 1]
     across = [(d, d ^ 1) for d in range(n)]
     near = [(z * Y + y, (z ^ 1) * Y + y) for z in range(line) for y in range(Y)]
-    far = [(z * Y + y, (((z + 1) ^ 1) - 1) * Y + y) for z in range(1, line - 1) for y in range(Y)]
+    far = []
+    for z in range(line):
+        inner = 0 < z < line - 1
+        for d in range(z * Y, (z + 1) * Y):
+            other = ((((z + 1) ^ 1) - 1) * Y + d % Y) if inner else d
+            far += [(d * 2 + core, other * 2 + (core if inner else 1 - core)) for core in range(2)]
 
     send, keep = shift_sums(psi, left_env, right_env, term_class, active, sector_rows, classes, len(pieces))
     recv = [lax.ppermute(x, "mpo", [(0, 1), (1, 0)]) for x in send]
@@ -360,36 +360,35 @@
     loads.append([(line - 1, i) for i in pieces])
     crossed, joined, came = {}, [], []
     last = ready(table)
-    for k, spots in enumerate(loads):
-        if k < len(pieces):
-            whole, packed = join(cap, table, keep[k], recv[k], last)
-            joined.append(whole)
-        else:
-            packed = pack(cap, spots, table, joined, last)
-        last = [packed]
-        if k == 3:
-            firsts = packed
-        came.append(lax.ppermute(packed, "sector", across))
+    packed = []
+    for i in pieces:
+        whole, first = join(cap, table, keep[i], recv[i], last)
+        joined.append(whole)
+        packed.append(first)
+        last = [first]
+    came = [lax.ppermute(x, "sector", across) for x in packed]
+    firsts = pack(cap, loads[2:4], table, joined, last)
+    came += [lax.ppermute(x, "sector", across) for x in firsts]
+    came += [lax.ppermute(x, "sector", across) for x in pack(cap, loads[4:], table, joined, [firsts[0], came[1]])]
+    for spots, x in zip(loads, came):
         for at, spot in enumerate(spots):
-            crossed[spot] = (came[k], at * cap)
-        if k >= 3:
-            last = [packed, came[k - 2]]
+            crossed[spot] = (x, at * cap)
 
     acc = [{} for _ in pieces]
     near_in, far_in = [None for _ in pieces], [None for _ in pieces]
-    last = [firsts]
+    last = [firsts[0]]
     for step in range(1, line):
         for i in pieces:
             out = advance(cap, n_s, line, step, i, table, joined[i], crossed, acc[i], near_in[i], far_in[i], last)
             last = [out[0]]
             near_in[i] = lax.ppermute(out[0], "sector", near)
-            far_in[i] = lax.ppermute(out[1], "sector", far) if step > 1 else None
+            far_in[i] = lax.ppermute(out[1], ("sector", "mpo"), far) if step > 1 else None
     limits = jnp.broadcast_to(sector_rows[:, None], (n_s, psi.shape[2]))
     out = None
     for i in pieces:
         base = gather(cap, line - 1, [i], n_s, table, joined, crossed, (), jnp.float32)
         arrived = [x[i] for x in (near_in, far_in) if x[i] is not None]
-        out = finish(n_s, i, limits, base, arrived, out)
+        out = finish(n_s, line, i, limits, base, arrived, out)
     return out
 
 

time: 67.4 us -> 64.9 us (0.963); the launches traced: 66.2 us -> 64.7 us
  waiting for transfers between devices: 9.63 us -> 13 us
  starting transfers between devices: 26.2 us -> 23.6 us
  Pallas kernels: 27.7 us -> 25.5 us
    ppermute x11, waiting for transfers between devices: 8.26 us -> 10.5 us  [the longest x3 5.92 us: body(): lax.ppermute(x, 'sector', across)]
    ppermute x11, starting transfers between devices: 11.7 us -> 9.75 us  [the longest x2 3.96 us: body(): came = [lax.ppermute(x, 'sector', across) for x in packed]]
    pallas_call x16 -> x13, Pallas kernels: 10.8 us -> 9.26 us  [small_call(): pl.pallas_call(body, out_shape=outs, in_specs=[SMEM] * len(front) + [VMEM...]
    ppermute x6, waiting for transfers between devices: 1.37 us -> 2.54 us  [body(): near_in[i] = lax.ppermute(out[0], 'sector', near)]
    pallas_call x1, Pallas kernels: 2.84 us -> 2.15 us  [make_table(): pl.pallas_call(functools.partial(table_kernel, n, cap), out_shape=jax.Sha...]
  transfers between devices with their start and end apart: 19 -> 19, of which waited for: 4 -> 5; matrix products, arithmetic and copies ran while one was open for 0% -> 0% of each run, Pallas kernels for 22% -> 19%
where the time goes in v6:
time: 64.9 us; the launch traced here: 64.7 us
  Pallas kernels  25.5 us (39%)
  starting transfers between devices  23.6 us (36%)
  waiting for transfers between devices  13 us (20%)
  other arithmetic  2.25 us (3%)
    ppermute x6, starting transfers between devices, body(): near_in[i] = lax.ppermute(out[0], 'sector', near)  13.3 us
    pallas_call x1, Pallas kernels, shift_sums(): pl.pallas_call(shifts_kernel, out_shape=[jax.ShapeDtypeStruct((classes, n...  12.4 us
    pallas_call x13, Pallas kernels, small_call(): pl.pallas_call(body, out_shape=outs, in_specs=[SMEM] * len(front) + [VMEM...  9.26 us
    ppermute x3, waiting for transfers between devices, body(): lax.ppermute(x, 'sector', across)  5.92 us
    ppermute x2, starting transfers between devices, body(): came = [lax.ppermute(x, 'sector', across) for x in packed]  3.96 us
    ppermute x2, waiting for transfers between devices, body(): came = [lax.ppermute(x, 'sector', across) for x in packed]  3.48 us
    ppermute x2, starting transfers between devices, body(): came += [lax.ppermute(x, 'sector', across) for x in firsts]  3.05 us
    ppermute x3, starting transfers between devices, body(): lax.ppermute(x, 'sector', across)  2.59 us
  transfers between devices with their start and end apart: 19, of which 5 were waited for; matrix products, arithmetic and copies ran while one was open for 0% of the time, Pallas kernels for 19%

profile of v6, /device:TPU:0, one launch (start us, length us, event | category | flops | bytes accessed | tf_op | source)
XLA Modules:
  0.0 64.7 jit_solution(5614957471189172115)
XLA Ops:
  0.0 0.8 %iota_compare_fusion = pred[8,256]{1,0:T(8,128)(4,1)S(1)} fusion(s32[8]{0:T(128)} %param.13), kind=kLoop, calls=%fused_computation.1 | loop fusion | flops 2048 | bytes 2080 | tf_op jit(solution)/shard_map/lt | solution.py:84
  0.8 1.5 %broadcast_select_fusion.masked = bf16[8,256,256]{2,1,0:T(8,128)(2,1)S(1)} fusion(bf16[8,256,256]{2,1,0:T(8,128)(2,1)} %param.7, pred[8,256]{1,0:T(8,128)(4,1)S(1)} %iota_compare_fusion), kind=kLoop, calls=%fused_computation | loop fusion | flops 524288 | bytes 2099200 | tf_op jit(solution)/shard_map/jit(_where)/select_n | solution.py:84
  2.3 0.0 copy-done.3
  2.3 0.0 copy-done.1
  2.3 0.0 copy-start
  2.3 12.4 %shard_map.74 = (bf16[5,8,64,256]{3,2,1,0:T(8,128)(2,1)S(1)}, bf16[5,8,64,256]{3,2,1,0:T(8,128)(2,1)S(1)}, bf16[5,8,64,256]{3,2,1,0:T(8,128)(2,1)S(1)}, bf16[5,8,64,256]{3,2,1,0:T(8,128)(2,1)S(1)}) custom-call(s32[8,13]{1,0:T(8,128)S(1)} %select_bitcast_fusion.slots, bf16[8,256,256]{2,1,0:T(8,128)(2,1)S(1)} %broadcast_select_fusion.masked, ...), custom_call_target="tpu_custom_call" | custom-call | flops 6979321856 | bytes 27262976 | tf_op jit(solution)/shard_map/pallas_call | solution.py:86
  14.7 0.5 collective-permute-start.1
  15.2 0.1 collective-permute-start
  15.3 0.0 copy-done
  15.3 2.1 %shard_map.73.refs_0_ = s32[169]{0:T(256)S(1)} custom-call(s32[5,8]{1,0:T(8,128)S(1)} %copy-done), custom_call_target="tpu_custom_call" | custom-call | flops 4000 | bytes 4000 | tf_op jit(solution)/shard_map/pallas_call | solution.py:146
  17.4 0.6 shard_map.75.refs_3_
  18.0 0.0 collective-permute-done.1.refs_2_
  18.0 0.7 %shard_map.76 = (bf16[40,64,256]{2,1,0:T(8,128)(2,1)S(1)}, bf16[6,64,256]{2,1,0:T(8,128)(2,1)S(1)}) custom-call(s32[169]{0:T(256)S(1)} %shard_map.73.refs_0_, bf16[40,64,256]{2,1,0:T(8,128)(2,1)S(1)} %bitcast.7, bf16[40,64,256]{2,1,0:T(8,128)(2,1)S(1)} %collective-permute-done.1.refs_2_, s32[8,128]{1,0:T(8,128)S(1)} %shard_map.75.refs_3_), custom_call_target="tpu_custom_call" | custom-call | bytes 1000 | tf_op jit(solution)/shard_map/pallas_call | solution.py:163
  18.8 3.0 %collective-permute-start.5 = (bf16[6,64,256]{2,1,0:T(8,128)(2,1)S(1)}, bf16[6,64,256]{2,1,0:T(8,128)(2,1)S(1)}, u32[]{:S(2)}, u32[]{:S(2)}) collective-permute-start(bf16[6,64,256]{2,1,0:T(8,128)(2,1)S(1)} %get-tuple-element.30.refs_3_), channel_id=1, source_target_pairs={{0,2},{2,0},{4,6},{6,4},{8,10},{10,8},{12,14},{14,12},{1,3},{3,1},... | collective-permute-start | bytes 589832 | tf_op jit(solution)/shard_map/ppermute | solution.py:369
  21.8 0.0 collective-permute-done.refs_2_
  21.8 0.7 %shard_map.77 = (bf16[40,64,256]{2,1,0:T(8,128)(2,1)S(1)}, bf16[6,64,256]{2,1,0:T(8,128)(2,1)S(1)}) custom-call(s32[169]{0:T(256)S(1)} %shard_map.73.refs_0_, bf16[40,64,256]{2,1,0:T(8,128)(2,1)S(1)} %bitcast.6, bf16[40,64,256]{2,1,0:T(8,128)(2,1)S(1)} %collective-permute-done.refs_2_, bf16[6,64,256]{2,1,0:T(8,128)(2,1)S(1)} %get-tuple-element.30.refs_3_), custom_call_target="tpu_custom_call" | custom-call | bytes 1000 | tf_op jit(solution)/shard_map/pallas_call | solution.py:163
  22.5 0.9 %collective-permute-start.2 = (bf16[6,64,256]{2,1,0:T(8,128)(2,1)S(1)}, bf16[6,64,256]{2,1,0:T(8,128)(2,1)S(1)}, u32[]{:S(2)}, u32[]{:S(2)}) collective-permute-start(bf16[6,64,256]{2,1,0:T(8,128)(2,1)S(1)} %get-tuple-element.33.refs_3_), channel_id=1, source_target_pairs={{0,2},{2,0},{4,6},{6,4},{8,10},{10,8},{12,14},{14,12},{1,3},{3,1},... | collective-permute-start | bytes 589832 | tf_op jit(solution)/shard_map/ppermute | solution.py:369
  23.4 0.6 shard_map.78
  24.0 3.5 %collective-permute-done.5.refs_2_ = bf16[6,64,256]{2,1,0:T(8,128)(2,1)S(1)} collective-permute-done((bf16[6,64,256]{2,1,0:T(8,128)(2,1)S(1)}, bf16[6,64,256]{2,1,0:T(8,128)(2,1)S(1)}, u32[]{:S(2)}, u32[]{:S(2)}) %collective-permute-start.5) | collective-permute-done | bytes 196640 | tf_op jit(solution)/shard_map/ppermute | solution.py:369
  27.5 0.7 %shard_map.81.refs_3_ = bf16[8,64,256]{2,1,0:T(8,128)(2,1)S(1)} custom-call(s32[169]{0:T(256)S(1)} %shard_map.73.refs_0_, bf16[40,64,256]{2,1,0:T(8,128)(2,1)S(1)} %get-tuple-element.32.refs_1_, bf16[6,64,256]{2,1,0:T(8,128)(2,1)S(1)} %collective-permute-done.5.refs_2_, bf16[6,64,256]{2,1,0:T(8,128)(2,1)S(1)} %get-tuple-element.34.refs_3_), custom_call_target="tpu_custom_call" | custom-call | bytes 1000 | tf_op jit(solution)/shard_map/pallas_call | solution.py:163
  28.2 2.2 %collective-permute-start.9 = (bf16[8,64,256]{2,1,0:T(8,128)(2,1)S(1)}, bf16[8,64,256]{2,1,0:T(8,128)(2,1)S(1)}, u32[]{:S(2)}, u32[]{:S(2)}) collective-permute-start(bf16[8,64,256]{2,1,0:T(8,128)(2,1)S(1)} %shard_map.81.refs_3_), channel_id=1, source_target_pairs={{0,4},{2,6},{4,0},{6,2},{8,12},{10,14},{12,8},{14,10},{1,5},{3,7},... | collective-permute-start | bytes 786440 | tf_op jit(solution)/shard_map/ppermute | solution.py:384
  30.4 1.5 %collective-permute-start.8 = (bf16[6,64,256]{2,1,0:T(8,128)(2,1)S(1)}, bf16[6,64,256]{2,1,0:T(8,128)(2,1)S(1)}, u32[]{:S(2)}, u32[]{:S(2)}) collective-permute-start(bf16[6,64,256]{2,1,0:T(8,128)(2,1)S(1)} %get-tuple-element.34.refs_3_), channel_id=1, source_target_pairs={{0,2},{2,0},{4,6},{6,4},{8,10},{10,8},{12,14},{14,12},{1,3},{3,1},... | collective-permute-start | bytes 589832 | tf_op jit(solution)/shard_map/ppermute | solution.py:371
  31.9 0.0 collective-permute-done.2.refs_4_.refs_2_
  31.9 0.7 %shard_map.82.refs_4_.refs_3_ = bf16[8,64,256]{2,1,0:T(8,128)(2,1)S(1)} custom-call(s32[169]{0:T(256)S(1)} %shard_map.73.refs_0_, bf16[40,64,256]{2,1,0:T(8,128)(2,1)S(1)} %get-tuple-element.31.refs_2_.refs_1_, bf16[6,64,256]{2,1,0:T(8,128)(2,1)S(1)} %collective-permute-done.2.refs_4_.refs_2_, bf16[8,64,256]{2,1,0:T(8,128)(2,1)S(1)} %shard_map.81.refs_3_), custom_call_target="tpu_custom_call" | custom-call | bytes 1000 | tf_op jit(solution)/shard_map/pallas_call | solution.py:163
  32.6 2.0 %collective-permute-start.7 = (bf16[8,64,256]{2,1,0:T(8,128)(2,1)S(1)}, bf16[8,64,256]{2,1,0:T(8,128)(2,1)S(1)}, u32[]{:S(2)}, u32[]{:S(2)}) collective-permute-start(bf16[8,64,256]{2,1,0:T(8,128)(2,1)S(1)} %shard_map.82.refs_4_.refs_3_), channel_id=1, source_target_pairs={{0,4},{2,6},{4,0},{6,2},{8,12},{10,14},{12,8},{14,10},{1,5},{3,7},... | collective-permute-start | bytes 786440 | tf_op jit(solution)/shard_map/ppermute | solution.py:384
  34.6 1.5 %collective-permute-start.6 = (bf16[6,64,256]{2,1,0:T(8,128)(2,1)S(1)}, bf16[6,64,256]{2,1,0:T(8,128)(2,1)S(1)}, u32[]{:S(2)}, u32[]{:S(2)}) collective-permute-start(bf16[6,64,256]{2,1,0:T(8,128)(2,1)S(1)} %get-tuple-element.37), channel_id=1, source_target_pairs={{0,2},{2,0},{4,6},{6,4},{8,10},{10,8},{12,14},{14,12},{1,3},{3,1},... | collective-permute-start | bytes 589832 | tf_op jit(solution)/shard_map/ppermute | solution.py:371
  36.1 0.6 shard_map.79
  36.7 0.6 collective-permute-start.12
  37.3 0.0 collective-permute-done.8.refs_2_
  37.3 0.0 collective-permute-done.9.refs_3_
  37.3 0.8 %shard_map.83 = (bf16[8,64,256]{2,1,0:T(8,128)(2,1)S(1)}, bf16[8,64,256]{2,1,0:T(8,128)(2,1)S(1)}) custom-call(s32[169]{0:T(256)S(1)} %shard_map.73.refs_0_, bf16[40,64,256]{2,1,0:T(8,128)(2,1)S(1)} %get-tuple-element.32.refs_1_, bf16[6,64,256]{2,1,0:T(8,128)(2,1)S(1)} %collective-permute-done.8.refs_2_, ...), custom_call_target="tpu_custom_call" | custom-call | bytes 1000 | tf_op jit(solution)/shard_map/pallas_call | solution.py:163
  38.0 0.1 collective-permute-start.13
  38.1 3.1 %collective-permute-start.14 = (bf16[8,64,256]{2,1,0:T(8,128)(2,1)S(1)}, bf16[8,64,256]{2,1,0:T(8,128)(2,1)S(1)}, u32[]{:S(2)}, u32[]{:S(2)}) collective-permute-start(bf16[8,64,256]{2,1,0:T(8,128)(2,1)S(1)} %get-tuple-element.38.refs_4_), channel_id=1, source_target_pairs={{0,4},{2,6},{4,0},{6,2},{8,12},{10,14},{12,8},{14,10},{1,5},{3,7},... | collective-permute-start | bytes 786440 | tf_op jit(solution)/shard_map/ppermute | solution.py:384
  41.3 1.1 %collective-permute-done.6.refs_2_ = bf16[6,64,256]{2,1,0:T(8,128)(2,1)S(1)} collective-permute-done((bf16[6,64,256]{2,1,0:T(8,128)(2,1)S(1)}, bf16[6,64,256]{2,1,0:T(8,128)(2,1)S(1)}, u32[]{:S(2)}, u32[]{:S(2)}) %collective-permute-start.6) | collective-permute-done | bytes 196640 | tf_op jit(solution)/shard_map/ppermute | solution.py:371
  42.4 0.0 collective-permute-done.7.refs_3_
  42.4 0.8 %shard_map.84 = (bf16[8,64,256]{2,1,0:T(8,128)(2,1)S(1)}, bf16[8,64,256]{2,1,0:T(8,128)(2,1)S(1)}) custom-call(s32[169]{0:T(256)S(1)} %shard_map.73.refs_0_, bf16[40,64,256]{2,1,0:T(8,128)(2,1)S(1)} %get-tuple-element.31.refs_2_.refs_1_, bf16[6,64,256]{2,1,0:T(8,128)(2,1)S(1)} %collective-permute-done.6.refs_2_, ...), custom_call_target="tpu_custom_call" | custom-call | bytes 1000 | tf_op jit(solution)/shard_map/pallas_call | solution.py:163
  43.1 0.1 collective-permute-start.10
  43.2 3.1 %collective-permute-start.11 = (bf16[8,64,256]{2,1,0:T(8,128)(2,1)S(1)}, bf16[8,64,256]{2,1,0:T(8,128)(2,1)S(1)}, u32[]{:S(2)}, u32[]{:S(2)}) collective-permute-start(bf16[8,64,256]{2,1,0:T(8,128)(2,1)S(1)} %get-tuple-element.40.refs_6_), channel_id=1, source_target_pairs={{0,4},{2,6},{4,0},{6,2},{8,12},{10,14},{12,8},{14,10},{1,5},{3,7},... | collective-permute-start | bytes 786440 | tf_op jit(solution)/shard_map/ppermute | solution.py:384
  46.3 0.0 collective-permute-done.12.refs_2_
  46.4 1.5 %collective-permute-start.4 = (bf16[6,64,256]{2,1,0:T(8,128)(2,1)S(1)}, bf16[6,64,256]{2,1,0:T(8,128)(2,1)S(1)}, u32[]{:S(2)}, u32[]{:S(2)}) collective-permute-start(bf16[6,64,256]{2,1,0:T(8,128)(2,1)S(1)} %get-tuple-element.36), channel_id=1, source_target_pairs={{0,2},{2,0},{4,6},{6,4},{8,10},{10,8},{12,14},{14,12},{1,3},{3,1},... | collective-permute-start | bytes 589832 | tf_op jit(solution)/shard_map/ppermute | solution.py:372
  47.9 0.0 collective-permute-done.13.refs_4_
  47.9 0.5 collective-permute-start.3
  48.4 0.0 collective-permute-done.14.refs_5_
  48.4 0.9 %shard_map.85 = (bf16[8,64,256]{2,1,0:T(8,128)(2,1)S(1)}, bf16[8,64,256]{2,1,0:T(8,128)(2,1)S(1)}) custom-call(s32[169]{0:T(256)S(1)} %shard_map.73.refs_0_, bf16[40,64,256]{2,1,0:T(8,128)(2,1)S(1)} %get-tuple-element.32.refs_1_, bf16[6,64,256]{2,1,0:T(8,128)(2,1)S(1)} %collective-permute-done.12.refs_2_, bf16[8,64,256]{2,1,0:T(8,128)(2,1)S(1)} %shard_map.81.refs_3_, ...), custom_call_target="tpu_custom_call" | custom-call | bytes 1000 | tf_op jit(solution)/shard_map/pallas_call | solution.py:163
  49.3 1.4 %collective-permute-start.17 = (bf16[8,64,256]{2,1,0:T(8,128)(2,1)S(1)}, bf16[8,64,256]{2,1,0:T(8,128)(2,1)S(1)}, u32[]{:S(2)}, u32[]{:S(2)}) collective-permute-start(bf16[8,64,256]{2,1,0:T(8,128)(2,1)S(1)} %get-tuple-element.43.refs_6_), channel_id=1, source_target_pairs={{0,4},{2,6},{4,0},{6,2},{8,12},{10,14},{12,8},{14,10},{1,5},{3,7},... | collective-permute-start | bytes 786440 | tf_op jit(solution)/shard_map/ppermute | solution.py:384
  50.7 3.5 %collective-permute-done.4.refs_2_ = bf16[6,64,256]{2,1,0:T(8,128)(2,1)S(1)} collective-permute-done((bf16[6,64,256]{2,1,0:T(8,128)(2,1)S(1)}, bf16[6,64,256]{2,1,0:T(8,128)(2,1)S(1)}, u32[]{:S(2)}, u32[]{:S(2)}) %collective-permute-start.4) | collective-permute-done | bytes 196640 | tf_op jit(solution)/shard_map/ppermute | solution.py:372
  54.2 0.0 collective-permute-start.18
  54.2 0.0 collective-permute-done.10.refs_4_
  54.2 0.0 collective-permute-done.11.refs_5_
  54.2 0.9 %shard_map.86 = (bf16[8,64,256]{2,1,0:T(8,128)(2,1)S(1)}, bf16[8,64,256]{2,1,0:T(8,128)(2,1)S(1)}) custom-call(s32[169]{0:T(256)S(1)} %shard_map.73.refs_0_, bf16[40,64,256]{2,1,0:T(8,128)(2,1)S(1)} %get-tuple-element.31.refs_2_.refs_1_, bf16[6,64,256]{2,1,0:T(8,128)(2,1)S(1)} %collective-permute-done.4.refs_2_, ...), custom_call_target="tpu_custom_call" | custom-call | bytes 1000 | tf_op jit(solution)/shard_map/pallas_call | solution.py:163
  55.1 1.5 %collective-permute-start.15 = (bf16[8,64,256]{2,1,0:T(8,128)(2,1)S(1)}, bf16[8,64,256]{2,1,0:T(8,128)(2,1)S(1)}, u32[]{:S(2)}, u32[]{:S(2)}) collective-permute-start(bf16[8,64,256]{2,1,0:T(8,128)(2,1)S(1)} %get-tuple-element.44), channel_id=1, source_target_pairs={{0,4},{2,6},{4,0},{6,2},{8,12},{10,14},{12,8},{14,10},{1,5},{3,7},... | collective-permute-start | bytes 786440 | tf_op jit(solution)/shard_map/ppermute | solution.py:384
  56.5 0.0 collective-permute-start.16
  56.5 2.4 %collective-permute-done.3.refs_2_ = bf16[12,64,256]{2,1,0:T(8,128)(2,1)S(1)} collective-permute-done((bf16[12,64,256]{2,1,0:T(8,128)(2,1)S(1)}, bf16[12,64,256]{2,1,0:T(8,128)(2,1)S(1)}, u32[]{:S(2)}, u32[]{:S(2)}) %collective-permute-start.3) | collective-permute-done | bytes 393248 | tf_op jit(solution)/shard_map/ppermute | solution.py:372
  58.9 0.7 %shard_map.87.base = f32[8,64,256]{2,1,0:T(8,128)S(1)} custom-call(s32[169]{0:T(256)S(1)} %shard_map.73.refs_0_, bf16[40,64,256]{2,1,0:T(8,128)(2,1)S(1)} %get-tuple-element.32.refs_1_, bf16[12,64,256]{2,1,0:T(8,128)(2,1)S(1)} %collective-permute-done.3.refs_2_), custom_call_target="tpu_custom_call" | custom-call | bytes 1000 | tf_op jit(solution)/shard_map/pallas_call | solution.py:163
  59.7 0.0 copy-start.2
  59.7 0.7 %shard_map.80.base = f32[8,64,256]{2,1,0:T(8,128)S(1)} custom-call(s32[169]{0:T(256)S(1)} %shard_map.73.refs_0_, bf16[40,64,256]{2,1,0:T(8,128)(2,1)S(1)} %get-tuple-element.31.refs_2_.refs_1_, bf16[12,64,256]{2,1,0:T(8,128)(2,1)S(1)} %collective-permute-done.3.refs_2_), custom_call_target="tpu_custom_call" | custom-call | bytes 1000 | tf_op jit(solution)/shard_map/pallas_call | solution.py:163
  60.4 0.0 collective-permute-done.17.refs_0_
  60.4 0.0 collective-permute-done.18.refs_1_
  60.4 0.0 copy-done.2
  60.4 0.1 broadcast_in_dim.32.rows
  60.5 0.8 %shard_map.88.refs_2_ = bf16[8,128,256]{2,1,0:T(8,128)(2,1)} custom-call(s32[8,256]{1,0:T(8,128)S(1)} %broadcast_in_dim.32.rows, f32[8,64,256]{2,1,0:T(8,128)S(1)} %shard_map.87.base, bf16[8,64,256]{2,1,0:T(8,128)(2,1)S(1)} %collective-permute-done.17.refs_0_, bf16[8,64,256]{2,1,0:T(8,128)(2,1)S(1)} %collective-permute-done.18.refs_1_), custom_call_target="tpu_custom_call" | custom-call | bytes 1000 | tf_op jit(solution)/shard_map/pallas_call | solution.py:328
  61.3 2.5 %collective-permute-done.15.refs_0_ = bf16[8,64,256]{2,1,0:T(8,128)(2,1)S(1)} collective-permute-done((bf16[8,64,256]{2,1,0:T(8,128)(2,1)S(1)}, bf16[8,64,256]{2,1,0:T(8,128)(2,1)S(1)}, u32[]{:S(2)}, u32[]{:S(2)}) %collective-permute-start.15) | collective-permute-done | bytes 262176 | tf_op jit(solution)/shard_map/ppermute | solution.py:384
  63.9 0.0 collective-permute-done.16.refs_1_
  63.9 0.8 %shard_map.89 = bf16[8,128,256]{2,1,0:T(8,128)(2,1)} custom-call(s32[8,256]{1,0:T(8,128)S(1)} %broadcast_in_dim.32.rows, f32[8,64,256]{2,1,0:T(8,128)S(1)} %shard_map.80.base, bf16[8,64,256]{2,1,0:T(8,128)(2,1)S(1)} %collective-permute-done.15.refs_0_, bf16[8,64,256]{2,1,0:T(8,128)(2,1)S(1)} %collective-permute-done.16.refs_1_, ...), custom_call_target="tpu_custom_call", output_to_operand_aliasing={{}: (4, {})} | custom-call | bytes 1000 | tf_op jit(solution)/shard_map/pallas_call | solution.py:328
  (3 shorter events, 0.0 us)
Async XLA Ops:
  0.0 2.3 %copy-start.3 = (s32[13]{0:T(128)S(1)}, s32[13]{0:T(128)}, u32[]{:S(2)}) copy-start(s32[13]{0:T(128)} %param.10) | copy-start | bytes 160
  0.0 2.3 %copy-start.1 = (s32[13,8]{0,1:T(8,128)S(1)}, s32[13,8]{0,1:T(8,128)}, u32[]{:S(2)}) copy-start(s32[13,8]{0,1:T(8,128)} %param.11) | copy-start | bytes 1252
  2.3 13.0 %copy-start = (s32[5,8]{1,0:T(8,128)S(1)}, s32[5,8]{1,0:T(8,128)}, u32[]{:S(2)}) copy-start(s32[5,8]{1,0:T(8,128)} %dest.1) | copy-start | bytes 484
  14.7 3.3 %collective-permute-start.1 = (bf16[40,64,256]{2,1,0:T(8,128)(2,1)S(1)}, bf16[40,64,256]{2,1,0:T(8,128)(2,1)S(1)}, u32[]{:S(2)}, u32[]{:S(2)}) collective-permute-start(bf16[40,64,256]{2,1,0:T(8,128)(2,1)S(1)} %bitcast.9), channel_id=1, source_target_pairs={{0,1},{1,0},{2,3},{3,2},{4,5},{5,4},{6,7},{7,6},{8,9},{9,8},{10,11... | collective-permute-start | bytes 3932168 | tf_op jit(solution)/shard_map/ppermute | solution.py:356
  15.2 6.6 %collective-permute-start = (bf16[40,64,256]{2,1,0:T(8,128)(2,1)S(1)}, bf16[40,64,256]{2,1,0:T(8,128)(2,1)S(1)}, u32[]{:S(2)}, u32[]{:S(2)}) collective-permute-start(bf16[40,64,256]{2,1,0:T(8,128)(2,1)S(1)} %bitcast.8), channel_id=1, source_target_pairs={{0,1},{1,0},{2,3},{3,2},{4,5},{5,4},{6,7},{7,6},{8,9},{9,8},{10,11... | collective-permute-start | bytes 3932168 | tf_op jit(solution)/shard_map/ppermute | solution.py:356
  18.8 8.7 %collective-permute-start.5 = (bf16[6,64,256]{2,1,0:T(8,128)(2,1)S(1)}, bf16[6,64,256]{2,1,0:T(8,128)(2,1)S(1)}, u32[]{:S(2)}, u32[]{:S(2)}) collective-permute-start(bf16[6,64,256]{2,1,0:T(8,128)(2,1)S(1)} %get-tuple-element.30.refs_3_), channel_id=1, source_target_pairs={{0,2},{2,0},{4,6},{6,4},{8,10},{10,8},{12,14},{14,12},{1,3},{3,1},... | collective-permute-start | bytes 589832 | tf_op jit(solution)/shard_map/ppermute | solution.py:369
  22.5 9.4 %collective-permute-start.2 = (bf16[6,64,256]{2,1,0:T(8,128)(2,1)S(1)}, bf16[6,64,256]{2,1,0:T(8,128)(2,1)S(1)}, u32[]{:S(2)}, u32[]{:S(2)}) collective-permute-start(bf16[6,64,256]{2,1,0:T(8,128)(2,1)S(1)} %get-tuple-element.33.refs_3_), channel_id=1, source_target_pairs={{0,2},{2,0},{4,6},{6,4},{8,10},{10,8},{12,14},{14,12},{1,3},{3,1},... | collective-permute-start | bytes 589832 | tf_op jit(solution)/shard_map/ppermute | solution.py:369
  28.2 9.1 %collective-permute-start.9 = (bf16[8,64,256]{2,1,0:T(8,128)(2,1)S(1)}, bf16[8,64,256]{2,1,0:T(8,128)(2,1)S(1)}, u32[]{:S(2)}, u32[]{:S(2)}) collective-permute-start(bf16[8,64,256]{2,1,0:T(8,128)(2,1)S(1)} %shard_map.81.refs_3_), channel_id=1, source_target_pairs={{0,4},{2,6},{4,0},{6,2},{8,12},{10,14},{12,8},{14,10},{1,5},{3,7},... | collective-permute-start | bytes 786440 | tf_op jit(solution)/shard_map/ppermute | solution.py:384
  30.4 6.9 %collective-permute-start.8 = (bf16[6,64,256]{2,1,0:T(8,128)(2,1)S(1)}, bf16[6,64,256]{2,1,0:T(8,128)(2,1)S(1)}, u32[]{:S(2)}, u32[]{:S(2)}) collective-permute-start(bf16[6,64,256]{2,1,0:T(8,128)(2,1)S(1)} %get-tuple-element.34.refs_3_), channel_id=1, source_target_pairs={{0,2},{2,0},{4,6},{6,4},{8,10},{10,8},{12,14},{14,12},{1,3},{3,1},... | collective-permute-start | bytes 589832 | tf_op jit(solution)/shard_map/ppermute | solution.py:371
  32.6 9.7 %collective-permute-start.7 = (bf16[8,64,256]{2,1,0:T(8,128)(2,1)S(1)}, bf16[8,64,256]{2,1,0:T(8,128)(2,1)S(1)}, u32[]{:S(2)}, u32[]{:S(2)}) collective-permute-start(bf16[8,64,256]{2,1,0:T(8,128)(2,1)S(1)} %shard_map.82.refs_4_.refs_3_), channel_id=1, source_target_pairs={{0,4},{2,6},{4,0},{6,2},{8,12},{10,14},{12,8},{14,10},{1,5},{3,7},... | collective-permute-start | bytes 786440 | tf_op jit(solution)/shard_map/ppermute | solution.py:384
  34.6 7.8 %collective-permute-start.6 = (bf16[6,64,256]{2,1,0:T(8,128)(2,1)S(1)}, bf16[6,64,256]{2,1,0:T(8,128)(2,1)S(1)}, u32[]{:S(2)}, u32[]{:S(2)}) collective-permute-start(bf16[6,64,256]{2,1,0:T(8,128)(2,1)S(1)} %get-tuple-element.37), channel_id=1, source_target_pairs={{0,2},{2,0},{4,6},{6,4},{8,10},{10,8},{12,14},{14,12},{1,3},{3,1},... | collective-permute-start | bytes 589832 | tf_op jit(solution)/shard_map/ppermute | solution.py:371
  36.7 9.6 %collective-permute-start.12 = (bf16[6,64,256]{2,1,0:T(8,128)(2,1)S(1)}, bf16[6,64,256]{2,1,0:T(8,128)(2,1)S(1)}, u32[]{:S(2)}, u32[]{:S(2)}) collective-permute-start(bf16[6,64,256]{2,1,0:T(8,128)(2,1)S(1)} %get-tuple-element.41), channel_id=1, source_target_pairs={{0,2},{2,0},{4,6},{6,4},{8,10},{10,8},{12,14},{14,12},{1,3},{3,1},... | collective-permute-start | bytes 589832 | tf_op jit(solution)/shard_map/ppermute | solution.py:372
  38.0 9.8 %collective-permute-start.13 = (bf16[8,64,256]{2,1,0:T(8,128)(2,1)S(1)}, bf16[8,64,256]{2,1,0:T(8,128)(2,1)S(1)}, u32[]{:S(2)}, u32[]{:S(2)}) collective-permute-start(bf16[8,64,256]{2,1,0:T(8,128)(2,1)S(1)} %get-tuple-element.42), channel_id=1, source_target_pairs={{0,1},{1,0},{2,3},{3,2},{4,8},{5,9},{6,10},{7,11},{8,4},{9,5},{10,... | collective-permute-start | bytes 786440 | tf_op jit(solution)/shard_map/ppermute | solution.py:385
  38.1 10.3 %collective-permute-start.14 = (bf16[8,64,256]{2,1,0:T(8,128)(2,1)S(1)}, bf16[8,64,256]{2,1,0:T(8,128)(2,1)S(1)}, u32[]{:S(2)}, u32[]{:S(2)}) collective-permute-start(bf16[8,64,256]{2,1,0:T(8,128)(2,1)S(1)} %get-tuple-element.38.refs_4_), channel_id=1, source_target_pairs={{0,4},{2,6},{4,0},{6,2},{8,12},{10,14},{12,8},{14,10},{1,5},{3,7},... | collective-permute-start | bytes 786440 | tf_op jit(solution)/shard_map/ppermute | solution.py:384
  43.1 11.1 %collective-permute-start.10 = (bf16[8,64,256]{2,1,0:T(8,128)(2,1)S(1)}, bf16[8,64,256]{2,1,0:T(8,128)(2,1)S(1)}, u32[]{:S(2)}, u32[]{:S(2)}) collective-permute-start(bf16[8,64,256]{2,1,0:T(8,128)(2,1)S(1)} %get-tuple-element.39), channel_id=1, source_target_pairs={{0,1},{1,0},{2,3},{3,2},{4,8},{5,9},{6,10},{7,11},{8,4},{9,5},{10,... | collective-permute-start | bytes 786440 | tf_op jit(solution)/shard_map/ppermute | solution.py:385
  43.2 11.0 %collective-permute-start.11 = (bf16[8,64,256]{2,1,0:T(8,128)(2,1)S(1)}, bf16[8,64,256]{2,1,0:T(8,128)(2,1)S(1)}, u32[]{:S(2)}, u32[]{:S(2)}) collective-permute-start(bf16[8,64,256]{2,1,0:T(8,128)(2,1)S(1)} %get-tuple-element.40.refs_6_), channel_id=1, source_target_pairs={{0,4},{2,6},{4,0},{6,2},{8,12},{10,14},{12,8},{14,10},{1,5},{3,7},... | collective-permute-start | bytes 786440 | tf_op jit(solution)/shard_map/ppermute | solution.py:384
  46.4 7.8 %collective-permute-start.4 = (bf16[6,64,256]{2,1,0:T(8,128)(2,1)S(1)}, bf16[6,64,256]{2,1,0:T(8,128)(2,1)S(1)}, u32[]{:S(2)}, u32[]{:S(2)}) collective-permute-start(bf16[6,64,256]{2,1,0:T(8,128)(2,1)S(1)} %get-tuple-element.36), channel_id=1, source_target_pairs={{0,2},{2,0},{4,6},{6,4},{8,10},{10,8},{12,14},{14,12},{1,3},{3,1},... | collective-permute-start | bytes 589832 | tf_op jit(solution)/shard_map/ppermute | solution.py:372
  47.9 11.1 %collective-permute-start.3 = (bf16[12,64,256]{2,1,0:T(8,128)(2,1)S(1)}, bf16[12,64,256]{2,1,0:T(8,128)(2,1)S(1)}, u32[]{:S(2)}, u32[]{:S(2)}) collective-permute-start(bf16[12,64,256]{2,1,0:T(8,128)(2,1)S(1)} %get-tuple-element.35), channel_id=1, source_target_pairs={{0,2},{2,0},{4,6},{6,4},{8,10},{10,8},{12,14},{14,12},{1,3},{3,1},... | collective-permute-start | bytes 1179656 | tf_op jit(solution)/shard_map/ppermute | solution.py:372
  49.3 11.1 %collective-permute-start.17 = (bf16[8,64,256]{2,1,0:T(8,128)(2,1)S(1)}, bf16[8,64,256]{2,1,0:T(8,128)(2,1)S(1)}, u32[]{:S(2)}, u32[]{:S(2)}) collective-permute-start(bf16[8,64,256]{2,1,0:T(8,128)(2,1)S(1)} %get-tuple-element.43.refs_6_), channel_id=1, source_target_pairs={{0,4},{2,6},{4,0},{6,2},{8,12},{10,14},{12,8},{14,10},{1,5},{3,7},... | collective-permute-start | bytes 786440 | tf_op jit(solution)/shard_map/ppermute | solution.py:384
  54.2 6.2 %collective-permute-start.18 = (bf16[8,64,256]{2,1,0:T(8,128)(2,1)S(1)}, bf16[8,64,256]{2,1,0:T(8,128)(2,1)S(1)}, u32[]{:S(2)}, u32[]{:S(2)}) collective-permute-start(bf16[8,64,256]{2,1,0:T(8,128)(2,1)S(1)} %get-tuple-element.46), channel_id=1, source_target_pairs={{0,1},{1,0},{2,3},{3,2},{4,8},{5,9},{6,10},{7,11},{8,4},{9,5},{10,... | collective-permute-start | bytes 786440 | tf_op jit(solution)/shard_map/ppermute | solution.py:385
  55.1 8.8 %collective-permute-start.15 = (bf16[8,64,256]{2,1,0:T(8,128)(2,1)S(1)}, bf16[8,64,256]{2,1,0:T(8,128)(2,1)S(1)}, u32[]{:S(2)}, u32[]{:S(2)}) collective-permute-start(bf16[8,64,256]{2,1,0:T(8,128)(2,1)S(1)} %get-tuple-element.44), channel_id=1, source_target_pairs={{0,4},{2,6},{4,0},{6,2},{8,12},{10,14},{12,8},{14,10},{1,5},{3,7},... | collective-permute-start | bytes 786440 | tf_op jit(solution)/shard_map/ppermute | solution.py:384
  56.5 7.3 %collective-permute-start.16 = (bf16[8,64,256]{2,1,0:T(8,128)(2,1)S(1)}, bf16[8,64,256]{2,1,0:T(8,128)(2,1)S(1)}, u32[]{:S(2)}, u32[]{:S(2)}) collective-permute-start(bf16[8,64,256]{2,1,0:T(8,128)(2,1)S(1)} %get-tuple-element.45), channel_id=1, source_target_pairs={{0,1},{1,0},{2,3},{3,2},{4,8},{5,9},{6,10},{7,11},{8,4},{9,5},{10,... | collective-permute-start | bytes 786440 | tf_op jit(solution)/shard_map/ppermute | solution.py:385
  59.7 0.8 %copy-start.2 = (s32[8]{0:T(128)S(1)}, s32[8]{0:T(128)}, u32[]{:S(2)}) copy-start(s32[8]{0:T(128)} %param.13) | copy-start | bytes 100

commit v7 on v6

--- a/solution.py
+++ b/solution.py
@@ -79,9 +79,9 @@
 def shift_sums(psi, left_env, right_env, term_class, active, sector_rows, classes, pieces):
     n_w, n_s, blk = left_env.shape[:3]
     size = blk // 2 // pieces
-    depth = 3
-    line = jnp.arange(blk, dtype=jnp.int32)
-    masked = jnp.where(line[None, :, None] < sector_rows[:, None, None], psi, jnp.zeros_like(psi))
+    depth = 4
+    line = lax.broadcasted_iota(jnp.int32, psi.shape, 1)
+    masked = jnp.where(line < lax.broadcast_in_dim(sector_rows, psi.shape, (0,)), psi, jnp.zeros_like(psi))
     slots = jnp.where(active.T == 1, term_class[None, :], classes)
     outs = pl.pallas_call(
         shifts_kernel,

time: 64.9 us -> 64.3 us (level)
    lt x1 -> x0, other arithmetic: 0.75 us -> none  [shift_sums(): line[None, :, None] < sector_rows[:, None, None]]
where the time goes in v7:
time: 64.3 us; the launch traced here: 64.1 us
  Pallas kernels  25.5 us (40%)
  starting transfers between devices  23.6 us (37%)
  waiting for transfers between devices  13 us (20%)
  other arithmetic  1.66 us (3%)
    ppermute x6, starting transfers between devices, body(): near_in[i] = lax.ppermute(out[0], 'sector', near)  13.3 us
    pallas_call x1, Pallas kernels, shift_sums(): pl.pallas_call(shifts_kernel, out_shape=[jax.ShapeDtypeStruct((classes, n...  12.4 us
    pallas_call x13, Pallas kernels, small_call(): pl.pallas_call(body, out_shape=outs, in_specs=[SMEM] * len(front) + [VMEM...  9.26 us
    ppermute x3, waiting for transfers between devices, body(): lax.ppermute(x, 'sector', across)  5.94 us
    ppermute x2, starting transfers between devices, body(): came = [lax.ppermute(x, 'sector', across) for x in packed]  3.94 us
    ppermute x2, waiting for transfers between devices, body(): came = [lax.ppermute(x, 'sector', across) for x in packed]  3.48 us
    ppermute x2, starting transfers between devices, body(): came += [lax.ppermute(x, 'sector', across) for x in firsts]  3.04 us
    ppermute x3, starting transfers between devices, body(): lax.ppermute(x, 'sector', across)  2.6 us
  transfers between devices with their start and end apart: 19, of which 5 were waited for; matrix products, arithmetic and copies ran while one was open for 0% of the time, Pallas kernels for 19%

profile of v7, /device:TPU:0, one launch (start us, length us, event | category | flops | bytes accessed | tf_op | source)
XLA Modules:
  0.0 64.1 jit_solution(14741839031626947489)
XLA Ops:
  0.0 0.0 copy-start.3
  0.0 1.7 %fusion.masked = bf16[8,256,256]{2,1,0:T(8,128)(2,1)S(1)} fusion(bf16[8,256,256]{2,1,0:T(8,128)(2,1)} %param.7, s32[8]{0:T(128)} %param.13), kind=kLoop, calls=%fused_computation.1 | loop fusion | flops 1048576 | bytes 2097184 | tf_op jit(solution)/shard_map/jit(_where)/select_n | solution.py:84
  1.7 0.0 copy-done.3
  1.7 0.0 copy-done.1
  1.7 0.0 copy-start
  1.7 12.4 %shard_map.74 = (bf16[5,8,64,256]{3,2,1,0:T(8,128)(2,1)S(1)}, bf16[5,8,64,256]{3,2,1,0:T(8,128)(2,1)S(1)}, bf16[5,8,64,256]{3,2,1,0:T(8,128)(2,1)S(1)}, bf16[5,8,64,256]{3,2,1,0:T(8,128)(2,1)S(1)}) custom-call(s32[8,13]{1,0:T(8,128)S(1)} %select_bitcast_fusion.slots, bf16[8,256,256]{2,1,0:T(8,128)(2,1)S(1)} %fusion.masked, bf16[13,8,256,256]{3,2,1,0:T(8,128)(2,1)} %left.1, ...), custom_call_target="tpu_custom_call" | custom-call | flops 6979321856 | bytes 27262976 | tf_op jit(solution)/shard_map/pallas_call | solution.py:86
  14.1 0.5 collective-permute-start.1
  14.6 0.1 collective-permute-start
  14.7 0.0 copy-done
  14.7 2.1 %shard_map.73.refs_0_ = s32[169]{0:T(256)S(1)} custom-call(s32[5,8]{1,0:T(8,128)S(1)} %copy-done), custom_call_target="tpu_custom_call" | custom-call | flops 4000 | bytes 4000 | tf_op jit(solution)/shard_map/pallas_call | solution.py:146
  16.9 0.6 shard_map.75.refs_3_
  17.4 0.0 collective-permute-done.1.refs_2_
  17.4 0.7 %shard_map.76 = (bf16[40,64,256]{2,1,0:T(8,128)(2,1)S(1)}, bf16[6,64,256]{2,1,0:T(8,128)(2,1)S(1)}) custom-call(s32[169]{0:T(256)S(1)} %shard_map.73.refs_0_, bf16[40,64,256]{2,1,0:T(8,128)(2,1)S(1)} %bitcast.7, bf16[40,64,256]{2,1,0:T(8,128)(2,1)S(1)} %collective-permute-done.1.refs_2_, s32[8,128]{1,0:T(8,128)S(1)} %shard_map.75.refs_3_), custom_call_target="tpu_custom_call" | custom-call | bytes 1000 | tf_op jit(solution)/shard_map/pallas_call | solution.py:163
  18.2 3.0 %collective-permute-start.5 = (bf16[6,64,256]{2,1,0:T(8,128)(2,1)S(1)}, bf16[6,64,256]{2,1,0:T(8,128)(2,1)S(1)}, u32[]{:S(2)}, u32[]{:S(2)}) collective-permute-start(bf16[6,64,256]{2,1,0:T(8,128)(2,1)S(1)} %get-tuple-element.30.refs_3_), channel_id=1, source_target_pairs={{0,2},{2,0},{4,6},{6,4},{8,10},{10,8},{12,14},{14,12},{1,3},{3,1},... | collective-permute-start | bytes 589832 | tf_op jit(solution)/shard_map/ppermute | solution.py:369
  21.2 0.0 collective-permute-done.refs_2_
  21.2 0.7 %shard_map.77 = (bf16[40,64,256]{2,1,0:T(8,128)(2,1)S(1)}, bf16[6,64,256]{2,1,0:T(8,128)(2,1)S(1)}) custom-call(s32[169]{0:T(256)S(1)} %shard_map.73.refs_0_, bf16[40,64,256]{2,1,0:T(8,128)(2,1)S(1)} %bitcast.6, bf16[40,64,256]{2,1,0:T(8,128)(2,1)S(1)} %collective-permute-done.refs_2_, bf16[6,64,256]{2,1,0:T(8,128)(2,1)S(1)} %get-tuple-element.30.refs_3_), custom_call_target="tpu_custom_call" | custom-call | bytes 1000 | tf_op jit(solution)/shard_map/pallas_call | solution.py:163
  21.9 0.9 %collective-permute-start.2 = (bf16[6,64,256]{2,1,0:T(8,128)(2,1)S(1)}, bf16[6,64,256]{2,1,0:T(8,128)(2,1)S(1)}, u32[]{:S(2)}, u32[]{:S(2)}) collective-permute-start(bf16[6,64,256]{2,1,0:T(8,128)(2,1)S(1)} %get-tuple-element.33.refs_3_), channel_id=1, source_target_pairs={{0,2},{2,0},{4,6},{6,4},{8,10},{10,8},{12,14},{14,12},{1,3},{3,1},... | collective-permute-start | bytes 589832 | tf_op jit(solution)/shard_map/ppermute | solution.py:369
  22.8 0.6 shard_map.78
  23.4 3.5 %collective-permute-done.5.refs_2_ = bf16[6,64,256]{2,1,0:T(8,128)(2,1)S(1)} collective-permute-done((bf16[6,64,256]{2,1,0:T(8,128)(2,1)S(1)}, bf16[6,64,256]{2,1,0:T(8,128)(2,1)S(1)}, u32[]{:S(2)}, u32[]{:S(2)}) %collective-permute-start.5) | collective-permute-done | bytes 196640 | tf_op jit(solution)/shard_map/ppermute | solution.py:369
  26.9 0.7 %shard_map.81.refs_3_ = bf16[8,64,256]{2,1,0:T(8,128)(2,1)S(1)} custom-call(s32[169]{0:T(256)S(1)} %shard_map.73.refs_0_, bf16[40,64,256]{2,1,0:T(8,128)(2,1)S(1)} %get-tuple-element.32.refs_1_, bf16[6,64,256]{2,1,0:T(8,128)(2,1)S(1)} %collective-permute-done.5.refs_2_, bf16[6,64,256]{2,1,0:T(8,128)(2,1)S(1)} %get-tuple-element.34.refs_3_), custom_call_target="tpu_custom_call" | custom-call | bytes 1000 | tf_op jit(solution)/shard_map/pallas_call | solution.py:163
  27.6 2.2 %collective-permute-start.9 = (bf16[8,64,256]{2,1,0:T(8,128)(2,1)S(1)}, bf16[8,64,256]{2,1,0:T(8,128)(2,1)S(1)}, u32[]{:S(2)}, u32[]{:S(2)}) collective-permute-start(bf16[8,64,256]{2,1,0:T(8,128)(2,1)S(1)} %shard_map.81.refs_3_), channel_id=1, source_target_pairs={{0,4},{2,6},{4,0},{6,2},{8,12},{10,14},{12,8},{14,10},{1,5},{3,7},... | collective-permute-start | bytes 786440 | tf_op jit(solution)/shard_map/ppermute | solution.py:384
  29.8 1.5 %collective-permute-start.8 = (bf16[6,64,256]{2,1,0:T(8,128)(2,1)S(1)}, bf16[6,64,256]{2,1,0:T(8,128)(2,1)S(1)}, u32[]{:S(2)}, u32[]{:S(2)}) collective-permute-start(bf16[6,64,256]{2,1,0:T(8,128)(2,1)S(1)} %get-tuple-element.34.refs_3_), channel_id=1, source_target_pairs={{0,2},{2,0},{4,6},{6,4},{8,10},{10,8},{12,14},{14,12},{1,3},{3,1},... | collective-permute-start | bytes 589832 | tf_op jit(solution)/shard_map/ppermute | solution.py:371
  31.3 0.0 collective-permute-done.2.refs_4_.refs_2_
  31.3 0.7 %shard_map.82.refs_4_.refs_3_ = bf16[8,64,256]{2,1,0:T(8,128)(2,1)S(1)} custom-call(s32[169]{0:T(256)S(1)} %shard_map.73.refs_0_, bf16[40,64,256]{2,1,0:T(8,128)(2,1)S(1)} %get-tuple-element.31.refs_2_.refs_1_, bf16[6,64,256]{2,1,0:T(8,128)(2,1)S(1)} %collective-permute-done.2.refs_4_.refs_2_, bf16[8,64,256]{2,1,0:T(8,128)(2,1)S(1)} %shard_map.81.refs_3_), custom_call_target="tpu_custom_call" | custom-call | bytes 1000 | tf_op jit(solution)/shard_map/pallas_call | solution.py:163
  32.0 2.0 %collective-permute-start.7 = (bf16[8,64,256]{2,1,0:T(8,128)(2,1)S(1)}, bf16[8,64,256]{2,1,0:T(8,128)(2,1)S(1)}, u32[]{:S(2)}, u32[]{:S(2)}) collective-permute-start(bf16[8,64,256]{2,1,0:T(8,128)(2,1)S(1)} %shard_map.82.refs_4_.refs_3_), channel_id=1, source_target_pairs={{0,4},{2,6},{4,0},{6,2},{8,12},{10,14},{12,8},{14,10},{1,5},{3,7},... | collective-permute-start | bytes 786440 | tf_op jit(solution)/shard_map/ppermute | solution.py:384
  34.0 1.5 %collective-permute-start.6 = (bf16[6,64,256]{2,1,0:T(8,128)(2,1)S(1)}, bf16[6,64,256]{2,1,0:T(8,128)(2,1)S(1)}, u32[]{:S(2)}, u32[]{:S(2)}) collective-permute-start(bf16[6,64,256]{2,1,0:T(8,128)(2,1)S(1)} %get-tuple-element.37), channel_id=1, source_target_pairs={{0,2},{2,0},{4,6},{6,4},{8,10},{10,8},{12,14},{14,12},{1,3},{3,1},... | collective-permute-start | bytes 589832 | tf_op jit(solution)/shard_map/ppermute | solution.py:371
  35.5 0.6 shard_map.79
  36.1 0.6 collective-permute-start.12
  36.7 0.0 collective-permute-done.8.refs_2_
  36.7 0.0 collective-permute-done.9.refs_3_
  36.7 0.8 %shard_map.83 = (bf16[8,64,256]{2,1,0:T(8,128)(2,1)S(1)}, bf16[8,64,256]{2,1,0:T(8,128)(2,1)S(1)}) custom-call(s32[169]{0:T(256)S(1)} %shard_map.73.refs_0_, bf16[40,64,256]{2,1,0:T(8,128)(2,1)S(1)} %get-tuple-element.32.refs_1_, bf16[6,64,256]{2,1,0:T(8,128)(2,1)S(1)} %collective-permute-done.8.refs_2_, ...), custom_call_target="tpu_custom_call" | custom-call | bytes 1000 | tf_op jit(solution)/shard_map/pallas_call | solution.py:163
  37.5 0.1 collective-permute-start.13
  37.5 3.1 %collective-permute-start.14 = (bf16[8,64,256]{2,1,0:T(8,128)(2,1)S(1)}, bf16[8,64,256]{2,1,0:T(8,128)(2,1)S(1)}, u32[]{:S(2)}, u32[]{:S(2)}) collective-permute-start(bf16[8,64,256]{2,1,0:T(8,128)(2,1)S(1)} %get-tuple-element.38.refs_4_), channel_id=1, source_target_pairs={{0,4},{2,6},{4,0},{6,2},{8,12},{10,14},{12,8},{14,10},{1,5},{3,7},... | collective-permute-start | bytes 786440 | tf_op jit(solution)/shard_map/ppermute | solution.py:384
  40.7 1.1 %collective-permute-done.6.refs_2_ = bf16[6,64,256]{2,1,0:T(8,128)(2,1)S(1)} collective-permute-done((bf16[6,64,256]{2,1,0:T(8,128)(2,1)S(1)}, bf16[6,64,256]{2,1,0:T(8,128)(2,1)S(1)}, u32[]{:S(2)}, u32[]{:S(2)}) %collective-permute-start.6) | collective-permute-done | bytes 196640 | tf_op jit(solution)/shard_map/ppermute | solution.py:371
  41.8 0.0 collective-permute-done.7.refs_3_
  41.8 0.8 %shard_map.84 = (bf16[8,64,256]{2,1,0:T(8,128)(2,1)S(1)}, bf16[8,64,256]{2,1,0:T(8,128)(2,1)S(1)}) custom-call(s32[169]{0:T(256)S(1)} %shard_map.73.refs_0_, bf16[40,64,256]{2,1,0:T(8,128)(2,1)S(1)} %get-tuple-element.31.refs_2_.refs_1_, bf16[6,64,256]{2,1,0:T(8,128)(2,1)S(1)} %collective-permute-done.6.refs_2_, ...), custom_call_target="tpu_custom_call" | custom-call | bytes 1000 | tf_op jit(solution)/shard_map/pallas_call | solution.py:163
  42.5 0.1 collective-permute-start.10
  42.6 3.1 %collective-permute-start.11 = (bf16[8,64,256]{2,1,0:T(8,128)(2,1)S(1)}, bf16[8,64,256]{2,1,0:T(8,128)(2,1)S(1)}, u32[]{:S(2)}, u32[]{:S(2)}) collective-permute-start(bf16[8,64,256]{2,1,0:T(8,128)(2,1)S(1)} %get-tuple-element.40.refs_6_), channel_id=1, source_target_pairs={{0,4},{2,6},{4,0},{6,2},{8,12},{10,14},{12,8},{14,10},{1,5},{3,7},... | collective-permute-start | bytes 786440 | tf_op jit(solution)/shard_map/ppermute | solution.py:384
  45.8 0.0 collective-permute-done.12.refs_2_
  45.8 1.5 %collective-permute-start.4 = (bf16[6,64,256]{2,1,0:T(8,128)(2,1)S(1)}, bf16[6,64,256]{2,1,0:T(8,128)(2,1)S(1)}, u32[]{:S(2)}, u32[]{:S(2)}) collective-permute-start(bf16[6,64,256]{2,1,0:T(8,128)(2,1)S(1)} %get-tuple-element.36), channel_id=1, source_target_pairs={{0,2},{2,0},{4,6},{6,4},{8,10},{10,8},{12,14},{14,12},{1,3},{3,1},... | collective-permute-start | bytes 589832 | tf_op jit(solution)/shard_map/ppermute | solution.py:372
  47.3 0.0 collective-permute-done.13.refs_4_
  47.3 0.5 collective-permute-start.3
  47.8 0.0 collective-permute-done.14.refs_5_
  47.8 0.9 %shard_map.85 = (bf16[8,64,256]{2,1,0:T(8,128)(2,1)S(1)}, bf16[8,64,256]{2,1,0:T(8,128)(2,1)S(1)}) custom-call(s32[169]{0:T(256)S(1)} %shard_map.73.refs_0_, bf16[40,64,256]{2,1,0:T(8,128)(2,1)S(1)} %get-tuple-element.32.refs_1_, bf16[6,64,256]{2,1,0:T(8,128)(2,1)S(1)} %collective-permute-done.12.refs_2_, bf16[8,64,256]{2,1,0:T(8,128)(2,1)S(1)} %shard_map.81.refs_3_, ...), custom_call_target="tpu_custom_call" | custom-call | bytes 1000 | tf_op jit(solution)/shard_map/pallas_call | solution.py:163
  48.7 1.4 %collective-permute-start.17 = (bf16[8,64,256]{2,1,0:T(8,128)(2,1)S(1)}, bf16[8,64,256]{2,1,0:T(8,128)(2,1)S(1)}, u32[]{:S(2)}, u32[]{:S(2)}) collective-permute-start(bf16[8,64,256]{2,1,0:T(8,128)(2,1)S(1)} %get-tuple-element.43.refs_6_), channel_id=1, source_target_pairs={{0,4},{2,6},{4,0},{6,2},{8,12},{10,14},{12,8},{14,10},{1,5},{3,7},... | collective-permute-start | bytes 786440 | tf_op jit(solution)/shard_map/ppermute | solution.py:384
  50.1 3.5 %collective-permute-done.4.refs_2_ = bf16[6,64,256]{2,1,0:T(8,128)(2,1)S(1)} collective-permute-done((bf16[6,64,256]{2,1,0:T(8,128)(2,1)S(1)}, bf16[6,64,256]{2,1,0:T(8,128)(2,1)S(1)}, u32[]{:S(2)}, u32[]{:S(2)}) %collective-permute-start.4) | collective-permute-done | bytes 196640 | tf_op jit(solution)/shard_map/ppermute | solution.py:372
  53.6 0.0 collective-permute-start.18
  53.6 0.0 collective-permute-done.10.refs_4_
  53.6 0.0 collective-permute-done.11.refs_5_
  53.6 0.9 %shard_map.86 = (bf16[8,64,256]{2,1,0:T(8,128)(2,1)S(1)}, bf16[8,64,256]{2,1,0:T(8,128)(2,1)S(1)}) custom-call(s32[169]{0:T(256)S(1)} %shard_map.73.refs_0_, bf16[40,64,256]{2,1,0:T(8,128)(2,1)S(1)} %get-tuple-element.31.refs_2_.refs_1_, bf16[6,64,256]{2,1,0:T(8,128)(2,1)S(1)} %collective-permute-done.4.refs_2_, ...), custom_call_target="tpu_custom_call" | custom-call | bytes 1000 | tf_op jit(solution)/shard_map/pallas_call | solution.py:163
  54.5 1.4 %collective-permute-start.15 = (bf16[8,64,256]{2,1,0:T(8,128)(2,1)S(1)}, bf16[8,64,256]{2,1,0:T(8,128)(2,1)S(1)}, u32[]{:S(2)}, u32[]{:S(2)}) collective-permute-start(bf16[8,64,256]{2,1,0:T(8,128)(2,1)S(1)} %get-tuple-element.44), channel_id=1, source_target_pairs={{0,4},{2,6},{4,0},{6,2},{8,12},{10,14},{12,8},{14,10},{1,5},{3,7},... | collective-permute-start | bytes 786440 | tf_op jit(solution)/shard_map/ppermute | solution.py:384
  55.9 0.0 collective-permute-start.16
  55.9 2.4 %collective-permute-done.3.refs_2_ = bf16[12,64,256]{2,1,0:T(8,128)(2,1)S(1)} collective-permute-done((bf16[12,64,256]{2,1,0:T(8,128)(2,1)S(1)}, bf16[12,64,256]{2,1,0:T(8,128)(2,1)S(1)}, u32[]{:S(2)}, u32[]{:S(2)}) %collective-permute-start.3) | collective-permute-done | bytes 393248 | tf_op jit(solution)/shard_map/ppermute | solution.py:372
  58.4 0.7 %shard_map.87.base = f32[8,64,256]{2,1,0:T(8,128)S(1)} custom-call(s32[169]{0:T(256)S(1)} %shard_map.73.refs_0_, bf16[40,64,256]{2,1,0:T(8,128)(2,1)S(1)} %get-tuple-element.32.refs_1_, bf16[12,64,256]{2,1,0:T(8,128)(2,1)S(1)} %collective-permute-done.3.refs_2_), custom_call_target="tpu_custom_call" | custom-call | bytes 1000 | tf_op jit(solution)/shard_map/pallas_call | solution.py:163
  59.1 0.0 copy-start.2
  59.1 0.7 %shard_map.80.base = f32[8,64,256]{2,1,0:T(8,128)S(1)} custom-call(s32[169]{0:T(256)S(1)} %shard_map.73.refs_0_, bf16[40,64,256]{2,1,0:T(8,128)(2,1)S(1)} %get-tuple-element.31.refs_2_.refs_1_, bf16[12,64,256]{2,1,0:T(8,128)(2,1)S(1)} %collective-permute-done.3.refs_2_), custom_call_target="tpu_custom_call" | custom-call | bytes 1000 | tf_op jit(solution)/shard_map/pallas_call | solution.py:163
  59.8 0.0 collective-permute-done.17.refs_0_
  59.8 0.0 collective-permute-done.18.refs_1_
  59.8 0.0 copy-done.2
  59.8 0.1 broadcast_in_dim.25.rows
  59.9 0.8 %shard_map.88.refs_2_ = bf16[8,128,256]{2,1,0:T(8,128)(2,1)} custom-call(s32[8,256]{1,0:T(8,128)S(1)} %broadcast_in_dim.25.rows, f32[8,64,256]{2,1,0:T(8,128)S(1)} %shard_map.87.base, bf16[8,64,256]{2,1,0:T(8,128)(2,1)S(1)} %collective-permute-done.17.refs_0_, bf16[8,64,256]{2,1,0:T(8,128)(2,1)S(1)} %collective-permute-done.18.refs_1_), custom_call_target="tpu_custom_call" | custom-call | bytes 1000 | tf_op jit(solution)/shard_map/pallas_call | solution.py:328
  60.8 2.5 %collective-permute-done.15.refs_0_ = bf16[8,64,256]{2,1,0:T(8,128)(2,1)S(1)} collective-permute-done((bf16[8,64,256]{2,1,0:T(8,128)(2,1)S(1)}, bf16[8,64,256]{2,1,0:T(8,128)(2,1)S(1)}, u32[]{:S(2)}, u32[]{:S(2)}) %collective-permute-start.15) | collective-permute-done | bytes 262176 | tf_op jit(solution)/shard_map/ppermute | solution.py:384
  63.3 0.0 collective-permute-done.16.refs_1_
  63.3 0.8 %shard_map.89 = bf16[8,128,256]{2,1,0:T(8,128)(2,1)} custom-call(s32[8,256]{1,0:T(8,128)S(1)} %broadcast_in_dim.25.rows, f32[8,64,256]{2,1,0:T(8,128)S(1)} %shard_map.80.base, bf16[8,64,256]{2,1,0:T(8,128)(2,1)S(1)} %collective-permute-done.15.refs_0_, bf16[8,64,256]{2,1,0:T(8,128)(2,1)S(1)} %collective-permute-done.16.refs_1_, ...), custom_call_target="tpu_custom_call", output_to_operand_aliasing={{}: (4, {})} | custom-call | bytes 1000 | tf_op jit(solution)/shard_map/pallas_call | solution.py:328
  (2 shorter events, 0.0 us)
Async XLA Ops:
  0.0 1.7 %copy-start.3 = (s32[13]{0:T(128)S(1)}, s32[13]{0:T(128)}, u32[]{:S(2)}) copy-start(s32[13]{0:T(128)} %param.10) | copy-start | bytes 160
  0.0 1.7 %copy-start.1 = (s32[13,8]{0,1:T(8,128)S(1)}, s32[13,8]{0,1:T(8,128)}, u32[]{:S(2)}) copy-start(s32[13,8]{0,1:T(8,128)} %param.11) | copy-start | bytes 1252
  1.7 13.0 %copy-start = (s32[5,8]{1,0:T(8,128)S(1)}, s32[5,8]{1,0:T(8,128)}, u32[]{:S(2)}) copy-start(s32[5,8]{1,0:T(8,128)} %dest.1) | copy-start | bytes 484
  14.1 3.3 %collective-permute-start.1 = (bf16[40,64,256]{2,1,0:T(8,128)(2,1)S(1)}, bf16[40,64,256]{2,1,0:T(8,128)(2,1)S(1)}, u32[]{:S(2)}, u32[]{:S(2)}) collective-permute-start(bf16[40,64,256]{2,1,0:T(8,128)(2,1)S(1)} %bitcast.9), channel_id=1, source_target_pairs={{0,1},{1,0},{2,3},{3,2},{4,5},{5,4},{6,7},{7,6},{8,9},{9,8},{10,11... | collective-permute-start | bytes 3932168 | tf_op jit(solution)/shard_map/ppermute | solution.py:356
  14.6 6.6 %collective-permute-start = (bf16[40,64,256]{2,1,0:T(8,128)(2,1)S(1)}, bf16[40,64,256]{2,1,0:T(8,128)(2,1)S(1)}, u32[]{:S(2)}, u32[]{:S(2)}) collective-permute-start(bf16[40,64,256]{2,1,0:T(8,128)(2,1)S(1)} %bitcast.8), channel_id=1, source_target_pairs={{0,1},{1,0},{2,3},{3,2},{4,5},{5,4},{6,7},{7,6},{8,9},{9,8},{10,11... | collective-permute-start | bytes 3932168 | tf_op jit(solution)/shard_map/ppermute | solution.py:356
  18.2 8.7 %collective-permute-start.5 = (bf16[6,64,256]{2,1,0:T(8,128)(2,1)S(1)}, bf16[6,64,256]{2,1,0:T(8,128)(2,1)S(1)}, u32[]{:S(2)}, u32[]{:S(2)}) collective-permute-start(bf16[6,64,256]{2,1,0:T(8,128)(2,1)S(1)} %get-tuple-element.30.refs_3_), channel_id=1, source_target_pairs={{0,2},{2,0},{4,6},{6,4},{8,10},{10,8},{12,14},{14,12},{1,3},{3,1},... | collective-permute-start | bytes 589832 | tf_op jit(solution)/shard_map/ppermute | solution.py:369
  21.9 9.4 %collective-permute-start.2 = (bf16[6,64,256]{2,1,0:T(8,128)(2,1)S(1)}, bf16[6,64,256]{2,1,0:T(8,128)(2,1)S(1)}, u32[]{:S(2)}, u32[]{:S(2)}) collective-permute-start(bf16[6,64,256]{2,1,0:T(8,128)(2,1)S(1)} %get-tuple-element.33.refs_3_), channel_id=1, source_target_pairs={{0,2},{2,0},{4,6},{6,4},{8,10},{10,8},{12,14},{14,12},{1,3},{3,1},... | collective-permute-start | bytes 589832 | tf_op jit(solution)/shard_map/ppermute | solution.py:369
  27.6 9.1 %collective-permute-start.9 = (bf16[8,64,256]{2,1,0:T(8,128)(2,1)S(1)}, bf16[8,64,256]{2,1,0:T(8,128)(2,1)S(1)}, u32[]{:S(2)}, u32[]{:S(2)}) collective-permute-start(bf16[8,64,256]{2,1,0:T(8,128)(2,1)S(1)} %shard_map.81.refs_3_), channel_id=1, source_target_pairs={{0,4},{2,6},{4,0},{6,2},{8,12},{10,14},{12,8},{14,10},{1,5},{3,7},... | collective-permute-start | bytes 786440 | tf_op jit(solution)/shard_map/ppermute | solution.py:384
  29.8 6.9 %collective-permute-start.8 = (bf16[6,64,256]{2,1,0:T(8,128)(2,1)S(1)}, bf16[6,64,256]{2,1,0:T(8,128)(2,1)S(1)}, u32[]{:S(2)}, u32[]{:S(2)}) collective-permute-start(bf16[6,64,256]{2,1,0:T(8,128)(2,1)S(1)} %get-tuple-element.34.refs_3_), channel_id=1, source_target_pairs={{0,2},{2,0},{4,6},{6,4},{8,10},{10,8},{12,14},{14,12},{1,3},{3,1},... | collective-permute-start | bytes 589832 | tf_op jit(solution)/shard_map/ppermute | solution.py:371
  32.0 9.8 %collective-permute-start.7 = (bf16[8,64,256]{2,1,0:T(8,128)(2,1)S(1)}, bf16[8,64,256]{2,1,0:T(8,128)(2,1)S(1)}, u32[]{:S(2)}, u32[]{:S(2)}) collective-permute-start(bf16[8,64,256]{2,1,0:T(8,128)(2,1)S(1)} %shard_map.82.refs_4_.refs_3_), channel_id=1, source_target_pairs={{0,4},{2,6},{4,0},{6,2},{8,12},{10,14},{12,8},{14,10},{1,5},{3,7},... | collective-permute-start | bytes 786440 | tf_op jit(solution)/shard_map/ppermute | solution.py:384
  34.0 7.8 %collective-permute-start.6 = (bf16[6,64,256]{2,1,0:T(8,128)(2,1)S(1)}, bf16[6,64,256]{2,1,0:T(8,128)(2,1)S(1)}, u32[]{:S(2)}, u32[]{:S(2)}) collective-permute-start(bf16[6,64,256]{2,1,0:T(8,128)(2,1)S(1)} %get-tuple-element.37), channel_id=1, source_target_pairs={{0,2},{2,0},{4,6},{6,4},{8,10},{10,8},{12,14},{14,12},{1,3},{3,1},... | collective-permute-start | bytes 589832 | tf_op jit(solution)/shard_map/ppermute | solution.py:371
  36.1 9.6 %collective-permute-start.12 = (bf16[6,64,256]{2,1,0:T(8,128)(2,1)S(1)}, bf16[6,64,256]{2,1,0:T(8,128)(2,1)S(1)}, u32[]{:S(2)}, u32[]{:S(2)}) collective-permute-start(bf16[6,64,256]{2,1,0:T(8,128)(2,1)S(1)} %get-tuple-element.41), channel_id=1, source_target_pairs={{0,2},{2,0},{4,6},{6,4},{8,10},{10,8},{12,14},{14,12},{1,3},{3,1},... | collective-permute-start | bytes 589832 | tf_op jit(solution)/shard_map/ppermute | solution.py:372
  37.5 9.8 %collective-permute-start.13 = (bf16[8,64,256]{2,1,0:T(8,128)(2,1)S(1)}, bf16[8,64,256]{2,1,0:T(8,128)(2,1)S(1)}, u32[]{:S(2)}, u32[]{:S(2)}) collective-permute-start(bf16[8,64,256]{2,1,0:T(8,128)(2,1)S(1)} %get-tuple-element.42), channel_id=1, source_target_pairs={{0,1},{1,0},{2,3},{3,2},{4,8},{5,9},{6,10},{7,11},{8,4},{9,5},{10,... | collective-permute-start | bytes 786440 | tf_op jit(solution)/shard_map/ppermute | solution.py:385
  37.5 10.2 %collective-permute-start.14 = (bf16[8,64,256]{2,1,0:T(8,128)(2,1)S(1)}, bf16[8,64,256]{2,1,0:T(8,128)(2,1)S(1)}, u32[]{:S(2)}, u32[]{:S(2)}) collective-permute-start(bf16[8,64,256]{2,1,0:T(8,128)(2,1)S(1)} %get-tuple-element.38.refs_4_), channel_id=1, source_target_pairs={{0,4},{2,6},{4,0},{6,2},{8,12},{10,14},{12,8},{14,10},{1,5},{3,7},... | collective-permute-start | bytes 786440 | tf_op jit(solution)/shard_map/ppermute | solution.py:384
  42.5 11.1 %collective-permute-start.10 = (bf16[8,64,256]{2,1,0:T(8,128)(2,1)S(1)}, bf16[8,64,256]{2,1,0:T(8,128)(2,1)S(1)}, u32[]{:S(2)}, u32[]{:S(2)}) collective-permute-start(bf16[8,64,256]{2,1,0:T(8,128)(2,1)S(1)} %get-tuple-element.39), channel_id=1, source_target_pairs={{0,1},{1,0},{2,3},{3,2},{4,8},{5,9},{6,10},{7,11},{8,4},{9,5},{10,... | collective-permute-start | bytes 786440 | tf_op jit(solution)/shard_map/ppermute | solution.py:385
  42.6 11.0 %collective-permute-start.11 = (bf16[8,64,256]{2,1,0:T(8,128)(2,1)S(1)}, bf16[8,64,256]{2,1,0:T(8,128)(2,1)S(1)}, u32[]{:S(2)}, u32[]{:S(2)}) collective-permute-start(bf16[8,64,256]{2,1,0:T(8,128)(2,1)S(1)} %get-tuple-element.40.refs_6_), channel_id=1, source_target_pairs={{0,4},{2,6},{4,0},{6,2},{8,12},{10,14},{12,8},{14,10},{1,5},{3,7},... | collective-permute-start | bytes 786440 | tf_op jit(solution)/shard_map/ppermute | solution.py:384
  45.8 7.8 %collective-permute-start.4 = (bf16[6,64,256]{2,1,0:T(8,128)(2,1)S(1)}, bf16[6,64,256]{2,1,0:T(8,128)(2,1)S(1)}, u32[]{:S(2)}, u32[]{:S(2)}) collective-permute-start(bf16[6,64,256]{2,1,0:T(8,128)(2,1)S(1)} %get-tuple-element.36), channel_id=1, source_target_pairs={{0,2},{2,0},{4,6},{6,4},{8,10},{10,8},{12,14},{14,12},{1,3},{3,1},... | collective-permute-start | bytes 589832 | tf_op jit(solution)/shard_map/ppermute | solution.py:372
  47.3 11.1 %collective-permute-start.3 = (bf16[12,64,256]{2,1,0:T(8,128)(2,1)S(1)}, bf16[12,64,256]{2,1,0:T(8,128)(2,1)S(1)}, u32[]{:S(2)}, u32[]{:S(2)}) collective-permute-start(bf16[12,64,256]{2,1,0:T(8,128)(2,1)S(1)} %get-tuple-element.35), channel_id=1, source_target_pairs={{0,2},{2,0},{4,6},{6,4},{8,10},{10,8},{12,14},{14,12},{1,3},{3,1},... | collective-permute-start | bytes 1179656 | tf_op jit(solution)/shard_map/ppermute | solution.py:372
  48.7 11.1 %collective-permute-start.17 = (bf16[8,64,256]{2,1,0:T(8,128)(2,1)S(1)}, bf16[8,64,256]{2,1,0:T(8,128)(2,1)S(1)}, u32[]{:S(2)}, u32[]{:S(2)}) collective-permute-start(bf16[8,64,256]{2,1,0:T(8,128)(2,1)S(1)} %get-tuple-element.43.refs_6_), channel_id=1, source_target_pairs={{0,4},{2,6},{4,0},{6,2},{8,12},{10,14},{12,8},{14,10},{1,5},{3,7},... | collective-permute-start | bytes 786440 | tf_op jit(solution)/shard_map/ppermute | solution.py:384
  53.6 6.2 %collective-permute-start.18 = (bf16[8,64,256]{2,1,0:T(8,128)(2,1)S(1)}, bf16[8,64,256]{2,1,0:T(8,128)(2,1)S(1)}, u32[]{:S(2)}, u32[]{:S(2)}) collective-permute-start(bf16[8,64,256]{2,1,0:T(8,128)(2,1)S(1)} %get-tuple-element.46), channel_id=1, source_target_pairs={{0,1},{1,0},{2,3},{3,2},{4,8},{5,9},{6,10},{7,11},{8,4},{9,5},{10,... | collective-permute-start | bytes 786440 | tf_op jit(solution)/shard_map/ppermute | solution.py:385
  54.5 8.8 %collective-permute-start.15 = (bf16[8,64,256]{2,1,0:T(8,128)(2,1)S(1)}, bf16[8,64,256]{2,1,0:T(8,128)(2,1)S(1)}, u32[]{:S(2)}, u32[]{:S(2)}) collective-permute-start(bf16[8,64,256]{2,1,0:T(8,128)(2,1)S(1)} %get-tuple-element.44), channel_id=1, source_target_pairs={{0,4},{2,6},{4,0},{6,2},{8,12},{10,14},{12,8},{14,10},{1,5},{3,7},... | collective-permute-start | bytes 786440 | tf_op jit(solution)/shard_map/ppermute | solution.py:384
  55.9 7.3 %collective-permute-start.16 = (bf16[8,64,256]{2,1,0:T(8,128)(2,1)S(1)}, bf16[8,64,256]{2,1,0:T(8,128)(2,1)S(1)}, u32[]{:S(2)}, u32[]{:S(2)}) collective-permute-start(bf16[8,64,256]{2,1,0:T(8,128)(2,1)S(1)} %get-tuple-element.45), channel_id=1, source_target_pairs={{0,1},{1,0},{2,3},{3,2},{4,8},{5,9},{6,10},{7,11},{8,4},{9,5},{10,... | collective-permute-start | bytes 786440 | tf_op jit(solution)/shard_map/ppermute | solution.py:385
  59.1 0.8 %copy-start.2 = (s32[8]{0:T(128)S(1)}, s32[8]{0:T(128)}, u32[]{:S(2)}) copy-start(s32[8]{0:T(128)} %param.13) | copy-start | bytes 100

commit v8 on v7

--- a/solution.py
+++ b/solution.py
@@ -219,7 +219,7 @@
     return (z > 0) & (z < line - 1)
 
 
-def gather(cap, q, pieces, n_s, table, joined, crossed, after, dtype=jnp.bfloat16, cost=1000):
+def gather(cap, q, pieces, n_s, table, joined, crossed, after, dtype=jnp.bfloat16, cost=1000, far_in=None, line=0):
     _, size, blk = joined[0].shape
     count = len(pieces)
     spots = [crossed[q, i] for i in pieces]
@@ -236,12 +236,15 @@
             at = table_at(cap, q, CROSS) + 1
             for slot in range(cap):
                 total[table[at + cap + slot]] += c[spots[k][1] + slot].astype(jnp.float32)
-            out[k * n_s:(k + 1) * n_s] = total[:n_s].astype(dtype)
+            sums = total[:n_s]
+            if far_in is not None:
+                sums += jnp.where(has_far(line), refs[2 * count][...].astype(jnp.float32), 0.0)
+            out[k * n_s:(k + 1) * n_s] = sums.astype(dtype)
 
     (out,) = small_call(
         kernel,
         [jax.ShapeDtypeStruct((count * n_s, size, blk), dtype)],
-        [joined[i] for i in pieces] + [x for x, _ in spots],
+        [joined[i] for i in pieces] + [x for x, _ in spots] + ([] if far_in is None else [far_in]),
         table,
         after,
         [pltpu.VMEM((n_s + 1, size, blk), jnp.float32)],
@@ -386,8 +389,11 @@
     limits = jnp.broadcast_to(sector_rows[:, None], (n_s, psi.shape[2]))
     out = None
     for i in pieces:
-        base = gather(cap, line - 1, [i], n_s, table, joined, crossed, (), jnp.float32)
-        arrived = [x[i] for x in (near_in, far_in) if x[i] is not None]
+        early = far_in[i] if i == 0 else None
+        base = gather(
+            cap, line - 1, [i], n_s, table, joined, crossed, (), jnp.float32, far_in=early, line=line
+        )
+        arrived = [near_in[i]] + ([far_in[i]] if i > 0 and far_in[i] is not None else [])
         out = finish(n_s, line, i, limits, base, arrived, out)
     return out
 

time: 64.3 us -> 64.1 us (level)
  starting transfers between devices: 23.6 us -> 22.9 us
    ppermute x6, starting transfers between devices: 13.3 us -> 12.5 us  [body(): near_in[i] = lax.ppermute(out[0], 'sector', near)]
    ppermute x3, waiting for transfers between devices: 5.94 us -> 6.61 us  [body(): lax.ppermute(x, 'sector', across)]
  transfers between devices with their start and end apart: 19 -> 19, of which waited for: 5 -> 6; matrix products, arithmetic and copies ran while one was open for 0% -> 0% of each run, Pallas kernels for 19% -> 19%
where the time goes in v8:
time: 64.1 us; the launch traced here: 64 us
  Pallas kernels  25.5 us (40%)
  starting transfers between devices  22.9 us (36%)
  waiting for transfers between devices  13.6 us (21%)
  other arithmetic  1.66 us (3%)
    ppermute x6, starting transfers between devices, body(): near_in[i] = lax.ppermute(out[0], 'sector', near)  12.5 us
    pallas_call x1, Pallas kernels, shift_sums(): pl.pallas_call(shifts_kernel, out_shape=[jax.ShapeDtypeStruct((classes, n...  12.4 us
    pallas_call x13, Pallas kernels, small_call(): pl.pallas_call(body, out_shape=outs, in_specs=[SMEM] * len(front) + [VMEM...  9.3 us
    ppermute x3, waiting for transfers between devices, body(): lax.ppermute(x, 'sector', across)  6.61 us
    ppermute x2, starting transfers between devices, body(): came = [lax.ppermute(x, 'sector', across) for x in packed]  3.94 us
    ppermute x2, waiting for transfers between devices, body(): came = [lax.ppermute(x, 'sector', across) for x in packed]  3.48 us
    ppermute x2, starting transfers between devices, body(): came += [lax.ppermute(x, 'sector', across) for x in firsts]  3.04 us
    ppermute x3, starting transfers between devices, body(): lax.ppermute(x, 'sector', across)  2.6 us
  transfers between devices with their start and end apart: 19, of which 6 were waited for; matrix products, arithmetic and copies ran while one was open for 0% of the time, Pallas kernels for 19%

profile of v8, /device:TPU:0, one launch (start us, length us, event | category | flops | bytes accessed | tf_op | source)
XLA Modules:
  0.0 64.0 jit_solution(9054757060133897075)
XLA Ops:
  0.0 0.0 copy-start.3
  0.0 1.7 %fusion.masked = bf16[8,256,256]{2,1,0:T(8,128)(2,1)S(1)} fusion(bf16[8,256,256]{2,1,0:T(8,128)(2,1)} %param.7, s32[8]{0:T(128)} %param.13), kind=kLoop, calls=%fused_computation.1 | loop fusion | flops 1048576 | bytes 2097184 | tf_op jit(solution)/shard_map/jit(_where)/select_n | solution.py:84
  1.7 0.0 copy-done.3
  1.7 0.0 copy-done.1
  1.7 0.0 copy-start
  1.7 12.4 %shard_map.74 = (bf16[5,8,64,256]{3,2,1,0:T(8,128)(2,1)S(1)}, bf16[5,8,64,256]{3,2,1,0:T(8,128)(2,1)S(1)}, bf16[5,8,64,256]{3,2,1,0:T(8,128)(2,1)S(1)}, bf16[5,8,64,256]{3,2,1,0:T(8,128)(2,1)S(1)}) custom-call(s32[8,13]{1,0:T(8,128)S(1)} %select_bitcast_fusion.slots, bf16[8,256,256]{2,1,0:T(8,128)(2,1)S(1)} %fusion.masked, bf16[13,8,256,256]{3,2,1,0:T(8,128)(2,1)} %left.1, ...), custom_call_target="tpu_custom_call" | custom-call | flops 6979321856 | bytes 27262976 | tf_op jit(solution)/shard_map/pallas_call | solution.py:86
  14.1 0.5 collective-permute-start.1
  14.6 0.1 collective-permute-start
  14.7 0.0 copy-done
  14.7 2.1 %shard_map.73.refs_0_ = s32[169]{0:T(256)S(1)} custom-call(s32[5,8]{1,0:T(8,128)S(1)} %copy-done), custom_call_target="tpu_custom_call" | custom-call | flops 4000 | bytes 4000 | tf_op jit(solution)/shard_map/pallas_call | solution.py:146
  16.9 0.6 shard_map.75.refs_3_
  17.4 0.0 collective-permute-done.1.refs_2_
  17.4 0.7 %shard_map.76 = (bf16[40,64,256]{2,1,0:T(8,128)(2,1)S(1)}, bf16[6,64,256]{2,1,0:T(8,128)(2,1)S(1)}) custom-call(s32[169]{0:T(256)S(1)} %shard_map.73.refs_0_, bf16[40,64,256]{2,1,0:T(8,128)(2,1)S(1)} %bitcast.7, bf16[40,64,256]{2,1,0:T(8,128)(2,1)S(1)} %collective-permute-done.1.refs_2_, s32[8,128]{1,0:T(8,128)S(1)} %shard_map.75.refs_3_), custom_call_target="tpu_custom_call" | custom-call | bytes 1000 | tf_op jit(solution)/shard_map/pallas_call | solution.py:163
  18.2 3.0 %collective-permute-start.5 = (bf16[6,64,256]{2,1,0:T(8,128)(2,1)S(1)}, bf16[6,64,256]{2,1,0:T(8,128)(2,1)S(1)}, u32[]{:S(2)}, u32[]{:S(2)}) collective-permute-start(bf16[6,64,256]{2,1,0:T(8,128)(2,1)S(1)} %get-tuple-element.30.refs_3_), channel_id=1, source_target_pairs={{0,2},{2,0},{4,6},{6,4},{8,10},{10,8},{12,14},{14,12},{1,3},{3,1},... | collective-permute-start | bytes 589832 | tf_op jit(solution)/shard_map/ppermute | solution.py:372
  21.2 0.0 collective-permute-done.refs_2_
  21.2 0.7 %shard_map.77 = (bf16[40,64,256]{2,1,0:T(8,128)(2,1)S(1)}, bf16[6,64,256]{2,1,0:T(8,128)(2,1)S(1)}) custom-call(s32[169]{0:T(256)S(1)} %shard_map.73.refs_0_, bf16[40,64,256]{2,1,0:T(8,128)(2,1)S(1)} %bitcast.6, bf16[40,64,256]{2,1,0:T(8,128)(2,1)S(1)} %collective-permute-done.refs_2_, bf16[6,64,256]{2,1,0:T(8,128)(2,1)S(1)} %get-tuple-element.30.refs_3_), custom_call_target="tpu_custom_call" | custom-call | bytes 1000 | tf_op jit(solution)/shard_map/pallas_call | solution.py:163
  21.9 0.9 %collective-permute-start.2 = (bf16[6,64,256]{2,1,0:T(8,128)(2,1)S(1)}, bf16[6,64,256]{2,1,0:T(8,128)(2,1)S(1)}, u32[]{:S(2)}, u32[]{:S(2)}) collective-permute-start(bf16[6,64,256]{2,1,0:T(8,128)(2,1)S(1)} %get-tuple-element.33.refs_3_), channel_id=1, source_target_pairs={{0,2},{2,0},{4,6},{6,4},{8,10},{10,8},{12,14},{14,12},{1,3},{3,1},... | collective-permute-start | bytes 589832 | tf_op jit(solution)/shard_map/ppermute | solution.py:372
  22.8 0.6 shard_map.78
  23.4 3.5 %collective-permute-done.5.refs_2_ = bf16[6,64,256]{2,1,0:T(8,128)(2,1)S(1)} collective-permute-done((bf16[6,64,256]{2,1,0:T(8,128)(2,1)S(1)}, bf16[6,64,256]{2,1,0:T(8,128)(2,1)S(1)}, u32[]{:S(2)}, u32[]{:S(2)}) %collective-permute-start.5) | collective-permute-done | bytes 196640 | tf_op jit(solution)/shard_map/ppermute | solution.py:372
  26.9 0.7 %shard_map.81.refs_3_ = bf16[8,64,256]{2,1,0:T(8,128)(2,1)S(1)} custom-call(s32[169]{0:T(256)S(1)} %shard_map.73.refs_0_, bf16[40,64,256]{2,1,0:T(8,128)(2,1)S(1)} %get-tuple-element.32.refs_1_, bf16[6,64,256]{2,1,0:T(8,128)(2,1)S(1)} %collective-permute-done.5.refs_2_, bf16[6,64,256]{2,1,0:T(8,128)(2,1)S(1)} %get-tuple-element.34.refs_3_), custom_call_target="tpu_custom_call" | custom-call | bytes 1000 | tf_op jit(solution)/shard_map/pallas_call | solution.py:163
  27.6 2.2 %collective-permute-start.9 = (bf16[8,64,256]{2,1,0:T(8,128)(2,1)S(1)}, bf16[8,64,256]{2,1,0:T(8,128)(2,1)S(1)}, u32[]{:S(2)}, u32[]{:S(2)}) collective-permute-start(bf16[8,64,256]{2,1,0:T(8,128)(2,1)S(1)} %shard_map.81.refs_3_), channel_id=1, source_target_pairs={{0,4},{2,6},{4,0},{6,2},{8,12},{10,14},{12,8},{14,10},{1,5},{3,7},... | collective-permute-start | bytes 786440 | tf_op jit(solution)/shard_map/ppermute | solution.py:387
  29.8 1.5 %collective-permute-start.8 = (bf16[6,64,256]{2,1,0:T(8,128)(2,1)S(1)}, bf16[6,64,256]{2,1,0:T(8,128)(2,1)S(1)}, u32[]{:S(2)}, u32[]{:S(2)}) collective-permute-start(bf16[6,64,256]{2,1,0:T(8,128)(2,1)S(1)} %get-tuple-element.34.refs_3_), channel_id=1, source_target_pairs={{0,2},{2,0},{4,6},{6,4},{8,10},{10,8},{12,14},{14,12},{1,3},{3,1},... | collective-permute-start | bytes 589832 | tf_op jit(solution)/shard_map/ppermute | solution.py:374
  31.3 0.0 collective-permute-done.2.refs_4_.refs_2_
  31.3 0.7 %shard_map.82.refs_4_.refs_3_ = bf16[8,64,256]{2,1,0:T(8,128)(2,1)S(1)} custom-call(s32[169]{0:T(256)S(1)} %shard_map.73.refs_0_, bf16[40,64,256]{2,1,0:T(8,128)(2,1)S(1)} %get-tuple-element.31.refs_2_.refs_1_, bf16[6,64,256]{2,1,0:T(8,128)(2,1)S(1)} %collective-permute-done.2.refs_4_.refs_2_, bf16[8,64,256]{2,1,0:T(8,128)(2,1)S(1)} %shard_map.81.refs_3_), custom_call_target="tpu_custom_call" | custom-call | bytes 1000 | tf_op jit(solution)/shard_map/pallas_call | solution.py:163
  32.0 2.0 %collective-permute-start.7 = (bf16[8,64,256]{2,1,0:T(8,128)(2,1)S(1)}, bf16[8,64,256]{2,1,0:T(8,128)(2,1)S(1)}, u32[]{:S(2)}, u32[]{:S(2)}) collective-permute-start(bf16[8,64,256]{2,1,0:T(8,128)(2,1)S(1)} %shard_map.82.refs_4_.refs_3_), channel_id=1, source_target_pairs={{0,4},{2,6},{4,0},{6,2},{8,12},{10,14},{12,8},{14,10},{1,5},{3,7},... | collective-permute-start | bytes 786440 | tf_op jit(solution)/shard_map/ppermute | solution.py:387
  34.0 1.5 %collective-permute-start.6 = (bf16[6,64,256]{2,1,0:T(8,128)(2,1)S(1)}, bf16[6,64,256]{2,1,0:T(8,128)(2,1)S(1)}, u32[]{:S(2)}, u32[]{:S(2)}) collective-permute-start(bf16[6,64,256]{2,1,0:T(8,128)(2,1)S(1)} %get-tuple-element.37), channel_id=1, source_target_pairs={{0,2},{2,0},{4,6},{6,4},{8,10},{10,8},{12,14},{14,12},{1,3},{3,1},... | collective-permute-start | bytes 589832 | tf_op jit(solution)/shard_map/ppermute | solution.py:374
  35.5 0.6 shard_map.79
  36.1 0.6 collective-permute-start.12
  36.7 0.0 collective-permute-done.8.refs_2_
  36.7 0.0 collective-permute-done.9.refs_3_
  36.7 0.8 %shard_map.83 = (bf16[8,64,256]{2,1,0:T(8,128)(2,1)S(1)}, bf16[8,64,256]{2,1,0:T(8,128)(2,1)S(1)}) custom-call(s32[169]{0:T(256)S(1)} %shard_map.73.refs_0_, bf16[40,64,256]{2,1,0:T(8,128)(2,1)S(1)} %get-tuple-element.32.refs_1_, bf16[6,64,256]{2,1,0:T(8,128)(2,1)S(1)} %collective-permute-done.8.refs_2_, ...), custom_call_target="tpu_custom_call" | custom-call | bytes 1000 | tf_op jit(solution)/shard_map/pallas_call | solution.py:163
  37.5 0.1 collective-permute-start.13
  37.6 3.1 %collective-permute-start.14 = (bf16[8,64,256]{2,1,0:T(8,128)(2,1)S(1)}, bf16[8,64,256]{2,1,0:T(8,128)(2,1)S(1)}, u32[]{:S(2)}, u32[]{:S(2)}) collective-permute-start(bf16[8,64,256]{2,1,0:T(8,128)(2,1)S(1)} %get-tuple-element.38.refs_4_), channel_id=1, source_target_pairs={{0,4},{2,6},{4,0},{6,2},{8,12},{10,14},{12,8},{14,10},{1,5},{3,7},... | collective-permute-start | bytes 786440 | tf_op jit(solution)/shard_map/ppermute | solution.py:387
  40.7 1.1 %collective-permute-done.6.refs_2_ = bf16[6,64,256]{2,1,0:T(8,128)(2,1)S(1)} collective-permute-done((bf16[6,64,256]{2,1,0:T(8,128)(2,1)S(1)}, bf16[6,64,256]{2,1,0:T(8,128)(2,1)S(1)}, u32[]{:S(2)}, u32[]{:S(2)}) %collective-permute-start.6) | collective-permute-done | bytes 196640 | tf_op jit(solution)/shard_map/ppermute | solution.py:374
  41.8 0.0 collective-permute-done.7.refs_3_
  41.8 0.8 %shard_map.84 = (bf16[8,64,256]{2,1,0:T(8,128)(2,1)S(1)}, bf16[8,64,256]{2,1,0:T(8,128)(2,1)S(1)}) custom-call(s32[169]{0:T(256)S(1)} %shard_map.73.refs_0_, bf16[40,64,256]{2,1,0:T(8,128)(2,1)S(1)} %get-tuple-element.31.refs_2_.refs_1_, bf16[6,64,256]{2,1,0:T(8,128)(2,1)S(1)} %collective-permute-done.6.refs_2_, ...), custom_call_target="tpu_custom_call" | custom-call | bytes 1000 | tf_op jit(solution)/shard_map/pallas_call | solution.py:163
  42.5 0.1 collective-permute-start.10
  42.6 3.1 %collective-permute-start.11 = (bf16[8,64,256]{2,1,0:T(8,128)(2,1)S(1)}, bf16[8,64,256]{2,1,0:T(8,128)(2,1)S(1)}, u32[]{:S(2)}, u32[]{:S(2)}) collective-permute-start(bf16[8,64,256]{2,1,0:T(8,128)(2,1)S(1)} %get-tuple-element.40.refs_6_), channel_id=1, source_target_pairs={{0,4},{2,6},{4,0},{6,2},{8,12},{10,14},{12,8},{14,10},{1,5},{3,7},... | collective-permute-start | bytes 786440 | tf_op jit(solution)/shard_map/ppermute | solution.py:387
  45.8 0.0 collective-permute-done.12.refs_2_
  45.8 1.5 %collective-permute-start.4 = (bf16[6,64,256]{2,1,0:T(8,128)(2,1)S(1)}, bf16[6,64,256]{2,1,0:T(8,128)(2,1)S(1)}, u32[]{:S(2)}, u32[]{:S(2)}) collective-permute-start(bf16[6,64,256]{2,1,0:T(8,128)(2,1)S(1)} %get-tuple-element.36), channel_id=1, source_target_pairs={{0,2},{2,0},{4,6},{6,4},{8,10},{10,8},{12,14},{14,12},{1,3},{3,1},... | collective-permute-start | bytes 589832 | tf_op jit(solution)/shard_map/ppermute | solution.py:375
  47.3 0.0 collective-permute-done.13.refs_4_
  47.3 0.5 collective-permute-start.3
  47.8 0.0 collective-permute-done.14.refs_5_
  47.8 0.9 %shard_map.85 = (bf16[8,64,256]{2,1,0:T(8,128)(2,1)S(1)}, bf16[8,64,256]{2,1,0:T(8,128)(2,1)S(1)}) custom-call(s32[169]{0:T(256)S(1)} %shard_map.73.refs_0_, bf16[40,64,256]{2,1,0:T(8,128)(2,1)S(1)} %get-tuple-element.32.refs_1_, bf16[6,64,256]{2,1,0:T(8,128)(2,1)S(1)} %collective-permute-done.12.refs_2_, bf16[8,64,256]{2,1,0:T(8,128)(2,1)S(1)} %shard_map.81.refs_3_, ...), custom_call_target="tpu_custom_call" | custom-call | bytes 1000 | tf_op jit(solution)/shard_map/pallas_call | solution.py:163
  48.7 0.1 collective-permute-start.17
  48.8 4.8 %collective-permute-done.4.refs_2_ = bf16[6,64,256]{2,1,0:T(8,128)(2,1)S(1)} collective-permute-done((bf16[6,64,256]{2,1,0:T(8,128)(2,1)S(1)}, bf16[6,64,256]{2,1,0:T(8,128)(2,1)S(1)}, u32[]{:S(2)}, u32[]{:S(2)}) %collective-permute-start.4) | collective-permute-done | bytes 196640 | tf_op jit(solution)/shard_map/ppermute | solution.py:375
  53.6 0.0 collective-permute-start.18
  53.6 0.0 collective-permute-done.10.refs_4_
  53.6 0.0 collective-permute-done.11.refs_5_
  53.6 0.9 %shard_map.86 = (bf16[8,64,256]{2,1,0:T(8,128)(2,1)S(1)}, bf16[8,64,256]{2,1,0:T(8,128)(2,1)S(1)}) custom-call(s32[169]{0:T(256)S(1)} %shard_map.73.refs_0_, bf16[40,64,256]{2,1,0:T(8,128)(2,1)S(1)} %get-tuple-element.31.refs_2_.refs_1_, bf16[6,64,256]{2,1,0:T(8,128)(2,1)S(1)} %collective-permute-done.4.refs_2_, ...), custom_call_target="tpu_custom_call" | custom-call | bytes 1000 | tf_op jit(solution)/shard_map/pallas_call | solution.py:163
  54.5 2.1 %collective-permute-start.15 = (bf16[8,64,256]{2,1,0:T(8,128)(2,1)S(1)}, bf16[8,64,256]{2,1,0:T(8,128)(2,1)S(1)}, u32[]{:S(2)}, u32[]{:S(2)}) collective-permute-start(bf16[8,64,256]{2,1,0:T(8,128)(2,1)S(1)} %get-tuple-element.44), channel_id=1, source_target_pairs={{0,4},{2,6},{4,0},{6,2},{8,12},{10,14},{12,8},{14,10},{1,5},{3,7},... | collective-permute-start | bytes 786440 | tf_op jit(solution)/shard_map/ppermute | solution.py:387
  56.6 0.0 collective-permute-start.16
  56.6 1.8 %collective-permute-done.3.refs_2_ = bf16[12,64,256]{2,1,0:T(8,128)(2,1)S(1)} collective-permute-done((bf16[12,64,256]{2,1,0:T(8,128)(2,1)S(1)}, bf16[12,64,256]{2,1,0:T(8,128)(2,1)S(1)}, u32[]{:S(2)}, u32[]{:S(2)}) %collective-permute-start.3) | collective-permute-done | bytes 393248 | tf_op jit(solution)/shard_map/ppermute | solution.py:375
  58.4 0.7 %shard_map.80.base = f32[8,64,256]{2,1,0:T(8,128)S(1)} custom-call(s32[169]{0:T(256)S(1)} %shard_map.73.refs_0_, bf16[40,64,256]{2,1,0:T(8,128)(2,1)S(1)} %get-tuple-element.31.refs_2_.refs_1_, bf16[12,64,256]{2,1,0:T(8,128)(2,1)S(1)} %collective-permute-done.3.refs_2_), custom_call_target="tpu_custom_call" | custom-call | bytes 1000 | tf_op jit(solution)/shard_map/pallas_call | solution.py:163
  59.1 0.0 copy-start.2
  59.1 0.0 collective-permute-done.17.refs_3_
  59.1 0.8 %shard_map.87.base = f32[8,64,256]{2,1,0:T(8,128)S(1)} custom-call(s32[169]{0:T(256)S(1)} %shard_map.73.refs_0_, bf16[40,64,256]{2,1,0:T(8,128)(2,1)S(1)} %get-tuple-element.32.refs_1_, bf16[12,64,256]{2,1,0:T(8,128)(2,1)S(1)} %collective-permute-done.3.refs_2_, bf16[8,64,256]{2,1,0:T(8,128)(2,1)S(1)} %collective-permute-done.17.refs_3_), custom_call_target="tpu_custom_call" | custom-call | bytes 1000 | tf_op jit(solution)/shard_map/pallas_call | solution.py:163
  59.9 0.5 collective-permute-done.18.refs_0_
  60.3 0.0 copy-done.2
  60.3 0.1 broadcast_in_dim.25.rows
  60.4 0.8 %shard_map.88.refs_2_ = bf16[8,128,256]{2,1,0:T(8,128)(2,1)} custom-call(s32[8,256]{1,0:T(8,128)S(1)} %broadcast_in_dim.25.rows, f32[8,64,256]{2,1,0:T(8,128)S(1)} %shard_map.87.base, bf16[8,64,256]{2,1,0:T(8,128)(2,1)S(1)} %collective-permute-done.18.refs_0_), custom_call_target="tpu_custom_call" | custom-call | bytes 1000 | tf_op jit(solution)/shard_map/pallas_call | solution.py:331
  61.2 1.9 %collective-permute-done.15.refs_0_ = bf16[8,64,256]{2,1,0:T(8,128)(2,1)S(1)} collective-permute-done((bf16[8,64,256]{2,1,0:T(8,128)(2,1)S(1)}, bf16[8,64,256]{2,1,0:T(8,128)(2,1)S(1)}, u32[]{:S(2)}, u32[]{:S(2)}) %collective-permute-start.15) | collective-permute-done | bytes 262176 | tf_op jit(solution)/shard_map/ppermute | solution.py:387
  63.1 0.0 collective-permute-done.16.refs_1_
  63.1 0.8 %shard_map.89 = bf16[8,128,256]{2,1,0:T(8,128)(2,1)} custom-call(s32[8,256]{1,0:T(8,128)S(1)} %broadcast_in_dim.25.rows, f32[8,64,256]{2,1,0:T(8,128)S(1)} %shard_map.80.base, bf16[8,64,256]{2,1,0:T(8,128)(2,1)S(1)} %collective-permute-done.15.refs_0_, bf16[8,64,256]{2,1,0:T(8,128)(2,1)S(1)} %collective-permute-done.16.refs_1_, ...), custom_call_target="tpu_custom_call", output_to_operand_aliasing={{}: (4, {})} | custom-call | bytes 1000 | tf_op jit(solution)/shard_map/pallas_call | solution.py:331
  (2 shorter events, 0.0 us)
Async XLA Ops:
  0.0 1.7 %copy-start.3 = (s32[13]{0:T(128)S(1)}, s32[13]{0:T(128)}, u32[]{:S(2)}) copy-start(s32[13]{0:T(128)} %param.10) | copy-start | bytes 160
  0.0 1.7 %copy-start.1 = (s32[13,8]{0,1:T(8,128)S(1)}, s32[13,8]{0,1:T(8,128)}, u32[]{:S(2)}) copy-start(s32[13,8]{0,1:T(8,128)} %param.11) | copy-start | bytes 1252
  1.7 13.0 %copy-start = (s32[5,8]{1,0:T(8,128)S(1)}, s32[5,8]{1,0:T(8,128)}, u32[]{:S(2)}) copy-start(s32[5,8]{1,0:T(8,128)} %dest.1) | copy-start | bytes 484
  14.1 3.3 %collective-permute-start.1 = (bf16[40,64,256]{2,1,0:T(8,128)(2,1)S(1)}, bf16[40,64,256]{2,1,0:T(8,128)(2,1)S(1)}, u32[]{:S(2)}, u32[]{:S(2)}) collective-permute-start(bf16[40,64,256]{2,1,0:T(8,128)(2,1)S(1)} %bitcast.9), channel_id=1, source_target_pairs={{0,1},{1,0},{2,3},{3,2},{4,5},{5,4},{6,7},{7,6},{8,9},{9,8},{10,11... | collective-permute-start | bytes 3932168 | tf_op jit(solution)/shard_map/ppermute | solution.py:359
  14.6 6.6 %collective-permute-start = (bf16[40,64,256]{2,1,0:T(8,128)(2,1)S(1)}, bf16[40,64,256]{2,1,0:T(8,128)(2,1)S(1)}, u32[]{:S(2)}, u32[]{:S(2)}) collective-permute-start(bf16[40,64,256]{2,1,0:T(8,128)(2,1)S(1)} %bitcast.8), channel_id=1, source_target_pairs={{0,1},{1,0},{2,3},{3,2},{4,5},{5,4},{6,7},{7,6},{8,9},{9,8},{10,11... | collective-permute-start | bytes 3932168 | tf_op jit(solution)/shard_map/ppermute | solution.py:359
  18.2 8.7 %collective-permute-start.5 = (bf16[6,64,256]{2,1,0:T(8,128)(2,1)S(1)}, bf16[6,64,256]{2,1,0:T(8,128)(2,1)S(1)}, u32[]{:S(2)}, u32[]{:S(2)}) collective-permute-start(bf16[6,64,256]{2,1,0:T(8,128)(2,1)S(1)} %get-tuple-element.30.refs_3_), channel_id=1, source_target_pairs={{0,2},{2,0},{4,6},{6,4},{8,10},{10,8},{12,14},{14,12},{1,3},{3,1},... | collective-permute-start | bytes 589832 | tf_op jit(solution)/shard_map/ppermute | solution.py:372
  21.9 9.4 %collective-permute-start.2 = (bf16[6,64,256]{2,1,0:T(8,128)(2,1)S(1)}, bf16[6,64,256]{2,1,0:T(8,128)(2,1)S(1)}, u32[]{:S(2)}, u32[]{:S(2)}) collective-permute-start(bf16[6,64,256]{2,1,0:T(8,128)(2,1)S(1)} %get-tuple-element.33.refs_3_), channel_id=1, source_target_pairs={{0,2},{2,0},{4,6},{6,4},{8,10},{10,8},{12,14},{14,12},{1,3},{3,1},... | collective-permute-start | bytes 589832 | tf_op jit(solution)/shard_map/ppermute | solution.py:372
  27.6 9.1 %collective-permute-start.9 = (bf16[8,64,256]{2,1,0:T(8,128)(2,1)S(1)}, bf16[8,64,256]{2,1,0:T(8,128)(2,1)S(1)}, u32[]{:S(2)}, u32[]{:S(2)}) collective-permute-start(bf16[8,64,256]{2,1,0:T(8,128)(2,1)S(1)} %shard_map.81.refs_3_), channel_id=1, source_target_pairs={{0,4},{2,6},{4,0},{6,2},{8,12},{10,14},{12,8},{14,10},{1,5},{3,7},... | collective-permute-start | bytes 786440 | tf_op jit(solution)/shard_map/ppermute | solution.py:387
  29.8 6.9 %collective-permute-start.8 = (bf16[6,64,256]{2,1,0:T(8,128)(2,1)S(1)}, bf16[6,64,256]{2,1,0:T(8,128)(2,1)S(1)}, u32[]{:S(2)}, u32[]{:S(2)}) collective-permute-start(bf16[6,64,256]{2,1,0:T(8,128)(2,1)S(1)} %get-tuple-element.34.refs_3_), channel_id=1, source_target_pairs={{0,2},{2,0},{4,6},{6,4},{8,10},{10,8},{12,14},{14,12},{1,3},{3,1},... | collective-permute-start | bytes 589832 | tf_op jit(solution)/shard_map/ppermute | solution.py:374
  32.0 9.8 %collective-permute-start.7 = (bf16[8,64,256]{2,1,0:T(8,128)(2,1)S(1)}, bf16[8,64,256]{2,1,0:T(8,128)(2,1)S(1)}, u32[]{:S(2)}, u32[]{:S(2)}) collective-permute-start(bf16[8,64,256]{2,1,0:T(8,128)(2,1)S(1)} %shard_map.82.refs_4_.refs_3_), channel_id=1, source_target_pairs={{0,4},{2,6},{4,0},{6,2},{8,12},{10,14},{12,8},{14,10},{1,5},{3,7},... | collective-permute-start | bytes 786440 | tf_op jit(solution)/shard_map/ppermute | solution.py:387
  34.0 7.8 %collective-permute-start.6 = (bf16[6,64,256]{2,1,0:T(8,128)(2,1)S(1)}, bf16[6,64,256]{2,1,0:T(8,128)(2,1)S(1)}, u32[]{:S(2)}, u32[]{:S(2)}) collective-permute-start(bf16[6,64,256]{2,1,0:T(8,128)(2,1)S(1)} %get-tuple-element.37), channel_id=1, source_target_pairs={{0,2},{2,0},{4,6},{6,4},{8,10},{10,8},{12,14},{14,12},{1,3},{3,1},... | collective-permute-start | bytes 589832 | tf_op jit(solution)/shard_map/ppermute | solution.py:374
  36.1 9.6 %collective-permute-start.12 = (bf16[6,64,256]{2,1,0:T(8,128)(2,1)S(1)}, bf16[6,64,256]{2,1,0:T(8,128)(2,1)S(1)}, u32[]{:S(2)}, u32[]{:S(2)}) collective-permute-start(bf16[6,64,256]{2,1,0:T(8,128)(2,1)S(1)} %get-tuple-element.41), channel_id=1, source_target_pairs={{0,2},{2,0},{4,6},{6,4},{8,10},{10,8},{12,14},{14,12},{1,3},{3,1},... | collective-permute-start | bytes 589832 | tf_op jit(solution)/shard_map/ppermute | solution.py:375
  37.5 9.8 %collective-permute-start.13 = (bf16[8,64,256]{2,1,0:T(8,128)(2,1)S(1)}, bf16[8,64,256]{2,1,0:T(8,128)(2,1)S(1)}, u32[]{:S(2)}, u32[]{:S(2)}) collective-permute-start(bf16[8,64,256]{2,1,0:T(8,128)(2,1)S(1)} %get-tuple-element.42), channel_id=1, source_target_pairs={{0,1},{1,0},{2,3},{3,2},{4,8},{5,9},{6,10},{7,11},{8,4},{9,5},{10,... | collective-permute-start | bytes 786440 | tf_op jit(solution)/shard_map/ppermute | solution.py:388
  37.6 10.2 %collective-permute-start.14 = (bf16[8,64,256]{2,1,0:T(8,128)(2,1)S(1)}, bf16[8,64,256]{2,1,0:T(8,128)(2,1)S(1)}, u32[]{:S(2)}, u32[]{:S(2)}) collective-permute-start(bf16[8,64,256]{2,1,0:T(8,128)(2,1)S(1)} %get-tuple-element.38.refs_4_), channel_id=1, source_target_pairs={{0,4},{2,6},{4,0},{6,2},{8,12},{10,14},{12,8},{14,10},{1,5},{3,7},... | collective-permute-start | bytes 786440 | tf_op jit(solution)/shard_map/ppermute | solution.py:387
  42.5 11.1 %collective-permute-start.10 = (bf16[8,64,256]{2,1,0:T(8,128)(2,1)S(1)}, bf16[8,64,256]{2,1,0:T(8,128)(2,1)S(1)}, u32[]{:S(2)}, u32[]{:S(2)}) collective-permute-start(bf16[8,64,256]{2,1,0:T(8,128)(2,1)S(1)} %get-tuple-element.39), channel_id=1, source_target_pairs={{0,1},{1,0},{2,3},{3,2},{4,8},{5,9},{6,10},{7,11},{8,4},{9,5},{10,... | collective-permute-start | bytes 786440 | tf_op jit(solution)/shard_map/ppermute | solution.py:388
  42.6 11.0 %collective-permute-start.11 = (bf16[8,64,256]{2,1,0:T(8,128)(2,1)S(1)}, bf16[8,64,256]{2,1,0:T(8,128)(2,1)S(1)}, u32[]{:S(2)}, u32[]{:S(2)}) collective-permute-start(bf16[8,64,256]{2,1,0:T(8,128)(2,1)S(1)} %get-tuple-element.40.refs_6_), channel_id=1, source_target_pairs={{0,4},{2,6},{4,0},{6,2},{8,12},{10,14},{12,8},{14,10},{1,5},{3,7},... | collective-permute-start | bytes 786440 | tf_op jit(solution)/shard_map/ppermute | solution.py:387
  45.8 7.8 %collective-permute-start.4 = (bf16[6,64,256]{2,1,0:T(8,128)(2,1)S(1)}, bf16[6,64,256]{2,1,0:T(8,128)(2,1)S(1)}, u32[]{:S(2)}, u32[]{:S(2)}) collective-permute-start(bf16[6,64,256]{2,1,0:T(8,128)(2,1)S(1)} %get-tuple-element.36), channel_id=1, source_target_pairs={{0,2},{2,0},{4,6},{6,4},{8,10},{10,8},{12,14},{14,12},{1,3},{3,1},... | collective-permute-start | bytes 589832 | tf_op jit(solution)/shard_map/ppermute | solution.py:375
  47.3 11.1 %collective-permute-start.3 = (bf16[12,64,256]{2,1,0:T(8,128)(2,1)S(1)}, bf16[12,64,256]{2,1,0:T(8,128)(2,1)S(1)}, u32[]{:S(2)}, u32[]{:S(2)}) collective-permute-start(bf16[12,64,256]{2,1,0:T(8,128)(2,1)S(1)} %get-tuple-element.35), channel_id=1, source_target_pairs={{0,2},{2,0},{4,6},{6,4},{8,10},{10,8},{12,14},{14,12},{1,3},{3,1},... | collective-permute-start | bytes 1179656 | tf_op jit(solution)/shard_map/ppermute | solution.py:375
  48.7 10.4 %collective-permute-start.17 = (bf16[8,64,256]{2,1,0:T(8,128)(2,1)S(1)}, bf16[8,64,256]{2,1,0:T(8,128)(2,1)S(1)}, u32[]{:S(2)}, u32[]{:S(2)}) collective-permute-start(bf16[8,64,256]{2,1,0:T(8,128)(2,1)S(1)} %get-tuple-element.46), channel_id=1, source_target_pairs={{0,1},{1,0},{2,3},{3,2},{4,8},{5,9},{6,10},{7,11},{8,4},{9,5},{10,... | collective-permute-start | bytes 786440 | tf_op jit(solution)/shard_map/ppermute | solution.py:388
  53.6 6.7 %collective-permute-start.18 = (bf16[8,64,256]{2,1,0:T(8,128)(2,1)S(1)}, bf16[8,64,256]{2,1,0:T(8,128)(2,1)S(1)}, u32[]{:S(2)}, u32[]{:S(2)}) collective-permute-start(bf16[8,64,256]{2,1,0:T(8,128)(2,1)S(1)} %get-tuple-element.43.refs_6_), channel_id=1, source_target_pairs={{0,4},{2,6},{4,0},{6,2},{8,12},{10,14},{12,8},{14,10},{1,5},{3,7},... | collective-permute-start | bytes 786440 | tf_op jit(solution)/shard_map/ppermute | solution.py:387
  54.5 8.6 %collective-permute-start.15 = (bf16[8,64,256]{2,1,0:T(8,128)(2,1)S(1)}, bf16[8,64,256]{2,1,0:T(8,128)(2,1)S(1)}, u32[]{:S(2)}, u32[]{:S(2)}) collective-permute-start(bf16[8,64,256]{2,1,0:T(8,128)(2,1)S(1)} %get-tuple-element.44), channel_id=1, source_target_pairs={{0,4},{2,6},{4,0},{6,2},{8,12},{10,14},{12,8},{14,10},{1,5},{3,7},... | collective-permute-start | bytes 786440 | tf_op jit(solution)/shard_map/ppermute | solution.py:387
  56.6 6.5 %collective-permute-start.16 = (bf16[8,64,256]{2,1,0:T(8,128)(2,1)S(1)}, bf16[8,64,256]{2,1,0:T(8,128)(2,1)S(1)}, u32[]{:S(2)}, u32[]{:S(2)}) collective-permute-start(bf16[8,64,256]{2,1,0:T(8,128)(2,1)S(1)} %get-tuple-element.45), channel_id=1, source_target_pairs={{0,1},{1,0},{2,3},{3,2},{4,8},{5,9},{6,10},{7,11},{8,4},{9,5},{10,... | collective-permute-start | bytes 786440 | tf_op jit(solution)/shard_map/ppermute | solution.py:388
  59.1 1.2 %copy-start.2 = (s32[8]{0:T(128)S(1)}, s32[8]{0:T(128)}, u32[]{:S(2)}) copy-start(s32[8]{0:T(128)} %param.13) | copy-start | bytes 100
